TPU v7x, 256 devices: a whole 4x4x8 slice. The times are simulated.
256 devices in a mesh: chan: 128 (over y_lo, x, z, core), tm: 2 (over y_hi).
Axes of the slice: x: 4, y: 4 (y_hi: 2, y_lo: 2; y = y_hi * 2 + y_lo), z: 8, core: 2. Of those that a mesh axis runs over, the one named last changes fastest.
Arguments:
- voltages: int32 [2, 512, 262144], P(None, 'chan', 'tm'), may hold values from -8 to 7
Outputs:
- visibilities: float32 [2, 1024, 512, 512], P(None, 'chan', 'tm')
Inputs may be any that keep to these rules, and one draw needn't show every extreme that they name: `voltages`: 4-bit two's complement samples.
All inputs are finite; a program needn't handle non-finite values.
Results may differ from a plain program's by a relative error of at most 0.001.
Values may be sent and summed in bfloat16 or wider, within the bound.
No kernel may reach another device: no remote copies, remote signals or barrier semaphores. Data moves between devices by JAX's collectives and lax.ppermute only.
A program may use at most 128 MiB of HBM per device.

v0:
```python
import jax
import jax.numpy as jnp
import numpy as np
from jax import lax
from jax.experimental import pallas as pl
from jax.experimental.pallas import tpu as pltpu
from jax.sharding import Mesh
from jax.sharding import PartitionSpec as P

NCH = 1024
TAPS = 4
RADIX = 8
FINE = NCH // RADIX
LANES = 128
NA = 4
SPEC = 128
STEP = 32
HIST = TAPS - 1
ROWS = RADIX * NA
GROUP = 64
PLANE = ("x", "z", "core")
FIRST = (0, 1, 2, 3, 4)
SECOND = (5, 6, 7)


def taps_table():
    k = np.arange(TAPS * NCH, dtype=np.float64)
    x = (k - 2.0 * NCH + 0.5) / NCH
    window = 0.54 - 0.46 * np.cos(2.0 * np.pi * (k + 0.5) / (TAPS * NCH))
    taps = (np.sinc(x) * window * 0.25).reshape(TAPS, RADIX, 1, LANES)
    return np.broadcast_to(taps, (TAPS, RADIX, NA, LANES)).reshape(TAPS, ROWS, LANES).astype(np.float32)


def turn_table():
    j = np.arange(RADIX)[:, None, None]
    q = np.arange(FINE)[None, :, None]
    l = np.arange(FINE)[None, None, :]
    angle = 2.0 * np.pi * ((l * (RADIX * q + j)) % NCH) / NCH
    cosine = np.cos(angle) / np.sqrt(NCH)
    sine = np.sin(angle) / np.sqrt(NCH)
    real = np.concatenate([cosine, sine], axis=2)
    imag = np.concatenate([-sine, cosine], axis=2)
    full = np.concatenate([real, imag], axis=1)
    high = full.astype(jnp.bfloat16)
    low = (full - high.astype(np.float64)).astype(jnp.bfloat16)
    return np.stack([high, low], axis=1)


def gather_table():
    table = np.zeros((256, 256), np.float32)
    for p in range(2):
        for r in range(32):
            for a in range(NA):
                table[p * 128 + r * NA + a, r * 8 + p * NA + a] = 1.0
    return table.astype(jnp.bfloat16)


def butterfly(x):
    def add(u, v):
        return (u[0] + v[0], u[1] + v[1])

    def sub(u, v):
        return (u[0] - v[0], u[1] - v[1])

    def minus_i(u):
        return (u[1], -u[0])

    def four(a, b, c, d):
        s, t = add(a, c), sub(a, c)
        u, v = add(b, d), minus_i(sub(b, d))
        return add(s, u), add(t, v), sub(s, u), sub(t, v)

    half = np.float32(np.sqrt(0.5))
    even = four(x[0], x[2], x[4], x[6])
    odd = four(x[1], x[3], x[5], x[7])
    o1 = ((odd[1][0] + odd[1][1]) * half, (odd[1][1] - odd[1][0]) * half)
    o2 = minus_i(odd[2])
    o3 = ((odd[3][1] - odd[3][0]) * half, -(odd[3][0] + odd[3][1]) * half)
    odd = (odd[0], o1, o2, o3)
    return [add(even[i], odd[i]) for i in range(4)] + [sub(even[i], odd[i]) for i in range(4)]


def channel_kernel(place, order, volts, tail, taps, turn, *rest):
    outs, (ext, filt, high, low, spread) = rest[:-5], rest[-5:]
    step = pl.program_id(0)

    @pl.when(step == 0)
    def _():
        ext[:, : HIST * ROWS, :] = tail[...].astype(jnp.float32)

    @pl.when(step < SPEC // STEP)
    def _():
        for p in range(2):

            @pl.loop(0, STEP // 4)
            def _(i):
                base = pl.multiple_of(i * 4 * ROWS, 4 * ROWS)
                ext[p, pl.ds(HIST * ROWS + base, 4 * ROWS), :] = volts[
                    p, pl.ds(base, 4 * ROWS), :
                ].astype(jnp.float32)

            @pl.loop(0, STEP // 4)
            def _(i):
                base = pl.multiple_of(i * 4 * ROWS, 4 * ROWS)
                for piece in range(ROWS // 8):
                    weights = [taps[t, piece * 8 : piece * 8 + 8, :] for t in range(TAPS)]
                    frames = [
                        ext[p, pl.ds(base + (s * ROWS + piece * 8), 8), :] for s in range(4 + HIST)
                    ]
                    for s in range(4):
                        total = weights[0] * frames[s]
                        for t in range(1, TAPS):
                            total = total + weights[t] * frames[s + t]
                        filt[p, pl.ds(base + (s * ROWS + piece * 8), 8), :] = total

            ext[p, : HIST * ROWS, :] = ext[p, STEP * ROWS :, :]

        for a in range(NA):
            for part in range(STEP // 16):
                x = [
                    tuple(
                        filt[p, pl.ds(part * 16 * ROWS + m * NA + a, 16, stride=ROWS), :]
                        for p in range(2)
                    )
                    for m in range(RADIX)
                ]
                y = butterfly(x)
                row = pl.multiple_of(a * SPEC + step * STEP + part * 16, 16)
                for j in range(RADIX):
                    for p in range(2):
                        value = y[j][p]
                        top = value.astype(jnp.bfloat16)
                        rest_ = (value - top.astype(jnp.float32)).astype(jnp.bfloat16)
                        high[j, pl.ds(row, 16), p * LANES : (p + 1) * LANES] = top
                        low[j, pl.ds(row, 16), p * LANES : (p + 1) * LANES] = rest_

    @pl.when(step >= SPEC // STEP)
    def _():
        now = order[step - SPEC // STEP]
        mine = place[0]
        rows = []
        for kind in range(2):
            pieces = []
            for p in range(2):
                for slot in range(2):
                    half = mine if slot == 0 else 1 - mine
                    start = pl.multiple_of(p * FINE + half * GROUP, GROUP)
                    pieces.append(turn[0, kind, pl.ds(start, GROUP), :])
            rows.append(jnp.concatenate(pieces, axis=0))

        def dot(left, right):
            return lax.dot_general(
                left, right, (((1,), (1,)), ((), ())), preferred_element_type=jnp.float32
            )

        tops = high[now]
        spectra = dot(rows[0], tops) + (dot(rows[1], tops) + dot(rows[0], low[now]))
        for p in range(2):
            for slot in range(2):
                for a in range(NA):
                    spread[
                        pl.ds(slot * GROUP * 8 + p * NA + a, GROUP, stride=8), :
                    ] = spectra[
                        (p * 2 + slot) * GROUP : (p * 2 + slot + 1) * GROUP,
                        a * SPEC : (a + 1) * SPEC,
                    ]
        for slot in range(2):
            block = spread[slot * GROUP * 8 : (slot + 1) * GROUP * 8, :]
            block = block.reshape(GROUP, 8, LANES).astype(jnp.bfloat16)
            at = step - SPEC // STEP
            if len(outs) == 1:
                outs[0][:, slot, 0] = block
            else:
                cut = len(SECOND)

                @pl.when(at < len(FIRST))
                def _():
                    outs[0][:, slot, 0] = block

                @pl.when(at >= len(FIRST))
                def _():
                    outs[1][:, slot, 0] = block


def channelize(place, volts, tail):
    lead = SPEC // STEP
    order = np.array(FIRST + SECOND, np.int32)
    sizes = [len(FIRST), len(SECOND)] if SECOND else [len(FIRST)]
    starts = [0, len(FIRST)]

    def out_map(start, size):
        return lambda i, place, order: (0, 0, jnp.clip(i - lead - start, 0, size - 1), 0, 0)

    return pl.pallas_call(
        channel_kernel,
        grid_spec=pltpu.PrefetchScalarGridSpec(
            num_scalar_prefetch=2,
            grid=(lead + RADIX,),
            in_specs=[
                pl.BlockSpec((2, STEP * ROWS, LANES), lambda i, *_: (0, jnp.minimum(i, lead - 1), 0)),
                pl.BlockSpec((2, HIST * ROWS, LANES), lambda i, *_: (0, 0, 0)),
                pl.BlockSpec((TAPS, ROWS, LANES), lambda i, *_: (0, 0, 0)),
                pl.BlockSpec(
                    (1, 2, 2 * FINE, 2 * FINE),
                    lambda i, place, order: (order[jnp.maximum(i - lead, 0)], 0, 0, 0),
                ),
            ],
            out_specs=[
                pl.BlockSpec((GROUP, 2, 1, 8, LANES), out_map(start, size))
                for start, size in zip(starts, sizes)
            ],
            scratch_shapes=[
                pltpu.VMEM((2, (HIST + STEP) * ROWS, LANES), jnp.float32),
                pltpu.VMEM((2, STEP * ROWS, LANES), jnp.float32),
                pltpu.VMEM((RADIX, NA * SPEC, 2 * LANES), jnp.bfloat16),
                pltpu.VMEM((RADIX, NA * SPEC, 2 * LANES), jnp.bfloat16),
                pltpu.VMEM((2 * GROUP * 8, LANES), jnp.float32),
            ],
        ),
        out_shape=[
            jax.ShapeDtypeStruct((GROUP, 2, size, 8, LANES), jnp.bfloat16) for size in sizes
        ],
        compiler_params=pltpu.CompilerParams(
            dimension_semantics=("arbitrary",), vmem_limit_bytes=40 * 1024 * 1024
        ),
        cost_estimate=pl.CostEstimate(
            flops=2 * 10**9, bytes_accessed=8 * 1024 * 1024, transcendentals=0
        ),
        name="channelize",
    )(place, jnp.asarray(order), volts, tail, jnp.asarray(taps_table()), jnp.asarray(turn_table()))


def correlate_kernel(scale, place, same, far, near, cross, table, *rest):
    out, stage = rest[-2], rest[-1]
    mine, time = place[0], place[1]
    for kind, (here, there) in enumerate(((same, far), (near, cross))):
        group = mine if kind == 0 else 1 - mine
        left = here[...].reshape(GROUP * 8, LANES)
        right = there[...].reshape(GROUP * 8, LANES)
        for half in range(2):
            block = jnp.concatenate(
                [left[half * 256 : half * 256 + 256], right[half * 256 : half * 256 + 256]], axis=1
            )
            sorted_ = jnp.dot(table[...], block, preferred_element_type=jnp.float32)
            sorted_ = sorted_.astype(jnp.bfloat16)
            for p in range(2):
                stage[group, half * 128 : half * 128 + 128, p * 256 : p * 256 + 256] = sorted_[
                    p * 128 : p * 128 + 128
                ]

    rows = stage[time]
    turned = jnp.concatenate([rows[:, 256:], -rows[:, :256]], axis=1)

    def dot(left, right):
        return lax.dot_general(
            left, right, (((1,), (1,)), ((), ())), preferred_element_type=jnp.float32
        )

    for group in range(2):
        columns = stage[group]
        out[0, 0, :, group * 256 : group * 256 + 256] = dot(rows, columns) * scale
        out[1, 0, :, group * 256 : group * 256 + 256] = dot(turned, columns) * scale


def correlate(place, scale, first, count, own, far, near, cross, earlier):
    block = (GROUP, 1, 8, LANES)
    in_specs = [
        pl.BlockSpec((GROUP, 1, 1, 8, LANES), lambda i, *_: (0, 0, i, 0, 0)),
        pl.BlockSpec(block, lambda i, *_: (0, i, 0, 0)),
        pl.BlockSpec(block, lambda i, *_: (0, i, 0, 0)),
        pl.BlockSpec(block, lambda i, *_: (0, i, 0, 0)),
        pl.BlockSpec((256, 256), lambda i, *_: (0, 0)),
    ]
    operands = [place, own, far, near, cross, jnp.asarray(gather_table())]
    aliases = {}
    if earlier is not None:
        in_specs.append(pl.BlockSpec(memory_space=pl.ANY))
        aliases = {len(operands): 0}
        operands.append(earlier)

    def kernel(*refs):
        correlate_kernel(scale, *refs)

    return pl.pallas_call(
        kernel,
        grid_spec=pltpu.PrefetchScalarGridSpec(
            num_scalar_prefetch=1,
            grid=(count,),
            in_specs=in_specs,
            out_specs=pl.BlockSpec((2, 1, 256, 512), lambda i, *_: (0, first + i, 0, 0)),
            scratch_shapes=[pltpu.VMEM((2, 256, 512), jnp.bfloat16)],
        ),
        out_shape=jax.ShapeDtypeStruct((2, 8, 256, 512), jnp.float32),
        input_output_aliases=aliases,
        compiler_params=pltpu.CompilerParams(
            dimension_semantics=("arbitrary",), vmem_limit_bytes=24 * 1024 * 1024
        ),
        cost_estimate=pl.CostEstimate(
            flops=count * 4 * 10**8, bytes_accessed=count * 3 * 512 * 1024, transcendentals=0
        ),
        name="correlate",
    )(*operands)


def exchange(near_part, far_part):
    flip = [(0, 1), (1, 0)]
    both = [(0, 3), (3, 0), (1, 2), (2, 1)]
    near = lax.ppermute(near_part, "y_lo", flip)
    cross = lax.ppermute(near_part, ("y_lo", "tm"), both)
    far = lax.ppermute(far_part, "tm", flip)
    return far, near, cross


def local(voltages):
    tiles = voltages.shape[2] // LANES
    volts = voltages.reshape(2, NA, tiles, LANES).transpose(0, 2, 1, 3).reshape(2, tiles * NA, LANES)
    tail = lax.ppermute(volts[:, (SPEC - HIST) * ROWS :], "tm", [(0, 1)])
    place = jnp.stack([lax.axis_index("y_lo"), lax.axis_index("tm")]).astype(jnp.int32)
    scale = np.float32(1.0 / (SPEC * lax.axis_size("tm")))
    parts = channelize(place, volts, tail)
    result = None
    first = 0
    for part in parts:
        turned = lax.all_to_all(part, PLANE, split_axis=0, concat_axis=0, tiled=True)
        far, near, cross = exchange(turned[:, 1], turned[:, 0])
        count = part.shape[2]
        result = correlate(place, scale, first, count, turned, far, near, cross, result)
        first += count
    return result


def solution(mesh):
    names = ("y_lo", "x", "z", "core", "tm")
    fine = Mesh(mesh.devices.reshape(2, 4, 8, 2, 2), names)
    chan = names[:-1]
    return jax.shard_map(
        local,
        mesh=fine,
        in_specs=P(None, chan, "tm"),
        out_specs=P(None, chan, "tm", None),
        check_vma=False,
    )
```

profile of v0, /device:TPU:1, one launch (start us, length us, event | category | flops | bytes accessed | tf_op | source)
XLA Modules:
  0.0 132.6 jit_solution(17484270126771369935)
XLA Ops:
  0.0 0.9 slice.20
  0.9 5.6 %collective-permute-start = (s32[2,96,128]{2,1,0:T(8,128)S(1)}, s32[2,96,128]{2,1,0:T(8,128)S(1)}, u32[]{:S(2)}, u32[]{:S(2)}) collective-permute-start(s32[2,96,128]{2,1,0:T(8,128)S(1)} %slice.20), channel_id=1, source_target_pairs={{0,1},{2,3},{4,5},{6,7},{8,9},{10,11},{12,13},{14,15},{16,17},{18,... | collective-permute-start | bytes 294920 | tf_op jit(solution)/shard_map/ppermute | solution.py:317
  6.6 0.1 pad_add_fusion.place.refs_0_
  6.6 1.5 %collective-permute-done.tail = s32[2,96,128]{2,1,0:T(8,128)S(1)} collective-permute-done((s32[2,96,128]{2,1,0:T(8,128)S(1)}, s32[2,96,128]{2,1,0:T(8,128)S(1)}, u32[]{:S(2)}, u32[]{:S(2)}) %collective-permute-start) | collective-permute-done | bytes 98336 | tf_op jit(solution)/shard_map/ppermute | solution.py:317
  8.2 2.2 %copy-done.1 = s32[2,4,131072]{2,1,0:T(4,128)S(1)} copy-done((s32[2,4,131072]{2,1,0:T(4,128)S(1)}, s32[2,4,131072]{2,1,0:T(4,128)}, u32[]{:S(2)}) %copy-start.1) | copy-done | bytes 4194328
  10.4 1.6 %copy-done.2 = bf16[8,2,256,256]{3,2,1,0:T(8,128)(2,1)S(1)} copy-done((bf16[8,2,256,256]{3,2,1,0:T(8,128)(2,1)S(1)}, bf16[8,2,256,256]{3,2,1,0:T(8,128)(2,1)}, u32[]{:S(2)}) %copy-start.2) | copy-done | bytes 2097176
  12.0 0.8 copy-done.3
  12.8 11.2 %channelize.1 = (bf16[64,2,5,8,128]{4,3,2,1,0:T(8,128)(2,1)S(1)}, bf16[64,2,3,8,128]{4,3,2,1,0:T(8,128)(2,1)}) custom-call(s32[2]{0:T(128)S(1)} %pad_add_fusion.place.refs_0_, s32[8]{0:T(128)S(1)} %call_exported.0.order, s32[2,4096,128]{2,1,0:T(8,128)S(1)} %bitcast.24, s32[2,96,128]{2,1,0:T(8,128)S(1)} %collective-permute-done.tail, ...), custom_call_target="tpu_custom_call" | custom-call | flops 2000000000 | bytes 8388608 | tf_op jit(solution)/shard_map/channelize/pallas_call | solution.py:194
  24.0 47.0 %all_to_all.10.refs_1_ = bf16[64,2,5,8,128]{4,3,2,1,0:T(8,128)(2,1)S(1)} all-to-all(bf16[64,2,5,8,128]{4,3,2,1,0:T(8,128)(2,1)S(1)} %get-tuple-element.8), channel_id=1, replica_groups=mesh['y_lo'=2,'x'=4,'z'=8,'core'=2,'tm'=2] {'x','z','core'}, dimensions={0} | all-to-all | bytes 2621440 | tf_op jit(solution)/shard_map/all_to_all | solution.py:324
  71.0 6.2 %all-to-all-start = ((bf16[64,2,3,8,128]{4,3,2,1,0:T(8,128)(2,1)}), bf16[64,2,3,8,128]{4,3,2,1,0:T(8,128)(2,1)S(1)}, u32[]{:S(2)}, u32[]{:S(2)}) async-start(bf16[64,2,3,8,128]{4,3,2,1,0:T(8,128)(2,1)} %get-tuple-element.7), calls=%async_computation | async-start | bytes 1572864 | tf_op jit(solution)/shard_map/all_to_all | solution.py:324
  77.2 0.0 copy-start
  77.2 1.2 slice_bitcast_fusion
  78.4 3.6 %collective-permute-start.4 = (bf16[64,5,8,128]{3,2,1,0:T(8,128)(2,1)}, bf16[64,5,8,128]{3,2,1,0:T(8,128)(2,1)S(1)}, u32[]{:S(2)}, u32[]{:S(2)}) collective-permute-start(bf16[64,5,8,128]{3,2,1,0:T(8,128)(2,1)} %get-tuple-element.10), channel_id=1, source_target_pairs={{0,1},{1,0},{2,3},{3,2},{4,5},{5,4},{6,7},{7,6},{8,9},{9,8},{10,11... | collective-permute-start | bytes 1966088 | tf_op jit(solution)/shard_map/ppermute | solution.py:310
  82.0 0.4 collective-permute-start.5
  82.4 17.8 %all-to-all-done.refs_1_ = bf16[64,2,3,8,128]{4,3,2,1,0:T(8,128)(2,1)S(1)} async-done(((bf16[64,2,3,8,128]{4,3,2,1,0:T(8,128)(2,1)}), bf16[64,2,3,8,128]{4,3,2,1,0:T(8,128)(2,1)S(1)}, u32[]{:S(2)}, u32[]{:S(2)}) %all-to-all-start) | async-done | bytes 786464 | tf_op jit(solution)/shard_map/all_to_all | solution.py:324
  100.2 0.1 slice_bitcast_fusion.2
  100.3 3.7 %collective-permute-start.1 = (bf16[64,3,8,128]{3,2,1,0:T(8,128)(2,1)S(1)}, bf16[64,3,8,128]{3,2,1,0:T(8,128)(2,1)S(1)}, u32[]{:S(2)}, u32[]{:S(2)}) collective-permute-start(bf16[64,3,8,128]{3,2,1,0:T(8,128)(2,1)S(1)} %get-tuple-element.12), channel_id=1, source_target_pairs={{0,1},{1,0},{2,3},{3,2},{4,5},{5,4},{6,7},{7,6},{8,9},{9,8},{10,11... | collective-permute-start | bytes 1179656 | tf_op jit(solution)/shard_map/ppermute | solution.py:310
  104.0 0.0 collective-permute-start.3
  104.0 0.4 collective-permute-start.2
  104.4 7.5 %collective-permute-done.6.refs_4_ = bf16[64,5,8,128]{3,2,1,0:T(8,128)(2,1)S(1)} collective-permute-done((bf16[64,5,8,128]{3,2,1,0:T(8,128)(2,1)}, bf16[64,5,8,128]{3,2,1,0:T(8,128)(2,1)S(1)}, u32[]{:S(2)}, u32[]{:S(2)}) %collective-permute-start.6) | collective-permute-done | bytes 655392 | tf_op jit(solution)/shard_map/ppermute | solution.py:309
  111.9 7.1 %correlate.2.refs_6_ = f32[2,8,256,512]{3,2,1,0:T(8,128)} custom-call(s32[2]{0:T(128)S(1)} %pad_add_fusion.place.refs_0_, bf16[64,2,5,8,128]{4,3,2,1,0:T(8,128)(2,1)S(1)} %all_to_all.10.refs_1_, bf16[64,5,8,128]{3,2,1,0:T(8,128)(2,1)S(1)} %collective-permute-done.4.refs_2_, bf16[64,5,8,128]{3,2,1,0:T(8,128)(2,1)} %collective-permute-done.5.refs_3_, ...), custom_call_target="tpu_custom_call" | custom-call | flops 2000000000 | bytes 7864320 | tf_op jit(solution)/shard_map/correlate/pallas_call | solution.py:284
  119.0 0.4 collective-permute-done.1.refs_2_
  119.5 8.8 %collective-permute-done.3.refs_4_ = bf16[64,3,8,128]{3,2,1,0:T(8,128)(2,1)S(1)} collective-permute-done((bf16[64,3,8,128]{3,2,1,0:T(8,128)(2,1)S(1)}, bf16[64,3,8,128]{3,2,1,0:T(8,128)(2,1)S(1)}, u32[]{:S(2)}, u32[]{:S(2)}) %collective-permute-start.3) | collective-permute-done | bytes 393248 | tf_op jit(solution)/shard_map/ppermute | solution.py:309
  128.3 4.3 %correlate.3 = f32[2,8,256,512]{3,2,1,0:T(8,128)} custom-call(s32[2]{0:T(128)S(1)} %pad_add_fusion.place.refs_0_, bf16[64,2,3,8,128]{4,3,2,1,0:T(8,128)(2,1)S(1)} %all-to-all-done.refs_1_, bf16[64,3,8,128]{3,2,1,0:T(8,128)(2,1)S(1)} %collective-permute-done.1.refs_2_, ...), custom_call_target="tpu_custom_call", output_to_operand_aliasing={{}: (6, {})} | custom-call | flops 1200000000 | bytes 4718592 | tf_op jit(solution)/shard_map/correlate/pallas_call | solution.py:284
  (9 shorter events, 0.0 us)
Async XLA Ops:
  0.9 7.3 %collective-permute-start = (s32[2,96,128]{2,1,0:T(8,128)S(1)}, s32[2,96,128]{2,1,0:T(8,128)S(1)}, u32[]{:S(2)}, u32[]{:S(2)}) collective-permute-start(s32[2,96,128]{2,1,0:T(8,128)S(1)} %slice.20), channel_id=1, source_target_pairs={{0,1},{2,3},{4,5},{6,7},{8,9},{10,11},{12,13},{14,15},{16,17},{18,... | collective-permute-start | bytes 294920 | tf_op jit(solution)/shard_map/ppermute | solution.py:317
  8.2 2.2 %copy-start.1 = (s32[2,4,131072]{2,1,0:T(4,128)S(1)}, s32[2,4,131072]{2,1,0:T(4,128)}, u32[]{:S(2)}) copy-start(s32[2,4,131072]{2,1,0:T(4,128)} %param.6) | copy-start | bytes 12582916
  10.4 1.6 %copy-start.2 = (bf16[8,2,256,256]{3,2,1,0:T(8,128)(2,1)S(1)}, bf16[8,2,256,256]{3,2,1,0:T(8,128)(2,1)}, u32[]{:S(2)}) copy-start(bf16[8,2,256,256]{3,2,1,0:T(8,128)(2,1)} %constant.17.clone.turn) | copy-start | bytes 6291460
  11.9 0.8 copy-start.3
  71.0 29.2 %all-to-all-start = ((bf16[64,2,3,8,128]{4,3,2,1,0:T(8,128)(2,1)}), bf16[64,2,3,8,128]{4,3,2,1,0:T(8,128)(2,1)S(1)}, u32[]{:S(2)}, u32[]{:S(2)}) async-start(bf16[64,2,3,8,128]{4,3,2,1,0:T(8,128)(2,1)} %get-tuple-element.7), calls=%async_computation | async-start | bytes 1572864 | tf_op jit(solution)/shard_map/all_to_all | solution.py:324
  77.2 34.7 %copy-start = (bf16[256,256]{1,0:T(8,128)(2,1)S(1)}, bf16[256,256]{1,0:T(8,128)(2,1)}, u32[]{:S(2)}) copy-start(bf16[256,256]{1,0:T(8,128)(2,1)} %constant.18.clone.refs_5_) | copy-start | bytes 393220
  78.4 25.6 %collective-permute-start.4 = (bf16[64,5,8,128]{3,2,1,0:T(8,128)(2,1)}, bf16[64,5,8,128]{3,2,1,0:T(8,128)(2,1)S(1)}, u32[]{:S(2)}, u32[]{:S(2)}) collective-permute-start(bf16[64,5,8,128]{3,2,1,0:T(8,128)(2,1)} %get-tuple-element.10), channel_id=1, source_target_pairs={{0,1},{1,0},{2,3},{3,2},{4,5},{5,4},{6,7},{7,6},{8,9},{9,8},{10,11... | collective-permute-start | bytes 1966088 | tf_op jit(solution)/shard_map/ppermute | solution.py:310
  82.0 29.9 %collective-permute-start.6 = (bf16[64,5,8,128]{3,2,1,0:T(8,128)(2,1)}, bf16[64,5,8,128]{3,2,1,0:T(8,128)(2,1)S(1)}, u32[]{:S(2)}, u32[]{:S(2)}) collective-permute-start(bf16[64,5,8,128]{3,2,1,0:T(8,128)(2,1)} %get-tuple-element.9), channel_id=1, source_target_pairs={{0,129},{129,0},{1,128},{128,1},{2,131},{131,2},{3,130},{130,3},{4... | collective-permute-start | bytes 1966088 | tf_op jit(solution)/shard_map/ppermute | solution.py:309
  82.0 29.9 %collective-permute-start.5 = (bf16[64,5,8,128]{3,2,1,0:T(8,128)(2,1)}, bf16[64,5,8,128]{3,2,1,0:T(8,128)(2,1)}, u32[]{:S(2)}, u32[]{:S(2)}) collective-permute-start(bf16[64,5,8,128]{3,2,1,0:T(8,128)(2,1)} %get-tuple-element.9), channel_id=1, source_target_pairs={{0,128},{128,0},{1,129},{129,1},{2,130},{130,2},{3,131},{131,3},{4... | collective-permute-start | bytes 1966088 | tf_op jit(solution)/shard_map/ppermute | solution.py:308
  100.3 19.2 %collective-permute-start.1 = (bf16[64,3,8,128]{3,2,1,0:T(8,128)(2,1)S(1)}, bf16[64,3,8,128]{3,2,1,0:T(8,128)(2,1)S(1)}, u32[]{:S(2)}, u32[]{:S(2)}) collective-permute-start(bf16[64,3,8,128]{3,2,1,0:T(8,128)(2,1)S(1)} %get-tuple-element.12), channel_id=1, source_target_pairs={{0,1},{1,0},{2,3},{3,2},{4,5},{5,4},{6,7},{7,6},{8,9},{9,8},{10,11... | collective-permute-start | bytes 1179656 | tf_op jit(solution)/shard_map/ppermute | solution.py:310
  104.0 24.3 %collective-permute-start.3 = (bf16[64,3,8,128]{3,2,1,0:T(8,128)(2,1)S(1)}, bf16[64,3,8,128]{3,2,1,0:T(8,128)(2,1)S(1)}, u32[]{:S(2)}, u32[]{:S(2)}) collective-permute-start(bf16[64,3,8,128]{3,2,1,0:T(8,128)(2,1)S(1)} %get-tuple-element.11), channel_id=1, source_target_pairs={{0,129},{129,0},{1,128},{128,1},{2,131},{131,2},{3,130},{130,3},{4... | collective-permute-start | bytes 1179656 | tf_op jit(solution)/shard_map/ppermute | solution.py:309
  104.0 24.3 %collective-permute-start.2 = (bf16[64,3,8,128]{3,2,1,0:T(8,128)(2,1)S(1)}, bf16[64,3,8,128]{3,2,1,0:T(8,128)(2,1)S(1)}, u32[]{:S(2)}, u32[]{:S(2)}) collective-permute-start(bf16[64,3,8,128]{3,2,1,0:T(8,128)(2,1)S(1)} %get-tuple-element.11), channel_id=1, source_target_pairs={{0,128},{128,0},{1,129},{129,1},{2,130},{130,2},{3,131},{131,3},{4... | collective-permute-start | bytes 1179656 | tf_op jit(solution)/shard_map/ppermute | solution.py:308
where the time goes:
time: 133 us
  blocking collectives  47 us (35%)
  waiting for transfers between devices  36.1 us (27%)
  Pallas kernels  22.7 us (17%)
  starting transfers between devices  19.9 us (15%)
  local copies, waits for them, and re-layouts  6.79 us (5%)
    all_to_all x1, blocking collectives, local(): lax.all_to_all(part, PLANE, split_axis=0, concat_axis=0, tiled=True)  47 us
    all_to_all x1, waiting for transfers between devices, local(): lax.all_to_all(part, PLANE, split_axis=0, concat_axis=0, tiled=True)  17.8 us
    ppermute x2, waiting for transfers between devices, exchange(): cross = lax.ppermute(near_part, ('y_lo', 'tm'), both)  16.3 us
    pallas_call x2, Pallas kernels, correlate(): pl.pallas_call(kernel, grid_spec=pltpu.PrefetchScalarGridSpec(num_scalar_...  11.4 us
    pallas_call x1, Pallas kernels, channelize(): pl.pallas_call(channel_kernel, grid_spec=pltpu.PrefetchScalarGridSpec(num...  11.2 us
    ppermute x2, starting transfers between devices, exchange(): far = lax.ppermute(far_part, 'tm', flip)  7.34 us
    all_to_all x1, starting transfers between devices, local(): lax.all_to_all(part, PLANE, split_axis=0, concat_axis=0, tiled=True)  6.16 us
    ppermute x1, starting transfers between devices, local(): tail = lax.ppermute(volts[:, (SPEC - HIST) * ROWS:], 'tm', [(0, 1)])  5.64 us
  transfers between devices with their start and end apart: 8, of which 5 were waited for; matrix products, arithmetic and copies ran while one was open for 1% of the time, Pallas kernels for 5%

commit v1 on v0

v1 whole, which is shorter than its diff:
```python
import jax
import jax.numpy as jnp
import numpy as np
from jax import lax
from jax.experimental import pallas as pl
from jax.experimental.pallas import tpu as pltpu
from jax.sharding import Mesh
from jax.sharding import PartitionSpec as P

NCH = 1024
TAPS = 4
RADIX = 8
FINE = NCH // RADIX
LANES = 128
NA = 4
SPEC = 128
STEP = 32
BATCH = 8
HIST = TAPS - 1
ROWS = RADIX * NA
GROUP = 64
PLANE = ("x", "z", "core")
PLANE_FIRST = (0, 1, 2, 3, 4)
Y_FIRST = (5, 6, 7)


def taps_table():
    k = jnp.arange(TAPS * NCH, dtype=jnp.float32)
    x = (k - 2.0 * NCH + 0.5) / NCH
    window = 0.54 - 0.46 * jnp.cos(2.0 * jnp.pi * (k + 0.5) / (TAPS * NCH))
    taps = (jnp.sinc(x) * window * 0.25).reshape(TAPS, RADIX, 1, LANES)
    return jnp.broadcast_to(taps, (TAPS, RADIX, NA, LANES)).reshape(TAPS, ROWS, LANES)


def turn_table():
    j = np.arange(RADIX)[:, None, None]
    q = np.arange(FINE)[None, :, None]
    l = np.arange(FINE)[None, None, :]
    angle = 2.0 * np.pi * ((l * (RADIX * q + j)) % NCH) / NCH
    cosine = np.cos(angle) / np.sqrt(NCH)
    sine = np.sin(angle) / np.sqrt(NCH)
    real = np.concatenate([cosine, sine], axis=2)
    imag = np.concatenate([-sine, cosine], axis=2)
    full = np.concatenate([real, imag], axis=1)
    high = full.astype(jnp.bfloat16)
    low = (full - high.astype(np.float64)).astype(jnp.bfloat16)
    return np.stack([high, low], axis=1)


def gather_table():
    table = np.zeros((256, 256), np.float32)
    for p in range(2):
        for r in range(32):
            for a in range(NA):
                table[p * 128 + r * NA + a, r * 8 + p * NA + a] = 1.0
    return table.astype(jnp.bfloat16)


def butterfly(x):
    def add(u, v):
        return (u[0] + v[0], u[1] + v[1])

    def sub(u, v):
        return (u[0] - v[0], u[1] - v[1])

    def minus_i(u):
        return (u[1], -u[0])

    def four(a, b, c, d):
        s, t = add(a, c), sub(a, c)
        u, v = add(b, d), minus_i(sub(b, d))
        return add(s, u), add(t, v), sub(s, u), sub(t, v)

    half = np.float32(np.sqrt(0.5))
    even = four(x[0], x[2], x[4], x[6])
    odd = four(x[1], x[3], x[5], x[7])
    o1 = ((odd[1][0] + odd[1][1]) * half, (odd[1][1] - odd[1][0]) * half)
    o2 = minus_i(odd[2])
    o3 = ((odd[3][1] - odd[3][0]) * half, -(odd[3][0] + odd[3][1]) * half)
    odd = (odd[0], o1, o2, o3)
    return [add(even[i], odd[i]) for i in range(4)] + [sub(even[i], odd[i]) for i in range(4)]


def channel_kernel(place, volts, tail, taps, turn, stay, leave, rest, raw, filt, high, low, table, spread, arrived):
    def chunk_copy(c):
        at = pl.multiple_of(c * STEP * ROWS, STEP * ROWS)
        return pltpu.make_async_copy(
            volts.at[:, pl.ds(at, STEP * ROWS), :],
            raw.at[:, pl.ds(HIST * ROWS + at, STEP * ROWS), :],
            arrived.at[c],
        )

    table_copy = pltpu.make_async_copy(turn, table, arrived.at[SPEC // STEP])
    for c in range(SPEC // STEP):
        chunk_copy(c).start()
    table_copy.start()
    raw[:, : HIST * ROWS, :] = tail[...]

    @pl.loop(0, SPEC // STEP)
    def _(c):
        chunk_copy(c).wait()
        for p in range(2):

            @pl.loop(0, STEP // BATCH)
            def _(i):
                into = pl.multiple_of(i * BATCH * ROWS, BATCH * ROWS)
                base = pl.multiple_of(c * STEP * ROWS + into, BATCH * ROWS)
                for piece in range(ROWS // 8):
                    weights = [taps[t, piece * 8 : piece * 8 + 8, :] for t in range(TAPS)]
                    frames = [
                        raw[p, pl.ds(base + (s * ROWS + piece * 8), 8), :].astype(jnp.float32)
                        for s in range(BATCH + HIST)
                    ]
                    for s in range(BATCH):
                        total = weights[0] * frames[s]
                        for t in range(1, TAPS):
                            total = total + weights[t] * frames[s + t]
                        filt[p, pl.ds(into + (s * ROWS + piece * 8), 8), :] = total

        for a in range(NA):
            for part in range(STEP // 16):
                x = [
                    tuple(
                        filt[p, pl.ds(part * 16 * ROWS + m * NA + a, 16, stride=ROWS), :]
                        for p in range(2)
                    )
                    for m in range(RADIX)
                ]
                y = butterfly(x)
                row = pl.multiple_of(a * SPEC + c * STEP + part * 16, 16)
                for j in range(RADIX):
                    for p in range(2):
                        value = y[j][p]
                        top = value.astype(jnp.bfloat16)
                        left_over = (value - top.astype(jnp.float32)).astype(jnp.bfloat16)
                        high[j, pl.ds(row, 16), p * LANES : (p + 1) * LANES] = top
                        low[j, pl.ds(row, 16), p * LANES : (p + 1) * LANES] = left_over

    table_copy.wait()
    mine = place[0]

    def dot(left, right):
        return lax.dot_general(
            left, right, (((1,), (1,)), ((), ())), preferred_element_type=jnp.float32
        )

    def transform(j):
        rows = []
        for kind in range(2):
            pieces = []
            for p in range(2):
                for slot in range(2):
                    half = mine if slot == 0 else 1 - mine
                    start = pl.multiple_of(p * FINE + half * GROUP, GROUP)
                    pieces.append(table[j, kind, pl.ds(start, GROUP), :])
            rows.append(jnp.concatenate(pieces, axis=0))
        tops = high[j]
        spectra = dot(rows[0], tops) + (dot(rows[1], tops) + dot(rows[0], low[j]))
        blocks = []
        for slot in range(2):
            for p in range(2):
                for a in range(NA):
                    spread[
                        pl.ds(slot * GROUP * 8 + p * NA + a, GROUP, stride=8), :
                    ] = spectra[
                        (p * 2 + slot) * GROUP : (p * 2 + slot + 1) * GROUP,
                        a * SPEC : (a + 1) * SPEC,
                    ]
            block = spread[slot * GROUP * 8 : (slot + 1) * GROUP * 8, :]
            blocks.append(block.reshape(GROUP, 8, LANES).astype(jnp.bfloat16))
        return blocks

    for i, j in enumerate(PLANE_FIRST):
        blocks = transform(j)
        for slot in range(2):
            rest[:, slot, i] = blocks[slot]

    for i, j in enumerate(Y_FIRST):
        stay[:, i], leave[:, i] = transform(j)


def channelize(place, volts, tail):
    few, many = len(Y_FIRST), len(PLANE_FIRST)
    vmem = pl.BlockSpec(memory_space=pltpu.VMEM)
    hbm = pl.BlockSpec(memory_space=pltpu.HBM)
    return pl.pallas_call(
        channel_kernel,
        in_specs=[pl.BlockSpec(memory_space=pltpu.SMEM), hbm, vmem, vmem, hbm],
        out_specs=[vmem, vmem, vmem],
        scratch_shapes=[
            pltpu.VMEM((2, (HIST + SPEC) * ROWS, LANES), jnp.int32),
            pltpu.VMEM((2, STEP * ROWS, LANES), jnp.float32),
            pltpu.VMEM((RADIX, NA * SPEC, 2 * LANES), jnp.bfloat16),
            pltpu.VMEM((RADIX, NA * SPEC, 2 * LANES), jnp.bfloat16),
            pltpu.VMEM((RADIX, 2, 2 * FINE, 2 * FINE), jnp.bfloat16),
            pltpu.VMEM((2 * GROUP * 8, LANES), jnp.float32),
            pltpu.SemaphoreType.DMA((SPEC // STEP + 1,)),
        ],
        out_shape=[
            jax.ShapeDtypeStruct((GROUP, few, 8, LANES), jnp.bfloat16),
            jax.ShapeDtypeStruct((GROUP, few, 8, LANES), jnp.bfloat16),
            jax.ShapeDtypeStruct((GROUP, 2, many, 8, LANES), jnp.bfloat16),
        ],
        compiler_params=pltpu.CompilerParams(vmem_limit_bytes=52 * 1024 * 1024),
        cost_estimate=pl.CostEstimate(
            flops=2 * 10**9, bytes_accessed=8 * 1024 * 1024, transcendentals=0
        ),
        name="channelize",
    )(place, volts, tail, taps_table(), jnp.asarray(turn_table()))


def correlate_kernel(scale, first, count, picks, place, *refs):
    operands, table, out = refs[: len(picks)], refs[len(picks)], refs[-3]
    held, sent = refs[-2:]
    mine, time = place[0], place[1]
    low_first = mine == 0

    def dot(left, right):
        return lax.dot_general(
            left, right, (((1,), (1,)), ((), ())), preferred_element_type=jnp.float32
        )

    def give(i):
        slot = i % 2
        return pltpu.make_async_copy(held.at[slot], out.at[:, first + i], sent.at[slot])

    for i in range(count):
        sets = []
        for kind in range(2):
            pair = [
                ref[:, at, i] if at is not None else ref[:, i]
                for ref, at in zip(operands[2 * kind : 2 * kind + 2], picks[2 * kind : 2 * kind + 2])
            ]
            pair = [block.reshape(GROUP * 8, LANES) for block in pair]
            parts = ([], [])
            for half in range(2):
                block = jnp.concatenate([b[half * 256 : half * 256 + 256] for b in pair], axis=1)
                ordered = jnp.dot(table[...], block, preferred_element_type=jnp.float32)
                ordered = ordered.astype(jnp.bfloat16)
                for p in range(2):
                    parts[p].append(ordered[p * 128 : p * 128 + 128])
            sets.append(jnp.concatenate([jnp.concatenate(part, axis=0) for part in parts], axis=1))
        columns = [jnp.where(low_first, sets[0], sets[1]), jnp.where(low_first, sets[1], sets[0])]
        rows = jnp.where(time == 0, columns[0], columns[1])
        turned = jnp.concatenate([rows[:, 256:], -rows[:, :256]], axis=1)

        if i >= 2:
            give(i - 2).wait()
        slot = i % 2
        for group in range(2):
            at = slice(group * 256, group * 256 + 256)
            held[slot, 0, :, at] = dot(rows, columns[group]) * scale
            held[slot, 1, :, at] = dot(turned, columns[group]) * scale
        give(i).start()

    for i in range(max(count - 2, 0), count):
        give(i).wait()


def correlate(place, scale, first, count, kinds, earlier):
    vmem = pl.BlockSpec(memory_space=pltpu.VMEM)
    hbm = pl.BlockSpec(memory_space=pltpu.HBM)
    picks = [at for _, at in kinds]
    operands = [place, *(block for block, _ in kinds), jnp.asarray(gather_table())]
    in_specs = [pl.BlockSpec(memory_space=pltpu.SMEM)] + [vmem] * (len(operands) - 1)
    aliases = {}
    if earlier is not None:
        in_specs.append(hbm)
        aliases = {len(operands): 0}
        operands.append(earlier)

    def kernel(*refs):
        correlate_kernel(scale, first, count, picks, *refs)

    return pl.pallas_call(
        kernel,
        in_specs=in_specs,
        out_specs=hbm,
        scratch_shapes=[
            pltpu.VMEM((2, 2, 256, 512), jnp.float32),
            pltpu.SemaphoreType.DMA((2,)),
        ],
        out_shape=jax.ShapeDtypeStruct((2, 8, 256, 512), jnp.float32),
        input_output_aliases=aliases,
        compiler_params=pltpu.CompilerParams(vmem_limit_bytes=24 * 1024 * 1024),
        cost_estimate=pl.CostEstimate(
            flops=count * 4 * 10**8, bytes_accessed=count * 3 * 512 * 1024, transcendentals=0
        ),
        name="correlate",
    )(*operands)


def exchange(near_part, far_part):
    flip = [(0, 1), (1, 0)]
    both = [(0, 3), (3, 0), (1, 2), (2, 1)]
    near = lax.ppermute(near_part, "y_lo", flip)
    cross = lax.ppermute(near_part, ("y_lo", "tm"), both)
    far = lax.ppermute(far_part, "tm", flip)
    return far, near, cross


def local(voltages):
    tiles = voltages.shape[2] // LANES
    volts = voltages.reshape(2, NA, tiles, LANES).transpose(0, 2, 1, 3).reshape(2, tiles * NA, LANES)
    tail = lax.ppermute(volts[:, (SPEC - HIST) * ROWS :], "tm", [(0, 1)])
    place = jnp.stack([lax.axis_index("y_lo"), lax.axis_index("tm")]).astype(jnp.int32)
    scale = np.float32(1.0 / (SPEC * lax.axis_size("tm")))
    stay, leave, rest = channelize(place, volts, tail)
    over = lax.all_to_all(rest, PLANE, split_axis=0, concat_axis=0, tiled=True)
    early = jnp.stack([stay, *exchange(leave, stay)], axis=1)
    far, near, cross = exchange(over[:, 1], over[:, 0])
    early = lax.all_to_all(early, PLANE, split_axis=0, concat_axis=0, tiled=True)
    result = correlate(
        place, scale, 0, len(PLANE_FIRST), [(over, 0), (far, None), (near, None), (cross, None)], None
    )
    return correlate(
        place, scale, len(PLANE_FIRST), len(Y_FIRST), [(early, kind) for kind in range(4)], result
    )


def solution(mesh):
    names = ("y_lo", "x", "z", "core", "tm")
    fine = Mesh(mesh.devices.reshape(2, 4, 8, 2, 2), names)
    chan = names[:-1]
    return jax.shard_map(
        local,
        mesh=fine,
        in_specs=P(None, chan, "tm"),
        out_specs=P(None, chan, "tm", None),
        check_vma=False,
    )
```

time: 133 us -> 115 us (0.86)
  blocking collectives: 47 us -> 0 us
  waiting for transfers between devices: 36.1 us -> 60.5 us
  starting transfers between devices: 19.9 us -> 33.1 us
  local copies, waits for them, and re-layouts: 6.79 us -> 1.03 us
  Pallas kernels: 22.7 us -> 18.2 us
  other arithmetic: 0.08 us -> 1.53 us
    all_to_all x1 -> x0, blocking collectives: 47 us -> none  [local(): lax.all_to_all(part, PLANE, split_axis=0, concat_axis=0, tiled=True)]
    ppermute x2, waiting for transfers between devices: 0.45 us -> 23.1 us  [exchange(): far = lax.ppermute(far_part, 'tm', flip)]
    all_to_all x1 -> x2, starting transfers between devices: 6.16 us -> 19.2 us  [the longest x1 13 us: local(): over = lax.all_to_all(rest, PLANE, split_axis=0, concat_axis=0, tiled=True)]
    ppermute x2, waiting for transfers between devices: 16.3 us -> 23.3 us  [exchange(): cross = lax.ppermute(near_part, ('y_lo', 'tm'), both)]
    all_to_all x1 -> x2, waiting for transfers between devices: 17.8 us -> 12.7 us  [the longest x1 11.1 us: local(): over = lax.all_to_all(rest, PLANE, split_axis=0, concat_axis=0, tiled=True)]
    unnamed x8 -> x2, local copies, waits for them, and re-layouts: 4.62 us -> 0.01 us
    pallas_call x3, Pallas kernels: 22.7 us -> 18.2 us  [the longest x1 9.36 us: channelize(): pl.pallas_call(channel_kernel, in_specs=[pl.BlockSpec(memory_space=pltpu....]
    another operation x0 -> x1, other arithmetic: none -> 1.35 us  [local(): early = jnp.stack([stay, *exchange(leave, stay)], axis=1)]
  transfers between devices with their start and end apart: 8 -> 9, of which waited for: 5 -> 7; matrix products, arithmetic and copies ran while one was open for 1% -> 1% of each run, Pallas kernels for 5% -> 4%
where the time goes in v1:
time: 115 us
  waiting for transfers between devices  60.5 us (53%)
  starting transfers between devices  33.1 us (29%)
  Pallas kernels  18.2 us (16%)
  other arithmetic  1.53 us (1%)
    ppermute x2, waiting for transfers between devices, exchange(): cross = lax.ppermute(near_part, ('y_lo', 'tm'), both)  23.3 us
    ppermute x2, waiting for transfers between devices, exchange(): far = lax.ppermute(far_part, 'tm', flip)  23.1 us
    all_to_all x1, starting transfers between devices, local(): over = lax.all_to_all(rest, PLANE, split_axis=0, concat_axis=0, tiled=True)  13 us
    all_to_all x1, waiting for transfers between devices, local(): over = lax.all_to_all(rest, PLANE, split_axis=0, concat_axis=0, tiled=True)  11.1 us
    pallas_call x1, Pallas kernels, channelize(): pl.pallas_call(channel_kernel, in_specs=[pl.BlockSpec(memory_space=pltpu....  9.36 us
    pallas_call x2, Pallas kernels, correlate(): pl.pallas_call(kernel, in_specs=in_specs, out_specs=hbm, scratch_shapes=[...  8.8 us
    ppermute x2, starting transfers between devices, exchange(): far = lax.ppermute(far_part, 'tm', flip)  7.44 us
    all_to_all x1, starting transfers between devices, local(): lax.all_to_all(early, PLANE, split_axis=0, concat_axis=0, tiled=True)  6.16 us
  transfers between devices with their start and end apart: 9, of which 7 were waited for; matrix products, arithmetic and copies ran while one was open for 1% of the time, Pallas kernels for 4%

profile of v1, /device:TPU:1, one launch (start us, length us, event | category | flops | bytes accessed | tf_op | source)
XLA Modules:
  0.0 114.6 jit_solution(15177916820165757467)
XLA Ops:
  0.0 0.9 slice.12
  0.9 5.6 %collective-permute-start = (s32[2,96,128]{2,1,0:T(8,128)S(1)}, s32[2,96,128]{2,1,0:T(8,128)S(1)}, u32[]{:S(2)}, u32[]{:S(2)}) collective-permute-start(s32[2,96,128]{2,1,0:T(8,128)S(1)} %slice.12), channel_id=1, source_target_pairs={{0,1},{2,3},{4,5},{6,7},{8,9},{10,11},{12,13},{14,15},{16,17},{18,... | collective-permute-start | bytes 294920 | tf_op jit(solution)/shard_map/ppermute | solution.py:305
  6.6 0.1 fusion.13
  6.7 0.1 pad_add_fusion.place.refs_0_
  6.7 1.4 %collective-permute-done.tail = s32[2,96,128]{2,1,0:T(8,128)S(1)} collective-permute-done((s32[2,96,128]{2,1,0:T(8,128)S(1)}, s32[2,96,128]{2,1,0:T(8,128)S(1)}, u32[]{:S(2)}, u32[]{:S(2)}) %collective-permute-start) | collective-permute-done | bytes 98336 | tf_op jit(solution)/shard_map/ppermute | solution.py:305
  8.2 9.4 %channelize.1 = (bf16[64,3,8,128]{3,2,1,0:T(8,128)(2,1)S(1)}, bf16[64,3,8,128]{3,2,1,0:T(8,128)(2,1)S(1)}, bf16[64,2,5,8,128]{4,3,2,1,0:T(8,128)(2,1)}) custom-call(s32[2]{0:T(128)S(1)} %pad_add_fusion.place.refs_0_, s32[2,4096,128]{2,1,0:T(8,128)} %bitcast.26, s32[2,96,128]{2,1,0:T(8,128)S(1)} %collective-permute-done.tail, f32[4,32,128]{2,1,0:T(8,128)S(1)} %bitcast.21, ...), custom_call_target="tpu_custom_call" | custom-call | flops 2000000000 | bytes 8388608 | tf_op jit(solution)/shard_map/channelize/pallas_call | solution.py:186
  17.5 13.0 %all-to-all-start.1 = ((bf16[64,2,5,8,128]{4,3,2,1,0:T(8,128)(2,1)}), bf16[64,2,5,8,128]{4,3,2,1,0:T(8,128)(2,1)S(1)}, u32[]{:S(2)}, u32[]{:S(2)}) async-start(bf16[64,2,5,8,128]{4,3,2,1,0:T(8,128)(2,1)} %get-tuple-element.10), calls=%async_computation.1 | async-start | bytes 2621440 | tf_op jit(solution)/shard_map/all_to_all | solution.py:309
  30.6 3.7 %collective-permute-start.1 = (bf16[64,3,8,128]{3,2,1,0:T(8,128)(2,1)S(1)}, bf16[64,3,8,128]{3,2,1,0:T(8,128)(2,1)S(1)}, u32[]{:S(2)}, u32[]{:S(2)}) collective-permute-start(bf16[64,3,8,128]{3,2,1,0:T(8,128)(2,1)S(1)} %get-tuple-element.8), channel_id=1, source_target_pairs={{0,1},{1,0},{2,3},{3,2},{4,5},{5,4},{6,7},{7,6},{8,9},{9,8},{10,11... | collective-permute-start | bytes 1179656 | tf_op jit(solution)/shard_map/ppermute | solution.py:298
  34.3 0.0 collective-permute-start.3
  34.3 0.4 collective-permute-start.2
  34.7 8.7 %collective-permute-done.1 = bf16[64,3,8,128]{3,2,1,0:T(8,128)(2,1)S(1)} collective-permute-done((bf16[64,3,8,128]{3,2,1,0:T(8,128)(2,1)S(1)}, bf16[64,3,8,128]{3,2,1,0:T(8,128)(2,1)S(1)}, u32[]{:S(2)}, u32[]{:S(2)}) %collective-permute-start.1) | collective-permute-done | bytes 393248 | tf_op jit(solution)/shard_map/ppermute | solution.py:298
  43.4 8.9 %collective-permute-done.3 = bf16[64,3,8,128]{3,2,1,0:T(8,128)(2,1)S(1)} collective-permute-done((bf16[64,3,8,128]{3,2,1,0:T(8,128)(2,1)S(1)}, bf16[64,3,8,128]{3,2,1,0:T(8,128)(2,1)S(1)}, u32[]{:S(2)}, u32[]{:S(2)}) %collective-permute-start.3) | collective-permute-done | bytes 393248 | tf_op jit(solution)/shard_map/ppermute | solution.py:297
  52.3 1.4 %pad_maximum_fusion = bf16[64,4,3,8,128]{4,3,2,1,0:T(8,128)(2,1)} fusion(bf16[64,1,3,8,128]{4,3,2,1,0:T(8,128)(2,1)S(1)} %bitcast.23, bf16[64,1,3,8,128]{4,3,2,1,0:T(8,128)(2,1)S(1)} %bitcast.24, bf16[64,1,3,8,128]{4,3,2,1,0:T(8,128)(2,1)S(1)} %bitcast.22, bf16[64,1,3,8,128]{4,3,2,1,0:T(8,128)(2,1)S(1)} %bitcast.20), kind=kLoop, calls=%fused_computation | loop fusion | flops 2359296 | bytes 3145728 | tf_op jit(solution)/shard_map/stack | solution.py:310
  53.7 11.1 %all-to-all-done.1.refs_1_ = bf16[64,2,5,8,128]{4,3,2,1,0:T(8,128)(2,1)S(1)} async-done(((bf16[64,2,5,8,128]{4,3,2,1,0:T(8,128)(2,1)}), bf16[64,2,5,8,128]{4,3,2,1,0:T(8,128)(2,1)S(1)}, u32[]{:S(2)}, u32[]{:S(2)}) %all-to-all-start.1) | async-done | bytes 1310752 | tf_op jit(solution)/shard_map/all_to_all | solution.py:309
  64.7 6.2 %all-to-all-start = ((bf16[64,4,3,8,128]{4,3,2,1,0:T(8,128)(2,1)}), bf16[64,4,3,8,128]{4,3,2,1,0:T(8,128)(2,1)S(1)}, u32[]{:S(2)}, u32[]{:S(2)}) async-start(bf16[64,4,3,8,128]{4,3,2,1,0:T(8,128)(2,1)} %pad_maximum_fusion), calls=%async_computation | async-start | bytes 3145728 | tf_op jit(solution)/shard_map/all_to_all | solution.py:312
  70.9 0.0 copy-start
  70.9 0.1 slice_bitcast_fusion
  71.1 3.7 %collective-permute-start.4 = (bf16[64,5,8,128]{3,2,1,0:T(8,128)(2,1)S(1)}, bf16[64,5,8,128]{3,2,1,0:T(8,128)(2,1)S(1)}, u32[]{:S(2)}, u32[]{:S(2)}) collective-permute-start(bf16[64,5,8,128]{3,2,1,0:T(8,128)(2,1)S(1)} %get-tuple-element.12), channel_id=1, source_target_pairs={{0,1},{1,0},{2,3},{3,2},{4,5},{5,4},{6,7},{7,6},{8,9},{9,8},{10,11... | collective-permute-start | bytes 1966088 | tf_op jit(solution)/shard_map/ppermute | solution.py:298
  74.8 0.4 collective-permute-start.5
  75.2 14.4 %collective-permute-done.4.refs_2_ = bf16[64,5,8,128]{3,2,1,0:T(8,128)(2,1)S(1)} collective-permute-done((bf16[64,5,8,128]{3,2,1,0:T(8,128)(2,1)S(1)}, bf16[64,5,8,128]{3,2,1,0:T(8,128)(2,1)S(1)}, u32[]{:S(2)}, u32[]{:S(2)}) %collective-permute-start.4) | collective-permute-done | bytes 655392 | tf_op jit(solution)/shard_map/ppermute | solution.py:298
  89.5 14.5 %collective-permute-done.6.refs_4_ = bf16[64,5,8,128]{3,2,1,0:T(8,128)(2,1)S(1)} collective-permute-done((bf16[64,5,8,128]{3,2,1,0:T(8,128)(2,1)S(1)}, bf16[64,5,8,128]{3,2,1,0:T(8,128)(2,1)S(1)}, u32[]{:S(2)}, u32[]{:S(2)}) %collective-permute-start.6) | collective-permute-done | bytes 655392 | tf_op jit(solution)/shard_map/ppermute | solution.py:297
  104.0 5.1 %correlate.2.refs_6_ = f32[2,8,256,512]{3,2,1,0:T(8,128)} custom-call(s32[2]{0:T(128)S(1)} %pad_add_fusion.place.refs_0_, bf16[64,2,5,8,128]{4,3,2,1,0:T(8,128)(2,1)S(1)} %all-to-all-done.1.refs_1_, bf16[64,5,8,128]{3,2,1,0:T(8,128)(2,1)S(1)} %collective-permute-done.4.refs_2_, bf16[64,5,8,128]{3,2,1,0:T(8,128)(2,1)S(1)} %collective-permute-done.5.refs_3_, ...), custom_call_target="tpu_custom_call" | custom-call | flops 2000000000 | bytes 7864320 | tf_op jit(solution)/shard_map/correlate/pallas_call | solution.py:275
  109.1 1.6 %all-to-all-done.refs_1_.refs_2_.refs_3_.refs_4_ = bf16[64,4,3,8,128]{4,3,2,1,0:T(8,128)(2,1)S(1)} async-done(((bf16[64,4,3,8,128]{4,3,2,1,0:T(8,128)(2,1)}), bf16[64,4,3,8,128]{4,3,2,1,0:T(8,128)(2,1)S(1)}, u32[]{:S(2)}, u32[]{:S(2)}) %all-to-all-start) | async-done | bytes 1572896 | tf_op jit(solution)/shard_map/all_to_all | solution.py:312
  110.7 3.7 %correlate.3 = f32[2,8,256,512]{3,2,1,0:T(8,128)} custom-call(s32[2]{0:T(128)S(1)} %pad_add_fusion.place.refs_0_, bf16[64,4,3,8,128]{4,3,2,1,0:T(8,128)(2,1)S(1)} %all-to-all-done.refs_1_.refs_2_.refs_3_.refs_4_, bf16[64,4,3,8,128]{4,3,2,1,0:T(8,128)(2,1)S(1)} %all-to-all-done.refs_1_.refs_2_.refs_3_.refs_4_, ...), custom_call_target="tpu_custom_call", output_to_operand_aliasing={{}: (6, {})} | custom-call | flops 1200000000 | bytes 4718592 | tf_op jit(solution)/shard_map/correlate/pallas_call | solution.py:275
  (5 shorter events, 0.0 us)
Async XLA Ops:
  0.9 7.3 %collective-permute-start = (s32[2,96,128]{2,1,0:T(8,128)S(1)}, s32[2,96,128]{2,1,0:T(8,128)S(1)}, u32[]{:S(2)}, u32[]{:S(2)}) collective-permute-start(s32[2,96,128]{2,1,0:T(8,128)S(1)} %slice.12), channel_id=1, source_target_pairs={{0,1},{2,3},{4,5},{6,7},{8,9},{10,11},{12,13},{14,15},{16,17},{18,... | collective-permute-start | bytes 294920 | tf_op jit(solution)/shard_map/ppermute | solution.py:305
  17.5 47.2 %all-to-all-start.1 = ((bf16[64,2,5,8,128]{4,3,2,1,0:T(8,128)(2,1)}), bf16[64,2,5,8,128]{4,3,2,1,0:T(8,128)(2,1)S(1)}, u32[]{:S(2)}, u32[]{:S(2)}) async-start(bf16[64,2,5,8,128]{4,3,2,1,0:T(8,128)(2,1)} %get-tuple-element.10), calls=%async_computation.1 | async-start | bytes 2621440 | tf_op jit(solution)/shard_map/all_to_all | solution.py:309
  30.6 12.9 %collective-permute-start.1 = (bf16[64,3,8,128]{3,2,1,0:T(8,128)(2,1)S(1)}, bf16[64,3,8,128]{3,2,1,0:T(8,128)(2,1)S(1)}, u32[]{:S(2)}, u32[]{:S(2)}) collective-permute-start(bf16[64,3,8,128]{3,2,1,0:T(8,128)(2,1)S(1)} %get-tuple-element.8), channel_id=1, source_target_pairs={{0,1},{1,0},{2,3},{3,2},{4,5},{5,4},{6,7},{7,6},{8,9},{9,8},{10,11... | collective-permute-start | bytes 1179656 | tf_op jit(solution)/shard_map/ppermute | solution.py:298
  34.3 18.0 %collective-permute-start.3 = (bf16[64,3,8,128]{3,2,1,0:T(8,128)(2,1)S(1)}, bf16[64,3,8,128]{3,2,1,0:T(8,128)(2,1)S(1)}, u32[]{:S(2)}, u32[]{:S(2)}) collective-permute-start(bf16[64,3,8,128]{3,2,1,0:T(8,128)(2,1)S(1)} %get-tuple-element.9), channel_id=1, source_target_pairs={{0,129},{129,0},{1,128},{128,1},{2,131},{131,2},{3,130},{130,3},{4... | collective-permute-start | bytes 1179656 | tf_op jit(solution)/shard_map/ppermute | solution.py:297
  34.3 18.0 %collective-permute-start.2 = (bf16[64,3,8,128]{3,2,1,0:T(8,128)(2,1)S(1)}, bf16[64,3,8,128]{3,2,1,0:T(8,128)(2,1)S(1)}, u32[]{:S(2)}, u32[]{:S(2)}) collective-permute-start(bf16[64,3,8,128]{3,2,1,0:T(8,128)(2,1)S(1)} %get-tuple-element.9), channel_id=1, source_target_pairs={{0,128},{128,0},{1,129},{129,1},{2,130},{130,2},{3,131},{131,3},{4... | collective-permute-start | bytes 1179656 | tf_op jit(solution)/shard_map/ppermute | solution.py:296
  64.7 46.0 %all-to-all-start = ((bf16[64,4,3,8,128]{4,3,2,1,0:T(8,128)(2,1)}), bf16[64,4,3,8,128]{4,3,2,1,0:T(8,128)(2,1)S(1)}, u32[]{:S(2)}, u32[]{:S(2)}) async-start(bf16[64,4,3,8,128]{4,3,2,1,0:T(8,128)(2,1)} %pad_maximum_fusion), calls=%async_computation | async-start | bytes 3145728 | tf_op jit(solution)/shard_map/all_to_all | solution.py:312
  70.9 33.1 %copy-start = (bf16[256,256]{1,0:T(8,128)(2,1)S(1)}, bf16[256,256]{1,0:T(8,128)(2,1)}, u32[]{:S(2)}) copy-start(bf16[256,256]{1,0:T(8,128)(2,1)} %constant.83.clone.refs_5_) | copy-start | bytes 393220
  71.1 18.5 %collective-permute-start.4 = (bf16[64,5,8,128]{3,2,1,0:T(8,128)(2,1)S(1)}, bf16[64,5,8,128]{3,2,1,0:T(8,128)(2,1)S(1)}, u32[]{:S(2)}, u32[]{:S(2)}) collective-permute-start(bf16[64,5,8,128]{3,2,1,0:T(8,128)(2,1)S(1)} %get-tuple-element.12), channel_id=1, source_target_pairs={{0,1},{1,0},{2,3},{3,2},{4,5},{5,4},{6,7},{7,6},{8,9},{9,8},{10,11... | collective-permute-start | bytes 1966088 | tf_op jit(solution)/shard_map/ppermute | solution.py:298
  74.8 29.2 %collective-permute-start.6 = (bf16[64,5,8,128]{3,2,1,0:T(8,128)(2,1)S(1)}, bf16[64,5,8,128]{3,2,1,0:T(8,128)(2,1)S(1)}, u32[]{:S(2)}, u32[]{:S(2)}) collective-permute-start(bf16[64,5,8,128]{3,2,1,0:T(8,128)(2,1)S(1)} %get-tuple-element.11), channel_id=1, source_target_pairs={{0,129},{129,0},{1,128},{128,1},{2,131},{131,2},{3,130},{130,3},{4... | collective-permute-start | bytes 1966088 | tf_op jit(solution)/shard_map/ppermute | solution.py:297
  74.8 29.2 %collective-permute-start.5 = (bf16[64,5,8,128]{3,2,1,0:T(8,128)(2,1)S(1)}, bf16[64,5,8,128]{3,2,1,0:T(8,128)(2,1)S(1)}, u32[]{:S(2)}, u32[]{:S(2)}) collective-permute-start(bf16[64,5,8,128]{3,2,1,0:T(8,128)(2,1)S(1)} %get-tuple-element.11), channel_id=1, source_target_pairs={{0,128},{128,0},{1,129},{129,1},{2,130},{130,2},{3,131},{131,3},{4... | collective-permute-start | bytes 1966088 | tf_op jit(solution)/shard_map/ppermute | solution.py:296

commit v2 on v1

--- a/solution.py
+++ b/solution.py
@@ -16,6 +16,8 @@
 SPEC = 128
 STEP = 32
 BATCH = 8
+SLOTS = 5
+VMEM_KIB = 50 * 1024
 HIST = TAPS - 1
 ROWS = RADIX * NA
 GROUP = 64
@@ -44,7 +46,8 @@
     full = np.concatenate([real, imag], axis=1)
     high = full.astype(jnp.bfloat16)
     low = (full - high.astype(np.float64)).astype(jnp.bfloat16)
-    return np.stack([high, low], axis=1)
+    blank = np.zeros_like(high)
+    return np.stack([high, low, blank, blank], axis=1)
 
 
 def gather_table():
@@ -81,7 +84,41 @@
     return [add(even[i], odd[i]) for i in range(4)] + [sub(even[i], odd[i]) for i in range(4)]
 
 
-def channel_kernel(place, volts, tail, taps, turn, stay, leave, rest, raw, filt, high, low, table, spread, arrived):
+def transform(mine, j, table, high, low, spread):
+    def dot(left, right):
+        return lax.dot_general(
+            left, right, (((1,), (1,)), ((), ())), preferred_element_type=jnp.float32
+        )
+
+    rows = []
+    for kind in range(2):
+        pieces = []
+        for p in range(2):
+            for slot in range(2):
+                half = mine if slot == 0 else 1 - mine
+                start = pl.multiple_of(p * FINE + half * GROUP, GROUP)
+                pieces.append(table[j, kind, pl.ds(start, GROUP), :])
+        rows.append(jnp.concatenate(pieces, axis=0))
+    tops = high[j]
+    spectra = dot(rows[0], tops) + (dot(rows[1], tops) + dot(rows[0], low[j]))
+    blocks = []
+    for slot in range(2):
+        for p in range(2):
+            for a in range(NA):
+                spread[
+                    pl.ds(slot * GROUP * 8 + p * NA + a, GROUP, stride=8), :
+                ] = spectra[
+                    (p * 2 + slot) * GROUP : (p * 2 + slot + 1) * GROUP,
+                    a * SPEC : (a + 1) * SPEC,
+                ]
+        block = spread[slot * GROUP * 8 : (slot + 1) * GROUP * 8, :]
+        blocks.append(block.reshape(GROUP, 8, LANES).astype(jnp.bfloat16))
+    return blocks
+
+
+def channel_kernel(
+    place, volts, tail, taps, turn, rest, late_high, late_low, raw, filt, high, low, table, spread, arrived
+):
     def chunk_copy(c):
         at = pl.multiple_of(c * STEP * ROWS, STEP * ROWS)
         return pltpu.make_async_copy(
@@ -90,7 +127,9 @@
             arrived.at[c],
         )
 
-    table_copy = pltpu.make_async_copy(turn, table, arrived.at[SPEC // STEP])
+    table_copy = pltpu.make_async_copy(
+        turn.at[pl.ds(0, len(PLANE_FIRST)), pl.ds(0, 2)], table, arrived.at[SPEC // STEP]
+    )
     for c in range(SPEC // STEP):
         chunk_copy(c).start()
     table_copy.start()
@@ -133,56 +172,34 @@
                         value = y[j][p]
                         top = value.astype(jnp.bfloat16)
                         left_over = (value - top.astype(jnp.float32)).astype(jnp.bfloat16)
-                        high[j, pl.ds(row, 16), p * LANES : (p + 1) * LANES] = top
-                        low[j, pl.ds(row, 16), p * LANES : (p + 1) * LANES] = left_over
+                        at = (slice(p * LANES, (p + 1) * LANES),)
+                        early = j < len(PLANE_FIRST)
+                        here = j if early else j - len(PLANE_FIRST)
+                        (high if early else late_high)[here, pl.ds(row, 16), *at] = top
+                        (low if early else late_low)[here, pl.ds(row, 16), *at] = left_over
 
     table_copy.wait()
-    mine = place[0]
-
-    def dot(left, right):
-        return lax.dot_general(
-            left, right, (((1,), (1,)), ((), ())), preferred_element_type=jnp.float32
-        )
-
-    def transform(j):
-        rows = []
-        for kind in range(2):
-            pieces = []
-            for p in range(2):
-                for slot in range(2):
-                    half = mine if slot == 0 else 1 - mine
-                    start = pl.multiple_of(p * FINE + half * GROUP, GROUP)
-                    pieces.append(table[j, kind, pl.ds(start, GROUP), :])
-            rows.append(jnp.concatenate(pieces, axis=0))
-        tops = high[j]
-        spectra = dot(rows[0], tops) + (dot(rows[1], tops) + dot(rows[0], low[j]))
-        blocks = []
-        for slot in range(2):
-            for p in range(2):
-                for a in range(NA):
-                    spread[
-                        pl.ds(slot * GROUP * 8 + p * NA + a, GROUP, stride=8), :
-                    ] = spectra[
-                        (p * 2 + slot) * GROUP : (p * 2 + slot + 1) * GROUP,
-                        a * SPEC : (a + 1) * SPEC,
-                    ]
-            block = spread[slot * GROUP * 8 : (slot + 1) * GROUP * 8, :]
-            blocks.append(block.reshape(GROUP, 8, LANES).astype(jnp.bfloat16))
-        return blocks
-
-    for i, j in enumerate(PLANE_FIRST):
-        blocks = transform(j)
+    for i in range(len(PLANE_FIRST)):
+        blocks = transform(place[0], i, table, high, low, spread)
         for slot in range(2):
             rest[:, slot, i] = blocks[slot]
 
-    for i, j in enumerate(Y_FIRST):
-        stay[:, i], leave[:, i] = transform(j)
-
-
-def channelize(place, volts, tail):
+
+def late_kernel(place, turn, high, low, stay, leave, table, spread, arrived):
+    table_copy = pltpu.make_async_copy(
+        turn.at[pl.ds(len(PLANE_FIRST), len(Y_FIRST)), pl.ds(0, 2)], table, arrived
+    )
+    table_copy.start()
+    table_copy.wait()
+    for i in range(len(Y_FIRST)):
+        stay[:, i], leave[:, i] = transform(place[0], i, table, high, low, spread)
+
+
+def channelize(place, volts, tail, turn):
     few, many = len(Y_FIRST), len(PLANE_FIRST)
     vmem = pl.BlockSpec(memory_space=pltpu.VMEM)
     hbm = pl.BlockSpec(memory_space=pltpu.HBM)
+    mixed = jax.ShapeDtypeStruct((few, NA * SPEC, 2 * LANES), jnp.bfloat16)
     return pl.pallas_call(
         channel_kernel,
         in_specs=[pl.BlockSpec(memory_space=pltpu.SMEM), hbm, vmem, vmem, hbm],
@@ -190,23 +207,42 @@
         scratch_shapes=[
             pltpu.VMEM((2, (HIST + SPEC) * ROWS, LANES), jnp.int32),
             pltpu.VMEM((2, STEP * ROWS, LANES), jnp.float32),
-            pltpu.VMEM((RADIX, NA * SPEC, 2 * LANES), jnp.bfloat16),
-            pltpu.VMEM((RADIX, NA * SPEC, 2 * LANES), jnp.bfloat16),
-            pltpu.VMEM((RADIX, 2, 2 * FINE, 2 * FINE), jnp.bfloat16),
+            pltpu.VMEM((many, NA * SPEC, 2 * LANES), jnp.bfloat16),
+            pltpu.VMEM((many, NA * SPEC, 2 * LANES), jnp.bfloat16),
+            pltpu.VMEM((many, 2, 2 * FINE, 2 * FINE), jnp.bfloat16),
             pltpu.VMEM((2 * GROUP * 8, LANES), jnp.float32),
             pltpu.SemaphoreType.DMA((SPEC // STEP + 1,)),
         ],
-        out_shape=[
-            jax.ShapeDtypeStruct((GROUP, few, 8, LANES), jnp.bfloat16),
-            jax.ShapeDtypeStruct((GROUP, few, 8, LANES), jnp.bfloat16),
-            jax.ShapeDtypeStruct((GROUP, 2, many, 8, LANES), jnp.bfloat16),
-        ],
-        compiler_params=pltpu.CompilerParams(vmem_limit_bytes=52 * 1024 * 1024),
+        out_shape=[jax.ShapeDtypeStruct((GROUP, 2, many, 8, LANES), jnp.bfloat16), mixed, mixed],
+        compiler_params=pltpu.CompilerParams(vmem_limit_bytes=VMEM_KIB * 1024),
         cost_estimate=pl.CostEstimate(
             flops=2 * 10**9, bytes_accessed=8 * 1024 * 1024, transcendentals=0
         ),
         name="channelize",
-    )(place, volts, tail, taps_table(), jnp.asarray(turn_table()))
+    )(place, volts, tail, taps_table(), turn)
+
+
+def channelize_late(place, turn, high, low):
+    few = len(Y_FIRST)
+    vmem = pl.BlockSpec(memory_space=pltpu.VMEM)
+    hbm = pl.BlockSpec(memory_space=pltpu.HBM)
+    block = jax.ShapeDtypeStruct((GROUP, few, 8, LANES), jnp.bfloat16)
+    return pl.pallas_call(
+        late_kernel,
+        in_specs=[pl.BlockSpec(memory_space=pltpu.SMEM), hbm, vmem, vmem],
+        out_specs=[vmem, vmem],
+        scratch_shapes=[
+            pltpu.VMEM((few, 2, 2 * FINE, 2 * FINE), jnp.bfloat16),
+            pltpu.VMEM((2 * GROUP * 8, LANES), jnp.float32),
+            pltpu.SemaphoreType.DMA(()),
+        ],
+        out_shape=[block, block],
+        compiler_params=pltpu.CompilerParams(vmem_limit_bytes=24 * 1024 * 1024),
+        cost_estimate=pl.CostEstimate(
+            flops=6 * 10**8, bytes_accessed=3 * 1024 * 1024, transcendentals=0
+        ),
+        name="channelize_late",
+    )(place, turn, high, low)
 
 
 def correlate_kernel(scale, first, count, picks, place, *refs):
@@ -220,9 +256,11 @@
             left, right, (((1,), (1,)), ((), ())), preferred_element_type=jnp.float32
         )
 
-    def give(i):
-        slot = i % 2
-        return pltpu.make_async_copy(held.at[slot], out.at[:, first + i], sent.at[slot])
+    def give(i, part):
+        slot = i % SLOTS
+        return pltpu.make_async_copy(
+            held.at[slot, part], out.at[part, first + i], sent.at[slot, part]
+        )
 
     for i in range(count):
         sets = []
@@ -244,17 +282,17 @@
         rows = jnp.where(time == 0, columns[0], columns[1])
         turned = jnp.concatenate([rows[:, 256:], -rows[:, :256]], axis=1)
 
-        if i >= 2:
-            give(i - 2).wait()
-        slot = i % 2
-        for group in range(2):
-            at = slice(group * 256, group * 256 + 256)
-            held[slot, 0, :, at] = dot(rows, columns[group]) * scale
-            held[slot, 1, :, at] = dot(turned, columns[group]) * scale
-        give(i).start()
-
-    for i in range(max(count - 2, 0), count):
-        give(i).wait()
+        slot = i % SLOTS
+        for part, left in enumerate((rows, turned)):
+            if i >= SLOTS:
+                give(i - SLOTS, part).wait()
+            for group in range(2):
+                at = slice(group * 256, group * 256 + 256)
+                held[slot, part, :, at] = dot(left, columns[group]) * scale
+            give(i, part).start()
+    for i in range(max(count - SLOTS, 0), count):
+        for part in range(2):
+            give(i, part).wait()
 
 
 def correlate(place, scale, first, count, kinds, earlier):
@@ -277,8 +315,8 @@
         in_specs=in_specs,
         out_specs=hbm,
         scratch_shapes=[
-            pltpu.VMEM((2, 2, 256, 512), jnp.float32),
-            pltpu.SemaphoreType.DMA((2,)),
+            pltpu.VMEM((SLOTS, 2, 256, 512), jnp.float32),
+            pltpu.SemaphoreType.DMA((SLOTS, 2)),
         ],
         out_shape=jax.ShapeDtypeStruct((2, 8, 256, 512), jnp.float32),
         input_output_aliases=aliases,
@@ -305,7 +343,9 @@
     tail = lax.ppermute(volts[:, (SPEC - HIST) * ROWS :], "tm", [(0, 1)])
     place = jnp.stack([lax.axis_index("y_lo"), lax.axis_index("tm")]).astype(jnp.int32)
     scale = np.float32(1.0 / (SPEC * lax.axis_size("tm")))
-    stay, leave, rest = channelize(place, volts, tail)
+    turn = jnp.asarray(turn_table())
+    rest, high, low = channelize(place, volts, tail, turn)
+    stay, leave = channelize_late(place, turn, high, low)
     over = lax.all_to_all(rest, PLANE, split_axis=0, concat_axis=0, tiled=True)
     early = jnp.stack([stay, *exchange(leave, stay)], axis=1)
     far, near, cross = exchange(over[:, 1], over[:, 0])

time: 115 us -> 114 us (level)
  waiting for transfers between devices: 60.5 us -> 57.4 us
  local copies, waits for them, and re-layouts: 1.03 us -> 3.22 us
    all_to_all x1, waiting for transfers between devices: 11.1 us -> 7.23 us  [local(): over = lax.all_to_all(rest, PLANE, split_axis=0, concat_axis=0, tiled=True)]
    unnamed x2 -> x4, local copies, waits for them, and re-layouts: 0.01 us -> 2.19 us
    pallas_call x0 -> x1, Pallas kernels: none -> 1.67 us  [channelize_late(): pl.pallas_call(late_kernel, in_specs=[pl.BlockSpec(memory_space=pltpu.SME...]
  transfers between devices with their start and end apart: 9 -> 9, of which waited for: 7 -> 7; matrix products, arithmetic and copies ran while one was open for 1% -> 1% of each run, Pallas kernels for 4% -> 5%
where the time goes in v2:
time: 114 us
  waiting for transfers between devices  57.4 us (50%)
  starting transfers between devices  33 us (29%)
  Pallas kernels  18.1 us (16%)
  local copies, waits for them, and re-layouts  3.22 us (3%)
  other arithmetic  1.53 us (1%)
    ppermute x2, waiting for transfers between devices, exchange(): cross = lax.ppermute(near_part, ('y_lo', 'tm'), both)  23.3 us
    ppermute x2, waiting for transfers between devices, exchange(): far = lax.ppermute(far_part, 'tm', flip)  23.1 us
    all_to_all x1, starting transfers between devices, local(): over = lax.all_to_all(rest, PLANE, split_axis=0, concat_axis=0, tiled=True)  13 us
    pallas_call x1, Pallas kernels, channelize(): pl.pallas_call(channel_kernel, in_specs=[pl.BlockSpec(memory_space=pltpu....  8.78 us
    pallas_call x2, Pallas kernels, correlate(): pl.pallas_call(kernel, in_specs=in_specs, out_specs=hbm, scratch_shapes=[...  7.65 us
    ppermute x2, starting transfers between devices, exchange(): far = lax.ppermute(far_part, 'tm', flip)  7.42 us
    all_to_all x1, waiting for transfers between devices, local(): over = lax.all_to_all(rest, PLANE, split_axis=0, concat_axis=0, tiled=True)  7.23 us
    all_to_all x1, starting transfers between devices, local(): lax.all_to_all(early, PLANE, split_axis=0, concat_axis=0, tiled=True)  6.16 us
  transfers between devices with their start and end apart: 9, of which 7 were waited for; matrix products, arithmetic and copies ran while one was open for 1% of the time, Pallas kernels for 5%

profile of v2, /device:TPU:1, one launch (start us, length us, event | category | flops | bytes accessed | tf_op | source)
XLA Modules:
  0.0 113.6 jit_solution(8407125901884378175)
XLA Ops:
  0.0 0.9 slice.12
  0.9 5.6 %collective-permute-start = (s32[2,96,128]{2,1,0:T(8,128)S(1)}, s32[2,96,128]{2,1,0:T(8,128)S(1)}, u32[]{:S(2)}, u32[]{:S(2)}) collective-permute-start(s32[2,96,128]{2,1,0:T(8,128)S(1)} %slice.12), channel_id=1, source_target_pairs={{0,1},{2,3},{4,5},{6,7},{8,9},{10,11},{12,13},{14,15},{16,17},{18,... | collective-permute-start | bytes 294920 | tf_op jit(solution)/shard_map/ppermute | solution.py:343
  6.6 0.1 fusion.13
  6.7 0.1 pad_add_fusion.place.refs_0_
  6.7 1.4 %collective-permute-done.tail = s32[2,96,128]{2,1,0:T(8,128)S(1)} collective-permute-done((s32[2,96,128]{2,1,0:T(8,128)S(1)}, s32[2,96,128]{2,1,0:T(8,128)S(1)}, u32[]{:S(2)}, u32[]{:S(2)}) %collective-permute-start) | collective-permute-done | bytes 98336 | tf_op jit(solution)/shard_map/ppermute | solution.py:343
  8.2 8.8 %channelize.1 = (bf16[64,2,5,8,128]{4,3,2,1,0:T(8,128)(2,1)}, bf16[3,512,256]{2,1,0:T(8,128)(2,1)S(1)}, bf16[3,512,256]{2,1,0:T(8,128)(2,1)S(1)}) custom-call(s32[2]{0:T(128)S(1)} %pad_add_fusion.place.refs_0_, s32[2,4096,128]{2,1,0:T(8,128)} %bitcast.23, s32[2,96,128]{2,1,0:T(8,128)S(1)} %collective-permute-done.tail, f32[4,32,128]{2,1,0:T(8,128)S(1)} %bitcast.21, ...), custom_call_target="tpu_custom_call" | custom-call | flops 2000000000 | bytes 8388608 | tf_op jit(solution)/shard_map/channelize/pallas_call | solution.py:203
  17.0 13.0 %all-to-all-start.1 = ((bf16[64,2,5,8,128]{4,3,2,1,0:T(8,128)(2,1)}), bf16[64,2,5,8,128]{4,3,2,1,0:T(8,128)(2,1)S(1)}, u32[]{:S(2)}, u32[]{:S(2)}) async-start(bf16[64,2,5,8,128]{4,3,2,1,0:T(8,128)(2,1)} %get-tuple-element.14), calls=%async_computation.1 | async-start | bytes 2621440 | tf_op jit(solution)/shard_map/all_to_all | solution.py:349
  30.0 2.2 %copy-done = bf16[8,4,256,256]{3,2,1,0:T(8,128)(2,1)S(1)} copy-done((bf16[8,4,256,256]{3,2,1,0:T(8,128)(2,1)S(1)}, bf16[8,4,256,256]{3,2,1,0:T(8,128)(2,1)}, u32[]{:S(2)}) %copy-start) | copy-done | bytes 4194328
  32.2 1.7 %channelize_late.1 = (bf16[64,3,8,128]{3,2,1,0:T(8,128)(2,1)S(1)}, bf16[64,3,8,128]{3,2,1,0:T(8,128)(2,1)S(1)}) custom-call(s32[2]{0:T(128)S(1)} %pad_add_fusion.place.refs_0_, bf16[8,4,256,256]{3,2,1,0:T(8,128)(2,1)S(1)} %copy-done, bf16[3,512,256]{2,1,0:T(8,128)(2,1)S(1)} %get-tuple-element.10.high, bf16[3,512,256]{2,1,0:T(8,128)(2,1)S(1)} %get-tuple-element.11.low), custom_call_target="tpu_custom_call" | custom-call | flops 600000000 | bytes 3145728 | tf_op jit(solution)/shard_map/channelize_late/pallas_call | solution.py:230
  33.9 3.7 %collective-permute-start.1 = (bf16[64,3,8,128]{3,2,1,0:T(8,128)(2,1)S(1)}, bf16[64,3,8,128]{3,2,1,0:T(8,128)(2,1)S(1)}, u32[]{:S(2)}, u32[]{:S(2)}) collective-permute-start(bf16[64,3,8,128]{3,2,1,0:T(8,128)(2,1)S(1)} %get-tuple-element.12), channel_id=1, source_target_pairs={{0,1},{1,0},{2,3},{3,2},{4,5},{5,4},{6,7},{7,6},{8,9},{9,8},{10,11... | collective-permute-start | bytes 1179656 | tf_op jit(solution)/shard_map/ppermute | solution.py:336
  37.6 0.4 collective-permute-start.2
  38.0 8.7 %collective-permute-done.1 = bf16[64,3,8,128]{3,2,1,0:T(8,128)(2,1)S(1)} collective-permute-done((bf16[64,3,8,128]{3,2,1,0:T(8,128)(2,1)S(1)}, bf16[64,3,8,128]{3,2,1,0:T(8,128)(2,1)S(1)}, u32[]{:S(2)}, u32[]{:S(2)}) %collective-permute-start.1) | collective-permute-done | bytes 393248 | tf_op jit(solution)/shard_map/ppermute | solution.py:336
  46.7 8.9 %collective-permute-done.3 = bf16[64,3,8,128]{3,2,1,0:T(8,128)(2,1)S(1)} collective-permute-done((bf16[64,3,8,128]{3,2,1,0:T(8,128)(2,1)S(1)}, bf16[64,3,8,128]{3,2,1,0:T(8,128)(2,1)S(1)}, u32[]{:S(2)}, u32[]{:S(2)}) %collective-permute-start.3) | collective-permute-done | bytes 393248 | tf_op jit(solution)/shard_map/ppermute | solution.py:335
  55.6 1.4 %pad_maximum_fusion = bf16[64,4,3,8,128]{4,3,2,1,0:T(8,128)(2,1)} fusion(bf16[64,1,3,8,128]{4,3,2,1,0:T(8,128)(2,1)S(1)} %bitcast.25, bf16[64,1,3,8,128]{4,3,2,1,0:T(8,128)(2,1)S(1)} %bitcast.26, bf16[64,1,3,8,128]{4,3,2,1,0:T(8,128)(2,1)S(1)} %bitcast.24, bf16[64,1,3,8,128]{4,3,2,1,0:T(8,128)(2,1)S(1)} %bitcast.20), kind=kLoop, calls=%fused_computation | loop fusion | flops 2359296 | bytes 3145728 | tf_op jit(solution)/shard_map/stack | solution.py:350
  56.9 7.2 %all-to-all-done.1.refs_1_ = bf16[64,2,5,8,128]{4,3,2,1,0:T(8,128)(2,1)S(1)} async-done(((bf16[64,2,5,8,128]{4,3,2,1,0:T(8,128)(2,1)}), bf16[64,2,5,8,128]{4,3,2,1,0:T(8,128)(2,1)S(1)}, u32[]{:S(2)}, u32[]{:S(2)}) %all-to-all-start.1) | async-done | bytes 1310752 | tf_op jit(solution)/shard_map/all_to_all | solution.py:349
  64.2 6.2 %all-to-all-start = ((bf16[64,4,3,8,128]{4,3,2,1,0:T(8,128)(2,1)}), bf16[64,4,3,8,128]{4,3,2,1,0:T(8,128)(2,1)S(1)}, u32[]{:S(2)}, u32[]{:S(2)}) async-start(bf16[64,4,3,8,128]{4,3,2,1,0:T(8,128)(2,1)} %pad_maximum_fusion), calls=%async_computation | async-start | bytes 3145728 | tf_op jit(solution)/shard_map/all_to_all | solution.py:352
  70.4 0.1 slice_bitcast_fusion
  70.5 3.7 %collective-permute-start.4 = (bf16[64,5,8,128]{3,2,1,0:T(8,128)(2,1)S(1)}, bf16[64,5,8,128]{3,2,1,0:T(8,128)(2,1)S(1)}, u32[]{:S(2)}, u32[]{:S(2)}) collective-permute-start(bf16[64,5,8,128]{3,2,1,0:T(8,128)(2,1)S(1)} %get-tuple-element.16), channel_id=1, source_target_pairs={{0,1},{1,0},{2,3},{3,2},{4,5},{5,4},{6,7},{7,6},{8,9},{9,8},{10,11... | collective-permute-start | bytes 1966088 | tf_op jit(solution)/shard_map/ppermute | solution.py:336
  74.2 0.4 collective-permute-start.5
  74.6 14.4 %collective-permute-done.4.refs_2_ = bf16[64,5,8,128]{3,2,1,0:T(8,128)(2,1)S(1)} collective-permute-done((bf16[64,5,8,128]{3,2,1,0:T(8,128)(2,1)S(1)}, bf16[64,5,8,128]{3,2,1,0:T(8,128)(2,1)S(1)}, u32[]{:S(2)}, u32[]{:S(2)}) %collective-permute-start.4) | collective-permute-done | bytes 655392 | tf_op jit(solution)/shard_map/ppermute | solution.py:336
  88.9 14.5 %collective-permute-done.6.refs_4_ = bf16[64,5,8,128]{3,2,1,0:T(8,128)(2,1)S(1)} collective-permute-done((bf16[64,5,8,128]{3,2,1,0:T(8,128)(2,1)S(1)}, bf16[64,5,8,128]{3,2,1,0:T(8,128)(2,1)S(1)}, u32[]{:S(2)}, u32[]{:S(2)}) %collective-permute-start.6) | collective-permute-done | bytes 655392 | tf_op jit(solution)/shard_map/ppermute | solution.py:335
  103.4 4.4 %correlate.2.refs_6_ = f32[2,8,256,512]{3,2,1,0:T(8,128)} custom-call(s32[2]{0:T(128)S(1)} %pad_add_fusion.place.refs_0_, bf16[64,2,5,8,128]{4,3,2,1,0:T(8,128)(2,1)S(1)} %all-to-all-done.1.refs_1_, bf16[64,5,8,128]{3,2,1,0:T(8,128)(2,1)S(1)} %collective-permute-done.4.refs_2_, bf16[64,5,8,128]{3,2,1,0:T(8,128)(2,1)S(1)} %collective-permute-done.5.refs_3_, ...), custom_call_target="tpu_custom_call" | custom-call | flops 2000000000 | bytes 7864320 | tf_op jit(solution)/shard_map/correlate/pallas_call | solution.py:313
  107.8 2.3 %all-to-all-done.refs_1_.refs_2_.refs_3_.refs_4_ = bf16[64,4,3,8,128]{4,3,2,1,0:T(8,128)(2,1)S(1)} async-done(((bf16[64,4,3,8,128]{4,3,2,1,0:T(8,128)(2,1)}), bf16[64,4,3,8,128]{4,3,2,1,0:T(8,128)(2,1)S(1)}, u32[]{:S(2)}, u32[]{:S(2)}) %all-to-all-start) | async-done | bytes 1572896 | tf_op jit(solution)/shard_map/all_to_all | solution.py:352
  110.1 3.3 %correlate.3 = f32[2,8,256,512]{3,2,1,0:T(8,128)} custom-call(s32[2]{0:T(128)S(1)} %pad_add_fusion.place.refs_0_, bf16[64,4,3,8,128]{4,3,2,1,0:T(8,128)(2,1)S(1)} %all-to-all-done.refs_1_.refs_2_.refs_3_.refs_4_, bf16[64,4,3,8,128]{4,3,2,1,0:T(8,128)(2,1)S(1)} %all-to-all-done.refs_1_.refs_2_.refs_3_.refs_4_, ...), custom_call_target="tpu_custom_call", output_to_operand_aliasing={{}: (6, {})} | custom-call | flops 1200000000 | bytes 4718592 | tf_op jit(solution)/shard_map/correlate/pallas_call | solution.py:313
  (8 shorter events, 0.0 us)
Async XLA Ops:
  0.9 7.3 %collective-permute-start = (s32[2,96,128]{2,1,0:T(8,128)S(1)}, s32[2,96,128]{2,1,0:T(8,128)S(1)}, u32[]{:S(2)}, u32[]{:S(2)}) collective-permute-start(s32[2,96,128]{2,1,0:T(8,128)S(1)} %slice.12), channel_id=1, source_target_pairs={{0,1},{2,3},{4,5},{6,7},{8,9},{10,11},{12,13},{14,15},{16,17},{18,... | collective-permute-start | bytes 294920 | tf_op jit(solution)/shard_map/ppermute | solution.py:343
  17.0 47.2 %all-to-all-start.1 = ((bf16[64,2,5,8,128]{4,3,2,1,0:T(8,128)(2,1)}), bf16[64,2,5,8,128]{4,3,2,1,0:T(8,128)(2,1)S(1)}, u32[]{:S(2)}, u32[]{:S(2)}) async-start(bf16[64,2,5,8,128]{4,3,2,1,0:T(8,128)(2,1)} %get-tuple-element.14), calls=%async_computation.1 | async-start | bytes 2621440 | tf_op jit(solution)/shard_map/all_to_all | solution.py:349
  30.0 2.2 %copy-start = (bf16[8,4,256,256]{3,2,1,0:T(8,128)(2,1)S(1)}, bf16[8,4,256,256]{3,2,1,0:T(8,128)(2,1)}, u32[]{:S(2)}) copy-start(bf16[8,4,256,256]{3,2,1,0:T(8,128)(2,1)} %constant.82.clone.turn) | copy-start | bytes 12582916
  33.9 12.8 %collective-permute-start.1 = (bf16[64,3,8,128]{3,2,1,0:T(8,128)(2,1)S(1)}, bf16[64,3,8,128]{3,2,1,0:T(8,128)(2,1)S(1)}, u32[]{:S(2)}, u32[]{:S(2)}) collective-permute-start(bf16[64,3,8,128]{3,2,1,0:T(8,128)(2,1)S(1)} %get-tuple-element.12), channel_id=1, source_target_pairs={{0,1},{1,0},{2,3},{3,2},{4,5},{5,4},{6,7},{7,6},{8,9},{9,8},{10,11... | collective-permute-start | bytes 1179656 | tf_op jit(solution)/shard_map/ppermute | solution.py:336
  37.6 18.0 %collective-permute-start.3 = (bf16[64,3,8,128]{3,2,1,0:T(8,128)(2,1)S(1)}, bf16[64,3,8,128]{3,2,1,0:T(8,128)(2,1)S(1)}, u32[]{:S(2)}, u32[]{:S(2)}) collective-permute-start(bf16[64,3,8,128]{3,2,1,0:T(8,128)(2,1)S(1)} %get-tuple-element.13), channel_id=1, source_target_pairs={{0,129},{129,0},{1,128},{128,1},{2,131},{131,2},{3,130},{130,3},{4... | collective-permute-start | bytes 1179656 | tf_op jit(solution)/shard_map/ppermute | solution.py:335
  37.6 18.0 %collective-permute-start.2 = (bf16[64,3,8,128]{3,2,1,0:T(8,128)(2,1)S(1)}, bf16[64,3,8,128]{3,2,1,0:T(8,128)(2,1)S(1)}, u32[]{:S(2)}, u32[]{:S(2)}) collective-permute-start(bf16[64,3,8,128]{3,2,1,0:T(8,128)(2,1)S(1)} %get-tuple-element.13), channel_id=1, source_target_pairs={{0,128},{128,0},{1,129},{129,1},{2,130},{130,2},{3,131},{131,3},{4... | collective-permute-start | bytes 1179656 | tf_op jit(solution)/shard_map/ppermute | solution.py:334
  64.2 46.0 %all-to-all-start = ((bf16[64,4,3,8,128]{4,3,2,1,0:T(8,128)(2,1)}), bf16[64,4,3,8,128]{4,3,2,1,0:T(8,128)(2,1)S(1)}, u32[]{:S(2)}, u32[]{:S(2)}) async-start(bf16[64,4,3,8,128]{4,3,2,1,0:T(8,128)(2,1)} %pad_maximum_fusion), calls=%async_computation | async-start | bytes 3145728 | tf_op jit(solution)/shard_map/all_to_all | solution.py:352
  70.3 33.1 %copy-start.1 = (bf16[256,256]{1,0:T(8,128)(2,1)S(1)}, bf16[256,256]{1,0:T(8,128)(2,1)}, u32[]{:S(2)}) copy-start(bf16[256,256]{1,0:T(8,128)(2,1)} %constant.83.clone.refs_5_) | copy-start | bytes 393220
  70.5 18.5 %collective-permute-start.4 = (bf16[64,5,8,128]{3,2,1,0:T(8,128)(2,1)S(1)}, bf16[64,5,8,128]{3,2,1,0:T(8,128)(2,1)S(1)}, u32[]{:S(2)}, u32[]{:S(2)}) collective-permute-start(bf16[64,5,8,128]{3,2,1,0:T(8,128)(2,1)S(1)} %get-tuple-element.16), channel_id=1, source_target_pairs={{0,1},{1,0},{2,3},{3,2},{4,5},{5,4},{6,7},{7,6},{8,9},{9,8},{10,11... | collective-permute-start | bytes 1966088 | tf_op jit(solution)/shard_map/ppermute | solution.py:336
  74.2 29.2 %collective-permute-start.6 = (bf16[64,5,8,128]{3,2,1,0:T(8,128)(2,1)S(1)}, bf16[64,5,8,128]{3,2,1,0:T(8,128)(2,1)S(1)}, u32[]{:S(2)}, u32[]{:S(2)}) collective-permute-start(bf16[64,5,8,128]{3,2,1,0:T(8,128)(2,1)S(1)} %get-tuple-element.15), channel_id=1, source_target_pairs={{0,129},{129,0},{1,128},{128,1},{2,131},{131,2},{3,130},{130,3},{4... | collective-permute-start | bytes 1966088 | tf_op jit(solution)/shard_map/ppermute | solution.py:335
  74.2 29.2 %collective-permute-start.5 = (bf16[64,5,8,128]{3,2,1,0:T(8,128)(2,1)S(1)}, bf16[64,5,8,128]{3,2,1,0:T(8,128)(2,1)S(1)}, u32[]{:S(2)}, u32[]{:S(2)}) collective-permute-start(bf16[64,5,8,128]{3,2,1,0:T(8,128)(2,1)S(1)} %get-tuple-element.15), channel_id=1, source_target_pairs={{0,128},{128,0},{1,129},{129,1},{2,130},{130,2},{3,131},{131,3},{4... | collective-permute-start | bytes 1966088 | tf_op jit(solution)/shard_map/ppermute | solution.py:334

commit v3 on v2

--- a/solution.py
+++ b/solution.py
@@ -20,6 +20,7 @@
 VMEM_KIB = 50 * 1024
 HIST = TAPS - 1
 ROWS = RADIX * NA
+PITCH = ROWS + 8
 GROUP = 64
 PLANE = ("x", "z", "core")
 PLANE_FIRST = (0, 1, 2, 3, 4)
@@ -133,7 +134,8 @@
     for c in range(SPEC // STEP):
         chunk_copy(c).start()
     table_copy.start()
-    raw[:, : HIST * ROWS, :] = tail[...]
+    before = tail[...].astype(jnp.float32).astype(jnp.int32)
+    raw[:, : HIST * ROWS, :] = jnp.where(place[1] > 0, before, 0)
 
     @pl.loop(0, SPEC // STEP)
     def _(c):
@@ -143,6 +145,7 @@
             @pl.loop(0, STEP // BATCH)
             def _(i):
                 into = pl.multiple_of(i * BATCH * ROWS, BATCH * ROWS)
+                there = pl.multiple_of(i * BATCH * PITCH, BATCH * PITCH)
                 base = pl.multiple_of(c * STEP * ROWS + into, BATCH * ROWS)
                 for piece in range(ROWS // 8):
                     weights = [taps[t, piece * 8 : piece * 8 + 8, :] for t in range(TAPS)]
@@ -154,13 +157,13 @@
                         total = weights[0] * frames[s]
                         for t in range(1, TAPS):
                             total = total + weights[t] * frames[s + t]
-                        filt[p, pl.ds(into + (s * ROWS + piece * 8), 8), :] = total
+                        filt[p, pl.ds(there + (s * PITCH + piece * 8), 8), :] = total
 
         for a in range(NA):
             for part in range(STEP // 16):
                 x = [
                     tuple(
-                        filt[p, pl.ds(part * 16 * ROWS + m * NA + a, 16, stride=ROWS), :]
+                        filt[p, pl.ds(part * 16 * PITCH + m * NA + a, 16, stride=PITCH), :]
                         for p in range(2)
                     )
                     for m in range(RADIX)
@@ -206,7 +209,7 @@
         out_specs=[vmem, vmem, vmem],
         scratch_shapes=[
             pltpu.VMEM((2, (HIST + SPEC) * ROWS, LANES), jnp.int32),
-            pltpu.VMEM((2, STEP * ROWS, LANES), jnp.float32),
+            pltpu.VMEM((2, STEP * PITCH, LANES), jnp.float32),
             pltpu.VMEM((many, NA * SPEC, 2 * LANES), jnp.bfloat16),
             pltpu.VMEM((many, NA * SPEC, 2 * LANES), jnp.bfloat16),
             pltpu.VMEM((many, 2, 2 * FINE, 2 * FINE), jnp.bfloat16),
@@ -340,7 +343,8 @@
 def local(voltages):
     tiles = voltages.shape[2] // LANES
     volts = voltages.reshape(2, NA, tiles, LANES).transpose(0, 2, 1, 3).reshape(2, tiles * NA, LANES)
-    tail = lax.ppermute(volts[:, (SPEC - HIST) * ROWS :], "tm", [(0, 1)])
+    tail = volts[:, (SPEC - HIST) * ROWS :].astype(jnp.bfloat16)
+    tail = lax.ppermute(tail, "tm", [(0, 1), (1, 0)])
     place = jnp.stack([lax.axis_index("y_lo"), lax.axis_index("tm")]).astype(jnp.int32)
     scale = np.float32(1.0 / (SPEC * lax.axis_size("tm")))
     turn = jnp.asarray(turn_table())

time: 114 us -> 111 us (0.974)
  starting transfers between devices: 33 us -> 30.9 us
  Pallas kernels: 18.1 us -> 16.6 us
    ppermute x1, starting transfers between devices: 5.64 us -> 3.83 us  [local(): tail = lax.ppermute(tail, 'tm', [(0, 1), (1, 0)])]
    ppermute x2, starting transfers between devices: 0.01 us -> 1.55 us  [exchange(): cross = lax.ppermute(near_part, ('y_lo', 'tm'), both)]
    pallas_call x1, Pallas kernels: 8.78 us -> 7.26 us  [channelize(): pl.pallas_call(channel_kernel, in_specs=[pl.BlockSpec(memory_space=pltpu....]
    ppermute x2, starting transfers between devices: 7.42 us -> 6.01 us  [exchange(): far = lax.ppermute(far_part, 'tm', flip)]
    ppermute x2, waiting for transfers between devices: 23.1 us -> 21.8 us  [exchange(): far = lax.ppermute(far_part, 'tm', flip)]
where the time goes in v3:
time: 111 us; the launch traced here: 110 us
  waiting for transfers between devices  58 us (52%)
  starting transfers between devices  30.9 us (28%)
  Pallas kernels  16.6 us (15%)
  other arithmetic  2.43 us (2%)
  local copies, waits for them, and re-layouts  2.32 us (2%)
    ppermute x2, waiting for transfers between devices, exchange(): cross = lax.ppermute(near_part, ('y_lo', 'tm'), both)  24 us
    ppermute x2, waiting for transfers between devices, exchange(): far = lax.ppermute(far_part, 'tm', flip)  21.8 us
    all_to_all x1, starting transfers between devices, local(): over = lax.all_to_all(rest, PLANE, split_axis=0, concat_axis=0, tiled=True)  13.4 us
    all_to_all x1, waiting for transfers between devices, local(): over = lax.all_to_all(rest, PLANE, split_axis=0, concat_axis=0, tiled=True)  7.89 us
    pallas_call x2, Pallas kernels, correlate(): pl.pallas_call(kernel, in_specs=in_specs, out_specs=hbm, scratch_shapes=[...  7.64 us
    pallas_call x1, Pallas kernels, channelize(): pl.pallas_call(channel_kernel, in_specs=[pl.BlockSpec(memory_space=pltpu....  7.26 us
    all_to_all x1, starting transfers between devices, local(): lax.all_to_all(early, PLANE, split_axis=0, concat_axis=0, tiled=True)  6.16 us
    ppermute x2, starting transfers between devices, exchange(): far = lax.ppermute(far_part, 'tm', flip)  6.01 us
  transfers between devices with their start and end apart: 9, of which 7 were waited for; matrix products, arithmetic and copies ran while one was open for 1% of the time, Pallas kernels for 5%

profile of v3, /device:TPU:1, one launch (start us, length us, event | category | flops | bytes accessed | tf_op | source)
XLA Modules:
  0.0 110.5 jit_solution(6323587567793938663)
XLA Ops:
  0.0 0.9 slice_convert_fusion
  0.9 3.8 %collective-permute-start = (bf16[2,96,128]{2,1,0:T(8,128)(2,1)S(1)}, bf16[2,96,128]{2,1,0:T(8,128)(2,1)S(1)}, u32[]{:S(2)}, u32[]{:S(2)}) collective-permute-start(bf16[2,96,128]{2,1,0:T(8,128)(2,1)S(1)} %slice_convert_fusion), channel_id=1, source_target_pairs={{0,1},{1,0},{2,3},{3,2},{4,5},{5,4},{6,7},{7,6},{8,9},{9,8},{10,11... | collective-permute-start | bytes 147464 | tf_op jit(solution)/shard_map/ppermute | solution.py:347
  4.7 0.1 fusion.13
  4.8 0.1 pad_add_fusion.place.refs_0_
  4.9 1.3 %collective-permute-done.tail = bf16[2,96,128]{2,1,0:T(8,128)(2,1)S(1)} collective-permute-done((bf16[2,96,128]{2,1,0:T(8,128)(2,1)S(1)}, bf16[2,96,128]{2,1,0:T(8,128)(2,1)S(1)}, u32[]{:S(2)}, u32[]{:S(2)}) %collective-permute-start) | collective-permute-done | bytes 49184 | tf_op jit(solution)/shard_map/ppermute | solution.py:347
  6.2 7.3 %channelize.1 = (bf16[64,2,5,8,128]{4,3,2,1,0:T(8,128)(2,1)}, bf16[3,512,256]{2,1,0:T(8,128)(2,1)S(1)}, bf16[3,512,256]{2,1,0:T(8,128)(2,1)S(1)}) custom-call(s32[2]{0:T(128)S(1)} %pad_add_fusion.place.refs_0_, s32[2,4096,128]{2,1,0:T(8,128)} %bitcast.23, bf16[2,96,128]{2,1,0:T(8,128)(2,1)S(1)} %collective-permute-done.tail, f32[4,32,128]{2,1,0:T(8,128)S(1)} %bitcast.21, ...), custom_call_target="tpu_custom_call" | custom-call | flops 2000000000 | bytes 8388608 | tf_op jit(solution)/shard_map/channelize/pallas_call | solution.py:206
  13.5 13.4 %all-to-all-start.1 = ((bf16[64,2,5,8,128]{4,3,2,1,0:T(8,128)(2,1)}), bf16[64,2,5,8,128]{4,3,2,1,0:T(8,128)(2,1)S(1)}, u32[]{:S(2)}, u32[]{:S(2)}) async-start(bf16[64,2,5,8,128]{4,3,2,1,0:T(8,128)(2,1)} %get-tuple-element.14), calls=%async_computation.1 | async-start | bytes 2621440 | tf_op jit(solution)/shard_map/all_to_all | solution.py:353
  26.9 2.2 %copy-done = bf16[8,4,256,256]{3,2,1,0:T(8,128)(2,1)S(1)} copy-done((bf16[8,4,256,256]{3,2,1,0:T(8,128)(2,1)S(1)}, bf16[8,4,256,256]{3,2,1,0:T(8,128)(2,1)}, u32[]{:S(2)}) %copy-start) | copy-done | bytes 4194328
  29.1 1.7 %channelize_late.1 = (bf16[64,3,8,128]{3,2,1,0:T(8,128)(2,1)S(1)}, bf16[64,3,8,128]{3,2,1,0:T(8,128)(2,1)S(1)}) custom-call(s32[2]{0:T(128)S(1)} %pad_add_fusion.place.refs_0_, bf16[8,4,256,256]{3,2,1,0:T(8,128)(2,1)S(1)} %copy-done, bf16[3,512,256]{2,1,0:T(8,128)(2,1)S(1)} %get-tuple-element.10.high, bf16[3,512,256]{2,1,0:T(8,128)(2,1)S(1)} %get-tuple-element.11.low), custom_call_target="tpu_custom_call" | custom-call | flops 600000000 | bytes 3145728 | tf_op jit(solution)/shard_map/channelize_late/pallas_call | solution.py:233
  30.8 3.0 %collective-permute-start.1 = (bf16[64,3,8,128]{3,2,1,0:T(8,128)(2,1)S(1)}, bf16[64,3,8,128]{3,2,1,0:T(8,128)(2,1)S(1)}, u32[]{:S(2)}, u32[]{:S(2)}) collective-permute-start(bf16[64,3,8,128]{3,2,1,0:T(8,128)(2,1)S(1)} %get-tuple-element.12), channel_id=1, source_target_pairs={{0,1},{1,0},{2,3},{3,2},{4,5},{5,4},{6,7},{7,6},{8,9},{9,8},{10,11... | collective-permute-start | bytes 1179656 | tf_op jit(solution)/shard_map/ppermute | solution.py:339
  33.8 0.8 collective-permute-start.3
  34.5 8.1 %collective-permute-done.1 = bf16[64,3,8,128]{3,2,1,0:T(8,128)(2,1)S(1)} collective-permute-done((bf16[64,3,8,128]{3,2,1,0:T(8,128)(2,1)S(1)}, bf16[64,3,8,128]{3,2,1,0:T(8,128)(2,1)S(1)}, u32[]{:S(2)}, u32[]{:S(2)}) %collective-permute-start.1) | collective-permute-done | bytes 393248 | tf_op jit(solution)/shard_map/ppermute | solution.py:339
  42.6 9.2 %collective-permute-done.3 = bf16[64,3,8,128]{3,2,1,0:T(8,128)(2,1)S(1)} collective-permute-done((bf16[64,3,8,128]{3,2,1,0:T(8,128)(2,1)S(1)}, bf16[64,3,8,128]{3,2,1,0:T(8,128)(2,1)S(1)}, u32[]{:S(2)}, u32[]{:S(2)}) %collective-permute-start.3) | collective-permute-done | bytes 393248 | tf_op jit(solution)/shard_map/ppermute | solution.py:338
  51.8 1.4 %pad_maximum_fusion = bf16[64,4,3,8,128]{4,3,2,1,0:T(8,128)(2,1)} fusion(bf16[64,1,3,8,128]{4,3,2,1,0:T(8,128)(2,1)S(1)} %bitcast.25, bf16[64,1,3,8,128]{4,3,2,1,0:T(8,128)(2,1)S(1)} %bitcast.26, bf16[64,1,3,8,128]{4,3,2,1,0:T(8,128)(2,1)S(1)} %bitcast.24, bf16[64,1,3,8,128]{4,3,2,1,0:T(8,128)(2,1)S(1)} %bitcast.20), kind=kLoop, calls=%fused_computation | loop fusion | flops 2359296 | bytes 3145728 | tf_op jit(solution)/shard_map/stack | solution.py:354
  53.2 7.9 %all-to-all-done.1.refs_1_ = bf16[64,2,5,8,128]{4,3,2,1,0:T(8,128)(2,1)S(1)} async-done(((bf16[64,2,5,8,128]{4,3,2,1,0:T(8,128)(2,1)}), bf16[64,2,5,8,128]{4,3,2,1,0:T(8,128)(2,1)S(1)}, u32[]{:S(2)}, u32[]{:S(2)}) %all-to-all-start.1) | async-done | bytes 1310752 | tf_op jit(solution)/shard_map/all_to_all | solution.py:353
  61.1 6.2 %all-to-all-start = ((bf16[64,4,3,8,128]{4,3,2,1,0:T(8,128)(2,1)}), bf16[64,4,3,8,128]{4,3,2,1,0:T(8,128)(2,1)S(1)}, u32[]{:S(2)}, u32[]{:S(2)}) async-start(bf16[64,4,3,8,128]{4,3,2,1,0:T(8,128)(2,1)} %pad_maximum_fusion), calls=%async_computation | async-start | bytes 3145728 | tf_op jit(solution)/shard_map/all_to_all | solution.py:356
  67.2 0.1 slice_bitcast_fusion
  67.4 3.0 %collective-permute-start.4 = (bf16[64,5,8,128]{3,2,1,0:T(8,128)(2,1)S(1)}, bf16[64,5,8,128]{3,2,1,0:T(8,128)(2,1)S(1)}, u32[]{:S(2)}, u32[]{:S(2)}) collective-permute-start(bf16[64,5,8,128]{3,2,1,0:T(8,128)(2,1)S(1)} %get-tuple-element.16), channel_id=1, source_target_pairs={{0,1},{1,0},{2,3},{3,2},{4,5},{5,4},{6,7},{7,6},{8,9},{9,8},{10,11... | collective-permute-start | bytes 1966088 | tf_op jit(solution)/shard_map/ppermute | solution.py:339
  70.4 0.8 collective-permute-start.6
  71.1 13.7 %collective-permute-done.4.refs_2_ = bf16[64,5,8,128]{3,2,1,0:T(8,128)(2,1)S(1)} collective-permute-done((bf16[64,5,8,128]{3,2,1,0:T(8,128)(2,1)S(1)}, bf16[64,5,8,128]{3,2,1,0:T(8,128)(2,1)S(1)}, u32[]{:S(2)}, u32[]{:S(2)}) %collective-permute-start.4) | collective-permute-done | bytes 655392 | tf_op jit(solution)/shard_map/ppermute | solution.py:339
  84.9 14.8 %collective-permute-done.6.refs_4_ = bf16[64,5,8,128]{3,2,1,0:T(8,128)(2,1)S(1)} collective-permute-done((bf16[64,5,8,128]{3,2,1,0:T(8,128)(2,1)S(1)}, bf16[64,5,8,128]{3,2,1,0:T(8,128)(2,1)S(1)}, u32[]{:S(2)}, u32[]{:S(2)}) %collective-permute-start.6) | collective-permute-done | bytes 655392 | tf_op jit(solution)/shard_map/ppermute | solution.py:338
  99.7 4.4 %correlate.2.refs_6_ = f32[2,8,256,512]{3,2,1,0:T(8,128)} custom-call(s32[2]{0:T(128)S(1)} %pad_add_fusion.place.refs_0_, bf16[64,2,5,8,128]{4,3,2,1,0:T(8,128)(2,1)S(1)} %all-to-all-done.1.refs_1_, bf16[64,5,8,128]{3,2,1,0:T(8,128)(2,1)S(1)} %collective-permute-done.4.refs_2_, bf16[64,5,8,128]{3,2,1,0:T(8,128)(2,1)S(1)} %collective-permute-done.5.refs_3_, ...), custom_call_target="tpu_custom_call" | custom-call | flops 2000000000 | bytes 7864320 | tf_op jit(solution)/shard_map/correlate/pallas_call | solution.py:316
  104.0 3.0 %all-to-all-done.refs_1_.refs_2_.refs_3_.refs_4_ = bf16[64,4,3,8,128]{4,3,2,1,0:T(8,128)(2,1)S(1)} async-done(((bf16[64,4,3,8,128]{4,3,2,1,0:T(8,128)(2,1)}), bf16[64,4,3,8,128]{4,3,2,1,0:T(8,128)(2,1)S(1)}, u32[]{:S(2)}, u32[]{:S(2)}) %all-to-all-start) | async-done | bytes 1572896 | tf_op jit(solution)/shard_map/all_to_all | solution.py:356
  107.0 3.3 %correlate.3 = f32[2,8,256,512]{3,2,1,0:T(8,128)} custom-call(s32[2]{0:T(128)S(1)} %pad_add_fusion.place.refs_0_, bf16[64,4,3,8,128]{4,3,2,1,0:T(8,128)(2,1)S(1)} %all-to-all-done.refs_1_.refs_2_.refs_3_.refs_4_, bf16[64,4,3,8,128]{4,3,2,1,0:T(8,128)(2,1)S(1)} %all-to-all-done.refs_1_.refs_2_.refs_3_.refs_4_, ...), custom_call_target="tpu_custom_call", output_to_operand_aliasing={{}: (6, {})} | custom-call | flops 1200000000 | bytes 4718592 | tf_op jit(solution)/shard_map/correlate/pallas_call | solution.py:316
  (8 shorter events, 0.0 us)
Async XLA Ops:
  0.9 5.3 %collective-permute-start = (bf16[2,96,128]{2,1,0:T(8,128)(2,1)S(1)}, bf16[2,96,128]{2,1,0:T(8,128)(2,1)S(1)}, u32[]{:S(2)}, u32[]{:S(2)}) collective-permute-start(bf16[2,96,128]{2,1,0:T(8,128)(2,1)S(1)} %slice_convert_fusion), channel_id=1, source_target_pairs={{0,1},{1,0},{2,3},{3,2},{4,5},{5,4},{6,7},{7,6},{8,9},{9,8},{10,11... | collective-permute-start | bytes 147464 | tf_op jit(solution)/shard_map/ppermute | solution.py:347
  13.5 47.6 %all-to-all-start.1 = ((bf16[64,2,5,8,128]{4,3,2,1,0:T(8,128)(2,1)}), bf16[64,2,5,8,128]{4,3,2,1,0:T(8,128)(2,1)S(1)}, u32[]{:S(2)}, u32[]{:S(2)}) async-start(bf16[64,2,5,8,128]{4,3,2,1,0:T(8,128)(2,1)} %get-tuple-element.14), calls=%async_computation.1 | async-start | bytes 2621440 | tf_op jit(solution)/shard_map/all_to_all | solution.py:353
  26.9 2.2 %copy-start = (bf16[8,4,256,256]{3,2,1,0:T(8,128)(2,1)S(1)}, bf16[8,4,256,256]{3,2,1,0:T(8,128)(2,1)}, u32[]{:S(2)}) copy-start(bf16[8,4,256,256]{3,2,1,0:T(8,128)(2,1)} %constant.82.clone.turn) | copy-start | bytes 12582916
  30.8 11.9 %collective-permute-start.1 = (bf16[64,3,8,128]{3,2,1,0:T(8,128)(2,1)S(1)}, bf16[64,3,8,128]{3,2,1,0:T(8,128)(2,1)S(1)}, u32[]{:S(2)}, u32[]{:S(2)}) collective-permute-start(bf16[64,3,8,128]{3,2,1,0:T(8,128)(2,1)S(1)} %get-tuple-element.12), channel_id=1, source_target_pairs={{0,1},{1,0},{2,3},{3,2},{4,5},{5,4},{6,7},{7,6},{8,9},{9,8},{10,11... | collective-permute-start | bytes 1179656 | tf_op jit(solution)/shard_map/ppermute | solution.py:339
  33.8 18.1 %collective-permute-start.3 = (bf16[64,3,8,128]{3,2,1,0:T(8,128)(2,1)S(1)}, bf16[64,3,8,128]{3,2,1,0:T(8,128)(2,1)S(1)}, u32[]{:S(2)}, u32[]{:S(2)}) collective-permute-start(bf16[64,3,8,128]{3,2,1,0:T(8,128)(2,1)S(1)} %get-tuple-element.13), channel_id=1, source_target_pairs={{0,129},{129,0},{1,128},{128,1},{2,131},{131,2},{3,130},{130,3},{4... | collective-permute-start | bytes 1179656 | tf_op jit(solution)/shard_map/ppermute | solution.py:338
  34.5 17.3 %collective-permute-start.2 = (bf16[64,3,8,128]{3,2,1,0:T(8,128)(2,1)S(1)}, bf16[64,3,8,128]{3,2,1,0:T(8,128)(2,1)S(1)}, u32[]{:S(2)}, u32[]{:S(2)}) collective-permute-start(bf16[64,3,8,128]{3,2,1,0:T(8,128)(2,1)S(1)} %get-tuple-element.13), channel_id=1, source_target_pairs={{0,128},{128,0},{1,129},{129,1},{2,130},{130,2},{3,131},{131,3},{4... | collective-permute-start | bytes 1179656 | tf_op jit(solution)/shard_map/ppermute | solution.py:337
  61.1 46.0 %all-to-all-start = ((bf16[64,4,3,8,128]{4,3,2,1,0:T(8,128)(2,1)}), bf16[64,4,3,8,128]{4,3,2,1,0:T(8,128)(2,1)S(1)}, u32[]{:S(2)}, u32[]{:S(2)}) async-start(bf16[64,4,3,8,128]{4,3,2,1,0:T(8,128)(2,1)} %pad_maximum_fusion), calls=%async_computation | async-start | bytes 3145728 | tf_op jit(solution)/shard_map/all_to_all | solution.py:356
  67.2 32.4 %copy-start.1 = (bf16[256,256]{1,0:T(8,128)(2,1)S(1)}, bf16[256,256]{1,0:T(8,128)(2,1)}, u32[]{:S(2)}) copy-start(bf16[256,256]{1,0:T(8,128)(2,1)} %constant.83.clone.refs_5_) | copy-start | bytes 393220
  67.4 17.5 %collective-permute-start.4 = (bf16[64,5,8,128]{3,2,1,0:T(8,128)(2,1)S(1)}, bf16[64,5,8,128]{3,2,1,0:T(8,128)(2,1)S(1)}, u32[]{:S(2)}, u32[]{:S(2)}) collective-permute-start(bf16[64,5,8,128]{3,2,1,0:T(8,128)(2,1)S(1)} %get-tuple-element.16), channel_id=1, source_target_pairs={{0,1},{1,0},{2,3},{3,2},{4,5},{5,4},{6,7},{7,6},{8,9},{9,8},{10,11... | collective-permute-start | bytes 1966088 | tf_op jit(solution)/shard_map/ppermute | solution.py:339
  70.4 29.3 %collective-permute-start.6 = (bf16[64,5,8,128]{3,2,1,0:T(8,128)(2,1)S(1)}, bf16[64,5,8,128]{3,2,1,0:T(8,128)(2,1)S(1)}, u32[]{:S(2)}, u32[]{:S(2)}) collective-permute-start(bf16[64,5,8,128]{3,2,1,0:T(8,128)(2,1)S(1)} %get-tuple-element.15), channel_id=1, source_target_pairs={{0,129},{129,0},{1,128},{128,1},{2,131},{131,2},{3,130},{130,3},{4... | collective-permute-start | bytes 1966088 | tf_op jit(solution)/shard_map/ppermute | solution.py:338
  71.1 28.5 %collective-permute-start.5 = (bf16[64,5,8,128]{3,2,1,0:T(8,128)(2,1)S(1)}, bf16[64,5,8,128]{3,2,1,0:T(8,128)(2,1)S(1)}, u32[]{:S(2)}, u32[]{:S(2)}) collective-permute-start(bf16[64,5,8,128]{3,2,1,0:T(8,128)(2,1)S(1)} %get-tuple-element.15), channel_id=1, source_target_pairs={{0,128},{128,0},{1,129},{129,1},{2,130},{130,2},{3,131},{131,3},{4... | collective-permute-start | bytes 1966088 | tf_op jit(solution)/shard_map/ppermute | solution.py:337

commit v4 on v3

--- a/solution.py
+++ b/solution.py
@@ -15,9 +15,11 @@
 NA = 4
 SPEC = 128
 STEP = 32
+BODY = SPEC - STEP
 BATCH = 8
 SLOTS = 5
 VMEM_KIB = 50 * 1024
+MORE_KIB = 50 * 1024
 HIST = TAPS - 1
 ROWS = RADIX * NA
 PITCH = ROWS + 8
@@ -85,7 +87,7 @@
     return [add(even[i], odd[i]) for i in range(4)] + [sub(even[i], odd[i]) for i in range(4)]
 
 
-def transform(mine, j, table, high, low, spread):
+def transform(mine, j, table, tops, lows, spread):
     def dot(left, right):
         return lax.dot_general(
             left, right, (((1,), (1,)), ((), ())), preferred_element_type=jnp.float32
@@ -100,8 +102,7 @@
                 start = pl.multiple_of(p * FINE + half * GROUP, GROUP)
                 pieces.append(table[j, kind, pl.ds(start, GROUP), :])
         rows.append(jnp.concatenate(pieces, axis=0))
-    tops = high[j]
-    spectra = dot(rows[0], tops) + (dot(rows[1], tops) + dot(rows[0], low[j]))
+    spectra = dot(rows[0], tops) + (dot(rows[1], tops) + dot(rows[0], lows))
     blocks = []
     for slot in range(2):
         for p in range(2):
@@ -117,122 +118,189 @@
     return blocks
 
 
-def channel_kernel(
-    place, volts, tail, taps, turn, rest, late_high, late_low, raw, filt, high, low, table, spread, arrived
-):
+def joined(head, body, j, k):
+    parts = []
+    for a in range(NA):
+        parts.append(head[k, a * STEP : (a + 1) * STEP, :])
+        parts.append(body[j, a * BODY : (a + 1) * BODY, :])
+    return jnp.concatenate(parts, axis=0)
+
+
+def mix(first, raw, taps, filt, store):
+    for p in range(2):
+
+        @pl.loop(0, STEP // BATCH)
+        def _(i):
+            base = pl.multiple_of(first + i * BATCH * ROWS, BATCH * ROWS)
+            there = pl.multiple_of(i * BATCH * PITCH, BATCH * PITCH)
+            for piece in range(ROWS // 8):
+                weights = [taps[t, piece * 8 : piece * 8 + 8, :] for t in range(TAPS)]
+                frames = [
+                    raw[p, pl.ds(base + (s * ROWS + piece * 8), 8), :].astype(jnp.float32)
+                    for s in range(BATCH + HIST)
+                ]
+                for s in range(BATCH):
+                    total = weights[0] * frames[s]
+                    for t in range(1, TAPS):
+                        total = total + weights[t] * frames[s + t]
+                    filt[p, pl.ds(there + (s * PITCH + piece * 8), 8), :] = total
+
+    for a in range(NA):
+        for part in range(STEP // 16):
+            x = [
+                tuple(
+                    filt[p, pl.ds(part * 16 * PITCH + m * NA + a, 16, stride=PITCH), :]
+                    for p in range(2)
+                )
+                for m in range(RADIX)
+            ]
+            y = butterfly(x)
+            for j in range(RADIX):
+                for p in range(2):
+                    value = y[j][p]
+                    top = value.astype(jnp.bfloat16)
+                    left_over = (value - top.astype(jnp.float32)).astype(jnp.bfloat16)
+                    store(j, a, part * 16, slice(p * LANES, (p + 1) * LANES), top, left_over)
+
+
+def body_kernel(volts, taps, high, low, late_high, late_low, raw, filt, arrived):
+    start = (STEP - HIST) * ROWS
+
     def chunk_copy(c):
         at = pl.multiple_of(c * STEP * ROWS, STEP * ROWS)
         return pltpu.make_async_copy(
-            volts.at[:, pl.ds(at, STEP * ROWS), :],
+            volts.at[:, pl.ds(STEP * ROWS + at, STEP * ROWS), :],
             raw.at[:, pl.ds(HIST * ROWS + at, STEP * ROWS), :],
             arrived.at[c],
         )
 
+    before = pltpu.make_async_copy(
+        volts.at[:, pl.ds(start, HIST * ROWS), :],
+        raw.at[:, pl.ds(0, HIST * ROWS), :],
+        arrived.at[BODY // STEP],
+    )
+    before.start()
+    for c in range(BODY // STEP):
+        chunk_copy(c).start()
+    before.wait()
+
+    @pl.loop(0, BODY // STEP)
+    def _(c):
+        chunk_copy(c).wait()
+
+        def store(j, a, row, lanes, top, left_over):
+            row = pl.multiple_of(a * BODY + c * STEP + row, 16)
+            early = j < len(PLANE_FIRST)
+            here = j if early else j - len(PLANE_FIRST)
+            (high if early else late_high)[here, pl.ds(row, 16), lanes] = top
+            (low if early else late_low)[here, pl.ds(row, 16), lanes] = left_over
+
+        mix(c * STEP * ROWS, raw, taps, filt, store)
+
+
+def channel_kernel(
+    place, volts, tail, taps, turn, body_high, body_low, rest, late_high, late_low,
+    raw, filt, high, low, table, spread, arrived,
+):
+    chunk = pltpu.make_async_copy(
+        volts.at[:, pl.ds(0, STEP * ROWS), :],
+        raw.at[:, pl.ds(HIST * ROWS, STEP * ROWS), :],
+        arrived.at[0],
+    )
     table_copy = pltpu.make_async_copy(
-        turn.at[pl.ds(0, len(PLANE_FIRST)), pl.ds(0, 2)], table, arrived.at[SPEC // STEP]
-    )
-    for c in range(SPEC // STEP):
-        chunk_copy(c).start()
+        turn.at[pl.ds(0, len(PLANE_FIRST)), pl.ds(0, 2)], table, arrived.at[1]
+    )
+    chunk.start()
     table_copy.start()
     before = tail[...].astype(jnp.float32).astype(jnp.int32)
     raw[:, : HIST * ROWS, :] = jnp.where(place[1] > 0, before, 0)
-
-    @pl.loop(0, SPEC // STEP)
-    def _(c):
-        chunk_copy(c).wait()
-        for p in range(2):
-
-            @pl.loop(0, STEP // BATCH)
-            def _(i):
-                into = pl.multiple_of(i * BATCH * ROWS, BATCH * ROWS)
-                there = pl.multiple_of(i * BATCH * PITCH, BATCH * PITCH)
-                base = pl.multiple_of(c * STEP * ROWS + into, BATCH * ROWS)
-                for piece in range(ROWS // 8):
-                    weights = [taps[t, piece * 8 : piece * 8 + 8, :] for t in range(TAPS)]
-                    frames = [
-                        raw[p, pl.ds(base + (s * ROWS + piece * 8), 8), :].astype(jnp.float32)
-                        for s in range(BATCH + HIST)
-                    ]
-                    for s in range(BATCH):
-                        total = weights[0] * frames[s]
-                        for t in range(1, TAPS):
-                            total = total + weights[t] * frames[s + t]
-                        filt[p, pl.ds(there + (s * PITCH + piece * 8), 8), :] = total
-
-        for a in range(NA):
-            for part in range(STEP // 16):
-                x = [
-                    tuple(
-                        filt[p, pl.ds(part * 16 * PITCH + m * NA + a, 16, stride=PITCH), :]
-                        for p in range(2)
-                    )
-                    for m in range(RADIX)
-                ]
-                y = butterfly(x)
-                row = pl.multiple_of(a * SPEC + c * STEP + part * 16, 16)
-                for j in range(RADIX):
-                    for p in range(2):
-                        value = y[j][p]
-                        top = value.astype(jnp.bfloat16)
-                        left_over = (value - top.astype(jnp.float32)).astype(jnp.bfloat16)
-                        at = (slice(p * LANES, (p + 1) * LANES),)
-                        early = j < len(PLANE_FIRST)
-                        here = j if early else j - len(PLANE_FIRST)
-                        (high if early else late_high)[here, pl.ds(row, 16), *at] = top
-                        (low if early else late_low)[here, pl.ds(row, 16), *at] = left_over
-
+    chunk.wait()
+
+    def store(j, a, row, lanes, top, left_over):
+        early = j < len(PLANE_FIRST)
+        here = j if early else j - len(PLANE_FIRST)
+        row = a * STEP + row
+        (high if early else late_high)[here, row : row + 16, lanes] = top
+        (low if early else late_low)[here, row : row + 16, lanes] = left_over
+
+    mix(0, raw, taps, filt, store)
     table_copy.wait()
     for i in range(len(PLANE_FIRST)):
-        blocks = transform(place[0], i, table, high, low, spread)
+        tops, lows = joined(high, body_high, i, i), joined(low, body_low, i, i)
+        blocks = transform(place[0], i, table, tops, lows, spread)
         for slot in range(2):
             rest[:, slot, i] = blocks[slot]
 
 
-def late_kernel(place, turn, high, low, stay, leave, table, spread, arrived):
+def late_kernel(place, turn, body_high, body_low, high, low, stay, leave, table, spread, arrived):
     table_copy = pltpu.make_async_copy(
         turn.at[pl.ds(len(PLANE_FIRST), len(Y_FIRST)), pl.ds(0, 2)], table, arrived
     )
     table_copy.start()
     table_copy.wait()
     for i in range(len(Y_FIRST)):
-        stay[:, i], leave[:, i] = transform(place[0], i, table, high, low, spread)
-
-
-def channelize(place, volts, tail, turn):
+        tops, lows = joined(high, body_high, i, i), joined(low, body_low, i, i)
+        stay[:, i], leave[:, i] = transform(place[0], i, table, tops, lows, spread)
+
+
+def channelize_body(volts, taps):
+    vmem = pl.BlockSpec(memory_space=pltpu.VMEM)
+    hbm = pl.BlockSpec(memory_space=pltpu.HBM)
+    mixed = jax.ShapeDtypeStruct((len(PLANE_FIRST), NA * BODY, 2 * LANES), jnp.bfloat16)
+    late = jax.ShapeDtypeStruct((len(Y_FIRST), NA * BODY, 2 * LANES), jnp.bfloat16)
+    return pl.pallas_call(
+        body_kernel,
+        in_specs=[hbm, vmem],
+        out_specs=[vmem] * 4,
+        scratch_shapes=[
+            pltpu.VMEM((2, (HIST + BODY) * ROWS, LANES), jnp.int32),
+            pltpu.VMEM((2, STEP * PITCH, LANES), jnp.float32),
+            pltpu.SemaphoreType.DMA((BODY // STEP + 1,)),
+        ],
+        out_shape=[mixed, mixed, late, late],
+        compiler_params=pltpu.CompilerParams(vmem_limit_bytes=VMEM_KIB * 1024),
+        cost_estimate=pl.CostEstimate(
+            flops=10**9, bytes_accessed=8 * 1024 * 1024, transcendentals=0
+        ),
+        name="channelize_body",
+    )(volts, taps)
+
+
+def channelize(place, volts, tail, taps, turn, high, low):
     few, many = len(Y_FIRST), len(PLANE_FIRST)
     vmem = pl.BlockSpec(memory_space=pltpu.VMEM)
     hbm = pl.BlockSpec(memory_space=pltpu.HBM)
-    mixed = jax.ShapeDtypeStruct((few, NA * SPEC, 2 * LANES), jnp.bfloat16)
+    mixed = jax.ShapeDtypeStruct((few, NA * STEP, 2 * LANES), jnp.bfloat16)
     return pl.pallas_call(
         channel_kernel,
-        in_specs=[pl.BlockSpec(memory_space=pltpu.SMEM), hbm, vmem, vmem, hbm],
+        in_specs=[pl.BlockSpec(memory_space=pltpu.SMEM), hbm, vmem, vmem, hbm, vmem, vmem],
         out_specs=[vmem, vmem, vmem],
         scratch_shapes=[
-            pltpu.VMEM((2, (HIST + SPEC) * ROWS, LANES), jnp.int32),
+            pltpu.VMEM((2, (HIST + STEP) * ROWS, LANES), jnp.int32),
             pltpu.VMEM((2, STEP * PITCH, LANES), jnp.float32),
-            pltpu.VMEM((many, NA * SPEC, 2 * LANES), jnp.bfloat16),
-            pltpu.VMEM((many, NA * SPEC, 2 * LANES), jnp.bfloat16),
+            pltpu.VMEM((many, NA * STEP, 2 * LANES), jnp.bfloat16),
+            pltpu.VMEM((many, NA * STEP, 2 * LANES), jnp.bfloat16),
             pltpu.VMEM((many, 2, 2 * FINE, 2 * FINE), jnp.bfloat16),
             pltpu.VMEM((2 * GROUP * 8, LANES), jnp.float32),
-            pltpu.SemaphoreType.DMA((SPEC // STEP + 1,)),
+            pltpu.SemaphoreType.DMA((2,)),
         ],
         out_shape=[jax.ShapeDtypeStruct((GROUP, 2, many, 8, LANES), jnp.bfloat16), mixed, mixed],
-        compiler_params=pltpu.CompilerParams(vmem_limit_bytes=VMEM_KIB * 1024),
+        compiler_params=pltpu.CompilerParams(vmem_limit_bytes=MORE_KIB * 1024),
         cost_estimate=pl.CostEstimate(
-            flops=2 * 10**9, bytes_accessed=8 * 1024 * 1024, transcendentals=0
+            flops=10**9, bytes_accessed=6 * 1024 * 1024, transcendentals=0
         ),
         name="channelize",
-    )(place, volts, tail, taps_table(), turn)
-
-
-def channelize_late(place, turn, high, low):
+    )(place, volts, tail, taps, turn, high, low)
+
+
+def channelize_late(place, turn, body_high, body_low, high, low):
     few = len(Y_FIRST)
     vmem = pl.BlockSpec(memory_space=pltpu.VMEM)
     hbm = pl.BlockSpec(memory_space=pltpu.HBM)
     block = jax.ShapeDtypeStruct((GROUP, few, 8, LANES), jnp.bfloat16)
     return pl.pallas_call(
         late_kernel,
-        in_specs=[pl.BlockSpec(memory_space=pltpu.SMEM), hbm, vmem, vmem],
+        in_specs=[pl.BlockSpec(memory_space=pltpu.SMEM), hbm, vmem, vmem, vmem, vmem],
         out_specs=[vmem, vmem],
         scratch_shapes=[
             pltpu.VMEM((few, 2, 2 * FINE, 2 * FINE), jnp.bfloat16),
@@ -245,7 +313,7 @@
             flops=6 * 10**8, bytes_accessed=3 * 1024 * 1024, transcendentals=0
         ),
         name="channelize_late",
-    )(place, turn, high, low)
+    )(place, turn, body_high, body_low, high, low)
 
 
 def correlate_kernel(scale, first, count, picks, place, *refs):
@@ -348,8 +416,10 @@
     place = jnp.stack([lax.axis_index("y_lo"), lax.axis_index("tm")]).astype(jnp.int32)
     scale = np.float32(1.0 / (SPEC * lax.axis_size("tm")))
     turn = jnp.asarray(turn_table())
-    rest, high, low = channelize(place, volts, tail, turn)
-    stay, leave = channelize_late(place, turn, high, low)
+    taps = taps_table()
+    body = channelize_body(volts, taps)
+    rest, *head = channelize(place, volts, tail, taps, turn, *body[:2])
+    stay, leave = channelize_late(place, turn, *body[2:], *head)
     over = lax.all_to_all(rest, PLANE, split_axis=0, concat_axis=0, tiled=True)
     early = jnp.stack([stay, *exchange(leave, stay)], axis=1)
     far, near, cross = exchange(over[:, 1], over[:, 0])

time: 111 us -> 110 us (level)
  starting transfers between devices: 30.9 us -> 28.2 us
  Pallas kernels: 16.6 us -> 17.9 us
    pallas_call x0 -> x1, Pallas kernels: none -> 3.48 us  [channelize_body(): pl.pallas_call(body_kernel, in_specs=[hbm, vmem], out_specs=[vmem] * 4, s...]
    ppermute x2, starting transfers between devices: 6.01 us -> 3.41 us  [exchange(): far = lax.ppermute(far_part, 'tm', flip)]
    pallas_call x1, Pallas kernels: 7.26 us -> 5.1 us  [channelize(): pl.pallas_call(channel_kernel, in_specs=[pl.BlockSpec(memory_space=pltpu....]
    ppermute x2, waiting for transfers between devices: 21.8 us -> 23.6 us  [exchange(): far = lax.ppermute(far_part, 'tm', flip)]
    ppermute x1, waiting for transfers between devices: 1.3 us -> 0.01 us  [local(): tail = lax.ppermute(tail, 'tm', [(0, 1), (1, 0)])]
  transfers between devices with their start and end apart: 9 -> 9, of which waited for: 7 -> 6; matrix products, arithmetic and copies ran while one was open for 1% -> 2% of each run, Pallas kernels for 5% -> 9%
where the time goes in v4:
time: 110 us
  waiting for transfers between devices  58.5 us (53%)
  starting transfers between devices  28.2 us (26%)
  Pallas kernels  17.9 us (16%)
  other arithmetic  2.45 us (2%)
  local copies, waits for them, and re-layouts  2.32 us (2%)
    ppermute x2, waiting for transfers between devices, exchange(): cross = lax.ppermute(near_part, ('y_lo', 'tm'), both)  24 us
    ppermute x2, waiting for transfers between devices, exchange(): far = lax.ppermute(far_part, 'tm', flip)  23.6 us
    all_to_all x1, starting transfers between devices, local(): over = lax.all_to_all(rest, PLANE, split_axis=0, concat_axis=0, tiled=True)  12.4 us
    all_to_all x1, waiting for transfers between devices, local(): over = lax.all_to_all(rest, PLANE, split_axis=0, concat_axis=0, tiled=True)  7.88 us
    pallas_call x2, Pallas kernels, correlate(): pl.pallas_call(kernel, in_specs=in_specs, out_specs=hbm, scratch_shapes=[...  7.61 us
    all_to_all x1, starting transfers between devices, local(): lax.all_to_all(early, PLANE, split_axis=0, concat_axis=0, tiled=True)  6.16 us
    pallas_call x1, Pallas kernels, channelize(): pl.pallas_call(channel_kernel, in_specs=[pl.BlockSpec(memory_space=pltpu....  5.1 us
    ppermute x1, starting transfers between devices, local(): tail = lax.ppermute(tail, 'tm', [(0, 1), (1, 0)])  3.83 us
  transfers between devices with their start and end apart: 9, of which 6 were waited for; matrix products, arithmetic and copies ran while one was open for 2% of the time, Pallas kernels for 9%

profile of v4, /device:TPU:1, one launch (start us, length us, event | category | flops | bytes accessed | tf_op | source)
XLA Modules:
  0.0 109.6 jit_solution(1187504484051595244)
XLA Ops:
  0.0 0.9 slice_convert_fusion
  0.9 3.8 %collective-permute-start = (bf16[2,96,128]{2,1,0:T(8,128)(2,1)S(1)}, bf16[2,96,128]{2,1,0:T(8,128)(2,1)S(1)}, u32[]{:S(2)}, u32[]{:S(2)}) collective-permute-start(bf16[2,96,128]{2,1,0:T(8,128)(2,1)S(1)} %slice_convert_fusion), channel_id=1, source_target_pairs={{0,1},{1,0},{2,3},{3,2},{4,5},{5,4},{6,7},{7,6},{8,9},{9,8},{10,11... | collective-permute-start | bytes 147464 | tf_op jit(solution)/shard_map/ppermute | solution.py:415
  4.7 0.1 fusion.13
  4.8 0.1 pad_add_fusion.place.refs_0_
  4.9 3.5 %channelize_body.1 = (bf16[5,384,256]{2,1,0:T(8,128)(2,1)S(1)}, bf16[5,384,256]{2,1,0:T(8,128)(2,1)S(1)}, bf16[3,384,256]{2,1,0:T(8,128)(2,1)S(1)}, bf16[3,384,256]{2,1,0:T(8,128)(2,1)S(1)}) custom-call(s32[2,4096,128]{2,1,0:T(8,128)} %bitcast.24, f32[4,32,128]{2,1,0:T(8,128)S(1)} %bitcast.20), custom_call_target="tpu_custom_call" | custom-call | flops 1000000000 | bytes 8388608 | tf_op jit(solution)/shard_map/channelize_body/pallas_call | solution.py:251
  8.4 5.1 %channelize.1 = (bf16[64,2,5,8,128]{4,3,2,1,0:T(8,128)(2,1)}, bf16[3,128,256]{2,1,0:T(8,128)(2,1)S(1)}, bf16[3,128,256]{2,1,0:T(8,128)(2,1)S(1)}) custom-call(s32[2]{0:T(128)S(1)} %pad_add_fusion.place.refs_0_, s32[2,4096,128]{2,1,0:T(8,128)} %bitcast.25, bf16[2,96,128]{2,1,0:T(8,128)(2,1)S(1)} %collective-permute-done.tail, f32[4,32,128]{2,1,0:T(8,128)S(1)} %bitcast.21, ...), custom_call_target="tpu_custom_call" | custom-call | flops 1000000000 | bytes 6291456 | tf_op jit(solution)/shard_map/channelize/pallas_call | solution.py:274
  13.5 12.4 %all-to-all-start.1 = ((bf16[64,2,5,8,128]{4,3,2,1,0:T(8,128)(2,1)}), bf16[64,2,5,8,128]{4,3,2,1,0:T(8,128)(2,1)S(1)}, u32[]{:S(2)}, u32[]{:S(2)}) async-start(bf16[64,2,5,8,128]{4,3,2,1,0:T(8,128)(2,1)} %get-tuple-element.22), calls=%async_computation.1 | async-start | bytes 2621440 | tf_op jit(solution)/shard_map/all_to_all | solution.py:423
  26.0 2.2 %copy-done = bf16[8,4,256,256]{3,2,1,0:T(8,128)(2,1)S(1)} copy-done((bf16[8,4,256,256]{3,2,1,0:T(8,128)(2,1)S(1)}, bf16[8,4,256,256]{3,2,1,0:T(8,128)(2,1)}, u32[]{:S(2)}) %copy-start) | copy-done | bytes 4194328
  28.2 1.7 %channelize_late.1 = (bf16[64,3,8,128]{3,2,1,0:T(8,128)(2,1)S(1)}, bf16[64,3,8,128]{3,2,1,0:T(8,128)(2,1)S(1)}) custom-call(s32[2]{0:T(128)S(1)} %pad_add_fusion.place.refs_0_, bf16[8,4,256,256]{3,2,1,0:T(8,128)(2,1)S(1)} %copy-done, bf16[3,384,256]{2,1,0:T(8,128)(2,1)S(1)} %get-tuple-element.14.body_high, ...), custom_call_target="tpu_custom_call" | custom-call | flops 600000000 | bytes 3145728 | tf_op jit(solution)/shard_map/channelize_late/pallas_call | solution.py:301
  29.9 1.7 %collective-permute-start.1 = (bf16[64,3,8,128]{3,2,1,0:T(8,128)(2,1)S(1)}, bf16[64,3,8,128]{3,2,1,0:T(8,128)(2,1)S(1)}, u32[]{:S(2)}, u32[]{:S(2)}) collective-permute-start(bf16[64,3,8,128]{3,2,1,0:T(8,128)(2,1)S(1)} %get-tuple-element.20), channel_id=1, source_target_pairs={{0,1},{1,0},{2,3},{3,2},{4,5},{5,4},{6,7},{7,6},{8,9},{9,8},{10,11... | collective-permute-start | bytes 1179656 | tf_op jit(solution)/shard_map/ppermute | solution.py:407
  31.6 1.2 %collective-permute-start.3 = (bf16[64,3,8,128]{3,2,1,0:T(8,128)(2,1)S(1)}, bf16[64,3,8,128]{3,2,1,0:T(8,128)(2,1)S(1)}, u32[]{:S(2)}, u32[]{:S(2)}) collective-permute-start(bf16[64,3,8,128]{3,2,1,0:T(8,128)(2,1)S(1)} %get-tuple-element.21), channel_id=1, source_target_pairs={{0,129},{129,0},{1,128},{128,1},{2,131},{131,2},{3,130},{130,3},{4... | collective-permute-start | bytes 1179656 | tf_op jit(solution)/shard_map/ppermute | solution.py:406
  32.7 9.0 %collective-permute-done.1 = bf16[64,3,8,128]{3,2,1,0:T(8,128)(2,1)S(1)} collective-permute-done((bf16[64,3,8,128]{3,2,1,0:T(8,128)(2,1)S(1)}, bf16[64,3,8,128]{3,2,1,0:T(8,128)(2,1)S(1)}, u32[]{:S(2)}, u32[]{:S(2)}) %collective-permute-start.1) | collective-permute-done | bytes 393248 | tf_op jit(solution)/shard_map/ppermute | solution.py:407
  41.7 9.2 %collective-permute-done.3 = bf16[64,3,8,128]{3,2,1,0:T(8,128)(2,1)S(1)} collective-permute-done((bf16[64,3,8,128]{3,2,1,0:T(8,128)(2,1)S(1)}, bf16[64,3,8,128]{3,2,1,0:T(8,128)(2,1)S(1)}, u32[]{:S(2)}, u32[]{:S(2)}) %collective-permute-start.3) | collective-permute-done | bytes 393248 | tf_op jit(solution)/shard_map/ppermute | solution.py:406
  50.9 1.4 %pad_maximum_fusion = bf16[64,4,3,8,128]{4,3,2,1,0:T(8,128)(2,1)} fusion(bf16[64,1,3,8,128]{4,3,2,1,0:T(8,128)(2,1)S(1)} %bitcast.27, bf16[64,1,3,8,128]{4,3,2,1,0:T(8,128)(2,1)S(1)} %bitcast.28, bf16[64,1,3,8,128]{4,3,2,1,0:T(8,128)(2,1)S(1)} %bitcast.26, bf16[64,1,3,8,128]{4,3,2,1,0:T(8,128)(2,1)S(1)} %bitcast.22), kind=kLoop, calls=%fused_computation | loop fusion | flops 2359296 | bytes 3145728 | tf_op jit(solution)/shard_map/stack | solution.py:424
  52.3 7.9 %all-to-all-done.1.refs_1_ = bf16[64,2,5,8,128]{4,3,2,1,0:T(8,128)(2,1)S(1)} async-done(((bf16[64,2,5,8,128]{4,3,2,1,0:T(8,128)(2,1)}), bf16[64,2,5,8,128]{4,3,2,1,0:T(8,128)(2,1)S(1)}, u32[]{:S(2)}, u32[]{:S(2)}) %all-to-all-start.1) | async-done | bytes 1310752 | tf_op jit(solution)/shard_map/all_to_all | solution.py:423
  60.2 6.2 %all-to-all-start = ((bf16[64,4,3,8,128]{4,3,2,1,0:T(8,128)(2,1)}), bf16[64,4,3,8,128]{4,3,2,1,0:T(8,128)(2,1)S(1)}, u32[]{:S(2)}, u32[]{:S(2)}) async-start(bf16[64,4,3,8,128]{4,3,2,1,0:T(8,128)(2,1)} %pad_maximum_fusion), calls=%async_computation | async-start | bytes 3145728 | tf_op jit(solution)/shard_map/all_to_all | solution.py:426
  66.3 0.1 slice_bitcast_fusion
  66.5 1.7 %collective-permute-start.4 = (bf16[64,5,8,128]{3,2,1,0:T(8,128)(2,1)S(1)}, bf16[64,5,8,128]{3,2,1,0:T(8,128)(2,1)S(1)}, u32[]{:S(2)}, u32[]{:S(2)}) collective-permute-start(bf16[64,5,8,128]{3,2,1,0:T(8,128)(2,1)S(1)} %get-tuple-element.24), channel_id=1, source_target_pairs={{0,1},{1,0},{2,3},{3,2},{4,5},{5,4},{6,7},{7,6},{8,9},{9,8},{10,11... | collective-permute-start | bytes 1966088 | tf_op jit(solution)/shard_map/ppermute | solution.py:407
  68.2 1.2 %collective-permute-start.6 = (bf16[64,5,8,128]{3,2,1,0:T(8,128)(2,1)S(1)}, bf16[64,5,8,128]{3,2,1,0:T(8,128)(2,1)S(1)}, u32[]{:S(2)}, u32[]{:S(2)}) collective-permute-start(bf16[64,5,8,128]{3,2,1,0:T(8,128)(2,1)S(1)} %get-tuple-element.23), channel_id=1, source_target_pairs={{0,129},{129,0},{1,128},{128,1},{2,131},{131,2},{3,130},{130,3},{4... | collective-permute-start | bytes 1966088 | tf_op jit(solution)/shard_map/ppermute | solution.py:406
  69.3 14.6 %collective-permute-done.4.refs_2_ = bf16[64,5,8,128]{3,2,1,0:T(8,128)(2,1)S(1)} collective-permute-done((bf16[64,5,8,128]{3,2,1,0:T(8,128)(2,1)S(1)}, bf16[64,5,8,128]{3,2,1,0:T(8,128)(2,1)S(1)}, u32[]{:S(2)}, u32[]{:S(2)}) %collective-permute-start.4) | collective-permute-done | bytes 655392 | tf_op jit(solution)/shard_map/ppermute | solution.py:407
  84.0 14.8 %collective-permute-done.6.refs_4_ = bf16[64,5,8,128]{3,2,1,0:T(8,128)(2,1)S(1)} collective-permute-done((bf16[64,5,8,128]{3,2,1,0:T(8,128)(2,1)S(1)}, bf16[64,5,8,128]{3,2,1,0:T(8,128)(2,1)S(1)}, u32[]{:S(2)}, u32[]{:S(2)}) %collective-permute-start.6) | collective-permute-done | bytes 655392 | tf_op jit(solution)/shard_map/ppermute | solution.py:406
  98.8 4.3 %correlate.2.refs_6_ = f32[2,8,256,512]{3,2,1,0:T(8,128)} custom-call(s32[2]{0:T(128)S(1)} %pad_add_fusion.place.refs_0_, bf16[64,2,5,8,128]{4,3,2,1,0:T(8,128)(2,1)S(1)} %all-to-all-done.1.refs_1_, bf16[64,5,8,128]{3,2,1,0:T(8,128)(2,1)S(1)} %collective-permute-done.4.refs_2_, bf16[64,5,8,128]{3,2,1,0:T(8,128)(2,1)S(1)} %collective-permute-done.5.refs_3_, ...), custom_call_target="tpu_custom_call" | custom-call | flops 2000000000 | bytes 7864320 | tf_op jit(solution)/shard_map/correlate/pallas_call | solution.py:384
  103.1 3.0 %all-to-all-done.refs_1_.refs_2_.refs_3_.refs_4_ = bf16[64,4,3,8,128]{4,3,2,1,0:T(8,128)(2,1)S(1)} async-done(((bf16[64,4,3,8,128]{4,3,2,1,0:T(8,128)(2,1)}), bf16[64,4,3,8,128]{4,3,2,1,0:T(8,128)(2,1)S(1)}, u32[]{:S(2)}, u32[]{:S(2)}) %all-to-all-start) | async-done | bytes 1572896 | tf_op jit(solution)/shard_map/all_to_all | solution.py:426
  106.1 3.3 %correlate.3 = f32[2,8,256,512]{3,2,1,0:T(8,128)} custom-call(s32[2]{0:T(128)S(1)} %pad_add_fusion.place.refs_0_, bf16[64,4,3,8,128]{4,3,2,1,0:T(8,128)(2,1)S(1)} %all-to-all-done.refs_1_.refs_2_.refs_3_.refs_4_, bf16[64,4,3,8,128]{4,3,2,1,0:T(8,128)(2,1)S(1)} %all-to-all-done.refs_1_.refs_2_.refs_3_.refs_4_, ...), custom_call_target="tpu_custom_call", output_to_operand_aliasing={{}: (6, {})} | custom-call | flops 1200000000 | bytes 4718592 | tf_op jit(solution)/shard_map/correlate/pallas_call | solution.py:384
  (9 shorter events, 0.0 us)
Async XLA Ops:
  0.9 7.5 %collective-permute-start = (bf16[2,96,128]{2,1,0:T(8,128)(2,1)S(1)}, bf16[2,96,128]{2,1,0:T(8,128)(2,1)S(1)}, u32[]{:S(2)}, u32[]{:S(2)}) collective-permute-start(bf16[2,96,128]{2,1,0:T(8,128)(2,1)S(1)} %slice_convert_fusion), channel_id=1, source_target_pairs={{0,1},{1,0},{2,3},{3,2},{4,5},{5,4},{6,7},{7,6},{8,9},{9,8},{10,11... | collective-permute-start | bytes 147464 | tf_op jit(solution)/shard_map/ppermute | solution.py:415
  13.5 46.6 %all-to-all-start.1 = ((bf16[64,2,5,8,128]{4,3,2,1,0:T(8,128)(2,1)}), bf16[64,2,5,8,128]{4,3,2,1,0:T(8,128)(2,1)S(1)}, u32[]{:S(2)}, u32[]{:S(2)}) async-start(bf16[64,2,5,8,128]{4,3,2,1,0:T(8,128)(2,1)} %get-tuple-element.22), calls=%async_computation.1 | async-start | bytes 2621440 | tf_op jit(solution)/shard_map/all_to_all | solution.py:423
  26.0 2.2 %copy-start = (bf16[8,4,256,256]{3,2,1,0:T(8,128)(2,1)S(1)}, bf16[8,4,256,256]{3,2,1,0:T(8,128)(2,1)}, u32[]{:S(2)}) copy-start(bf16[8,4,256,256]{3,2,1,0:T(8,128)(2,1)} %constant.82.clone.turn) | copy-start | bytes 12582916
  29.9 11.9 %collective-permute-start.1 = (bf16[64,3,8,128]{3,2,1,0:T(8,128)(2,1)S(1)}, bf16[64,3,8,128]{3,2,1,0:T(8,128)(2,1)S(1)}, u32[]{:S(2)}, u32[]{:S(2)}) collective-permute-start(bf16[64,3,8,128]{3,2,1,0:T(8,128)(2,1)S(1)} %get-tuple-element.20), channel_id=1, source_target_pairs={{0,1},{1,0},{2,3},{3,2},{4,5},{5,4},{6,7},{7,6},{8,9},{9,8},{10,11... | collective-permute-start | bytes 1179656 | tf_op jit(solution)/shard_map/ppermute | solution.py:407
  31.6 19.3 %collective-permute-start.3 = (bf16[64,3,8,128]{3,2,1,0:T(8,128)(2,1)S(1)}, bf16[64,3,8,128]{3,2,1,0:T(8,128)(2,1)S(1)}, u32[]{:S(2)}, u32[]{:S(2)}) collective-permute-start(bf16[64,3,8,128]{3,2,1,0:T(8,128)(2,1)S(1)} %get-tuple-element.21), channel_id=1, source_target_pairs={{0,129},{129,0},{1,128},{128,1},{2,131},{131,2},{3,130},{130,3},{4... | collective-permute-start | bytes 1179656 | tf_op jit(solution)/shard_map/ppermute | solution.py:406
  32.7 18.2 %collective-permute-start.2 = (bf16[64,3,8,128]{3,2,1,0:T(8,128)(2,1)S(1)}, bf16[64,3,8,128]{3,2,1,0:T(8,128)(2,1)S(1)}, u32[]{:S(2)}, u32[]{:S(2)}) collective-permute-start(bf16[64,3,8,128]{3,2,1,0:T(8,128)(2,1)S(1)} %get-tuple-element.21), channel_id=1, source_target_pairs={{0,128},{128,0},{1,129},{129,1},{2,130},{130,2},{3,131},{131,3},{4... | collective-permute-start | bytes 1179656 | tf_op jit(solution)/shard_map/ppermute | solution.py:405
  60.2 46.0 %all-to-all-start = ((bf16[64,4,3,8,128]{4,3,2,1,0:T(8,128)(2,1)}), bf16[64,4,3,8,128]{4,3,2,1,0:T(8,128)(2,1)S(1)}, u32[]{:S(2)}, u32[]{:S(2)}) async-start(bf16[64,4,3,8,128]{4,3,2,1,0:T(8,128)(2,1)} %pad_maximum_fusion), calls=%async_computation | async-start | bytes 3145728 | tf_op jit(solution)/shard_map/all_to_all | solution.py:426
  66.3 32.4 %copy-start.1 = (bf16[256,256]{1,0:T(8,128)(2,1)S(1)}, bf16[256,256]{1,0:T(8,128)(2,1)}, u32[]{:S(2)}) copy-start(bf16[256,256]{1,0:T(8,128)(2,1)} %constant.83.clone.refs_5_) | copy-start | bytes 393220
  66.5 17.5 %collective-permute-start.4 = (bf16[64,5,8,128]{3,2,1,0:T(8,128)(2,1)S(1)}, bf16[64,5,8,128]{3,2,1,0:T(8,128)(2,1)S(1)}, u32[]{:S(2)}, u32[]{:S(2)}) collective-permute-start(bf16[64,5,8,128]{3,2,1,0:T(8,128)(2,1)S(1)} %get-tuple-element.24), channel_id=1, source_target_pairs={{0,1},{1,0},{2,3},{3,2},{4,5},{5,4},{6,7},{7,6},{8,9},{9,8},{10,11... | collective-permute-start | bytes 1966088 | tf_op jit(solution)/shard_map/ppermute | solution.py:407
  68.2 30.6 %collective-permute-start.6 = (bf16[64,5,8,128]{3,2,1,0:T(8,128)(2,1)S(1)}, bf16[64,5,8,128]{3,2,1,0:T(8,128)(2,1)S(1)}, u32[]{:S(2)}, u32[]{:S(2)}) collective-permute-start(bf16[64,5,8,128]{3,2,1,0:T(8,128)(2,1)S(1)} %get-tuple-element.23), channel_id=1, source_target_pairs={{0,129},{129,0},{1,128},{128,1},{2,131},{131,2},{3,130},{130,3},{4... | collective-permute-start | bytes 1966088 | tf_op jit(solution)/shard_map/ppermute | solution.py:406
  69.3 29.4 %collective-permute-start.5 = (bf16[64,5,8,128]{3,2,1,0:T(8,128)(2,1)S(1)}, bf16[64,5,8,128]{3,2,1,0:T(8,128)(2,1)S(1)}, u32[]{:S(2)}, u32[]{:S(2)}) collective-permute-start(bf16[64,5,8,128]{3,2,1,0:T(8,128)(2,1)S(1)} %get-tuple-element.23), channel_id=1, source_target_pairs={{0,128},{128,0},{1,129},{129,1},{2,130},{130,2},{3,131},{131,3},{4... | collective-permute-start | bytes 1966088 | tf_op jit(solution)/shard_map/ppermute | solution.py:405

commit v5 on v4

--- a/solution.py
+++ b/solution.py
@@ -14,7 +14,7 @@
 LANES = 128
 NA = 4
 SPEC = 128
-STEP = 32
+STEP = 16
 BODY = SPEC - STEP
 BATCH = 8
 SLOTS = 5

time: 110 us -> 110 us (level)
  no operation moved by 1% of the time
where the time goes in v5:
time: 110 us; the launch traced here: 109 us
  waiting for transfers between devices  58.5 us (53%)
  starting transfers between devices  28.2 us (26%)
  Pallas kernels  17.6 us (16%)
  other arithmetic  2.45 us (2%)
  local copies, waits for them, and re-layouts  2.32 us (2%)
    ppermute x2, waiting for transfers between devices, exchange(): cross = lax.ppermute(near_part, ('y_lo', 'tm'), both)  24 us
    ppermute x2, waiting for transfers between devices, exchange(): far = lax.ppermute(far_part, 'tm', flip)  23.6 us
    all_to_all x1, starting transfers between devices, local(): over = lax.all_to_all(rest, PLANE, split_axis=0, concat_axis=0, tiled=True)  12.5 us
    all_to_all x1, waiting for transfers between devices, local(): over = lax.all_to_all(rest, PLANE, split_axis=0, concat_axis=0, tiled=True)  7.88 us
    pallas_call x2, Pallas kernels, correlate(): pl.pallas_call(kernel, in_specs=in_specs, out_specs=hbm, scratch_shapes=[...  7.62 us
    all_to_all x1, starting transfers between devices, local(): lax.all_to_all(early, PLANE, split_axis=0, concat_axis=0, tiled=True)  6.16 us
    pallas_call x1, Pallas kernels, channelize(): pl.pallas_call(channel_kernel, in_specs=[pl.BlockSpec(memory_space=pltpu....  4.63 us
    ppermute x1, starting transfers between devices, local(): tail = lax.ppermute(tail, 'tm', [(0, 1), (1, 0)])  3.83 us
  transfers between devices with their start and end apart: 9, of which 6 were waited for; matrix products, arithmetic and copies ran while one was open for 2% of the time, Pallas kernels for 9%

profile of v5, /device:TPU:1, one launch (start us, length us, event | category | flops | bytes accessed | tf_op | source)
XLA Modules:
  0.0 109.3 jit_solution(7316126595312732649)
XLA Ops:
  0.0 0.9 slice_convert_fusion
  0.9 3.8 %collective-permute-start = (bf16[2,96,128]{2,1,0:T(8,128)(2,1)S(1)}, bf16[2,96,128]{2,1,0:T(8,128)(2,1)S(1)}, u32[]{:S(2)}, u32[]{:S(2)}) collective-permute-start(bf16[2,96,128]{2,1,0:T(8,128)(2,1)S(1)} %slice_convert_fusion), channel_id=1, source_target_pairs={{0,1},{1,0},{2,3},{3,2},{4,5},{5,4},{6,7},{7,6},{8,9},{9,8},{10,11... | collective-permute-start | bytes 147464 | tf_op jit(solution)/shard_map/ppermute | solution.py:415
  4.7 0.1 fusion.13
  4.8 0.1 pad_add_fusion.place.refs_0_
  4.9 3.7 %channelize_body.1 = (bf16[5,448,256]{2,1,0:T(8,128)(2,1)S(1)}, bf16[5,448,256]{2,1,0:T(8,128)(2,1)S(1)}, bf16[3,448,256]{2,1,0:T(8,128)(2,1)S(1)}, bf16[3,448,256]{2,1,0:T(8,128)(2,1)S(1)}) custom-call(s32[2,4096,128]{2,1,0:T(8,128)} %bitcast.24, f32[4,32,128]{2,1,0:T(8,128)S(1)} %bitcast.20), custom_call_target="tpu_custom_call" | custom-call | flops 1000000000 | bytes 8388608 | tf_op jit(solution)/shard_map/channelize_body/pallas_call | solution.py:251
  8.6 4.6 %channelize.1 = (bf16[64,2,5,8,128]{4,3,2,1,0:T(8,128)(2,1)}, bf16[3,64,256]{2,1,0:T(8,128)(2,1)S(1)}, bf16[3,64,256]{2,1,0:T(8,128)(2,1)S(1)}) custom-call(s32[2]{0:T(128)S(1)} %pad_add_fusion.place.refs_0_, s32[2,4096,128]{2,1,0:T(8,128)} %bitcast.25, bf16[2,96,128]{2,1,0:T(8,128)(2,1)S(1)} %collective-permute-done.tail, f32[4,32,128]{2,1,0:T(8,128)S(1)} %bitcast.21, ...), custom_call_target="tpu_custom_call" | custom-call | flops 1000000000 | bytes 6291456 | tf_op jit(solution)/shard_map/channelize/pallas_call | solution.py:274
  13.3 12.5 %all-to-all-start.1 = ((bf16[64,2,5,8,128]{4,3,2,1,0:T(8,128)(2,1)}), bf16[64,2,5,8,128]{4,3,2,1,0:T(8,128)(2,1)S(1)}, u32[]{:S(2)}, u32[]{:S(2)}) async-start(bf16[64,2,5,8,128]{4,3,2,1,0:T(8,128)(2,1)} %get-tuple-element.22), calls=%async_computation.1 | async-start | bytes 2621440 | tf_op jit(solution)/shard_map/all_to_all | solution.py:423
  25.8 2.2 %copy-done = bf16[8,4,256,256]{3,2,1,0:T(8,128)(2,1)S(1)} copy-done((bf16[8,4,256,256]{3,2,1,0:T(8,128)(2,1)S(1)}, bf16[8,4,256,256]{3,2,1,0:T(8,128)(2,1)}, u32[]{:S(2)}) %copy-start) | copy-done | bytes 4194328
  27.9 1.7 %channelize_late.1 = (bf16[64,3,8,128]{3,2,1,0:T(8,128)(2,1)S(1)}, bf16[64,3,8,128]{3,2,1,0:T(8,128)(2,1)S(1)}) custom-call(s32[2]{0:T(128)S(1)} %pad_add_fusion.place.refs_0_, bf16[8,4,256,256]{3,2,1,0:T(8,128)(2,1)S(1)} %copy-done, bf16[3,448,256]{2,1,0:T(8,128)(2,1)S(1)} %get-tuple-element.14.body_high, ...), custom_call_target="tpu_custom_call" | custom-call | flops 600000000 | bytes 3145728 | tf_op jit(solution)/shard_map/channelize_late/pallas_call | solution.py:301
  29.6 1.5 %collective-permute-start.1 = (bf16[64,3,8,128]{3,2,1,0:T(8,128)(2,1)S(1)}, bf16[64,3,8,128]{3,2,1,0:T(8,128)(2,1)S(1)}, u32[]{:S(2)}, u32[]{:S(2)}) collective-permute-start(bf16[64,3,8,128]{3,2,1,0:T(8,128)(2,1)S(1)} %get-tuple-element.20), channel_id=1, source_target_pairs={{0,1},{1,0},{2,3},{3,2},{4,5},{5,4},{6,7},{7,6},{8,9},{9,8},{10,11... | collective-permute-start | bytes 1179656 | tf_op jit(solution)/shard_map/ppermute | solution.py:407
  31.1 1.4 %collective-permute-start.3 = (bf16[64,3,8,128]{3,2,1,0:T(8,128)(2,1)S(1)}, bf16[64,3,8,128]{3,2,1,0:T(8,128)(2,1)S(1)}, u32[]{:S(2)}, u32[]{:S(2)}) collective-permute-start(bf16[64,3,8,128]{3,2,1,0:T(8,128)(2,1)S(1)} %get-tuple-element.21), channel_id=1, source_target_pairs={{0,129},{129,0},{1,128},{128,1},{2,131},{131,2},{3,130},{130,3},{4... | collective-permute-start | bytes 1179656 | tf_op jit(solution)/shard_map/ppermute | solution.py:406
  32.5 9.0 %collective-permute-done.1 = bf16[64,3,8,128]{3,2,1,0:T(8,128)(2,1)S(1)} collective-permute-done((bf16[64,3,8,128]{3,2,1,0:T(8,128)(2,1)S(1)}, bf16[64,3,8,128]{3,2,1,0:T(8,128)(2,1)S(1)}, u32[]{:S(2)}, u32[]{:S(2)}) %collective-permute-start.1) | collective-permute-done | bytes 393248 | tf_op jit(solution)/shard_map/ppermute | solution.py:407
  41.5 9.2 %collective-permute-done.3 = bf16[64,3,8,128]{3,2,1,0:T(8,128)(2,1)S(1)} collective-permute-done((bf16[64,3,8,128]{3,2,1,0:T(8,128)(2,1)S(1)}, bf16[64,3,8,128]{3,2,1,0:T(8,128)(2,1)S(1)}, u32[]{:S(2)}, u32[]{:S(2)}) %collective-permute-start.3) | collective-permute-done | bytes 393248 | tf_op jit(solution)/shard_map/ppermute | solution.py:406
  50.7 1.4 %pad_maximum_fusion = bf16[64,4,3,8,128]{4,3,2,1,0:T(8,128)(2,1)} fusion(bf16[64,1,3,8,128]{4,3,2,1,0:T(8,128)(2,1)S(1)} %bitcast.27, bf16[64,1,3,8,128]{4,3,2,1,0:T(8,128)(2,1)S(1)} %bitcast.28, bf16[64,1,3,8,128]{4,3,2,1,0:T(8,128)(2,1)S(1)} %bitcast.26, bf16[64,1,3,8,128]{4,3,2,1,0:T(8,128)(2,1)S(1)} %bitcast.22), kind=kLoop, calls=%fused_computation | loop fusion | flops 2359296 | bytes 3145728 | tf_op jit(solution)/shard_map/stack | solution.py:424
  52.0 7.9 %all-to-all-done.1.refs_1_ = bf16[64,2,5,8,128]{4,3,2,1,0:T(8,128)(2,1)S(1)} async-done(((bf16[64,2,5,8,128]{4,3,2,1,0:T(8,128)(2,1)}), bf16[64,2,5,8,128]{4,3,2,1,0:T(8,128)(2,1)S(1)}, u32[]{:S(2)}, u32[]{:S(2)}) %all-to-all-start.1) | async-done | bytes 1310752 | tf_op jit(solution)/shard_map/all_to_all | solution.py:423
  59.9 6.2 %all-to-all-start = ((bf16[64,4,3,8,128]{4,3,2,1,0:T(8,128)(2,1)}), bf16[64,4,3,8,128]{4,3,2,1,0:T(8,128)(2,1)S(1)}, u32[]{:S(2)}, u32[]{:S(2)}) async-start(bf16[64,4,3,8,128]{4,3,2,1,0:T(8,128)(2,1)} %pad_maximum_fusion), calls=%async_computation | async-start | bytes 3145728 | tf_op jit(solution)/shard_map/all_to_all | solution.py:426
  66.1 0.1 slice_bitcast_fusion
  66.2 1.5 %collective-permute-start.4 = (bf16[64,5,8,128]{3,2,1,0:T(8,128)(2,1)S(1)}, bf16[64,5,8,128]{3,2,1,0:T(8,128)(2,1)S(1)}, u32[]{:S(2)}, u32[]{:S(2)}) collective-permute-start(bf16[64,5,8,128]{3,2,1,0:T(8,128)(2,1)S(1)} %get-tuple-element.24), channel_id=1, source_target_pairs={{0,1},{1,0},{2,3},{3,2},{4,5},{5,4},{6,7},{7,6},{8,9},{9,8},{10,11... | collective-permute-start | bytes 1966088 | tf_op jit(solution)/shard_map/ppermute | solution.py:407
  67.7 1.4 %collective-permute-start.6 = (bf16[64,5,8,128]{3,2,1,0:T(8,128)(2,1)S(1)}, bf16[64,5,8,128]{3,2,1,0:T(8,128)(2,1)S(1)}, u32[]{:S(2)}, u32[]{:S(2)}) collective-permute-start(bf16[64,5,8,128]{3,2,1,0:T(8,128)(2,1)S(1)} %get-tuple-element.23), channel_id=1, source_target_pairs={{0,129},{129,0},{1,128},{128,1},{2,131},{131,2},{3,130},{130,3},{4... | collective-permute-start | bytes 1966088 | tf_op jit(solution)/shard_map/ppermute | solution.py:406
  69.1 14.6 %collective-permute-done.4.refs_2_ = bf16[64,5,8,128]{3,2,1,0:T(8,128)(2,1)S(1)} collective-permute-done((bf16[64,5,8,128]{3,2,1,0:T(8,128)(2,1)S(1)}, bf16[64,5,8,128]{3,2,1,0:T(8,128)(2,1)S(1)}, u32[]{:S(2)}, u32[]{:S(2)}) %collective-permute-start.4) | collective-permute-done | bytes 655392 | tf_op jit(solution)/shard_map/ppermute | solution.py:407
  83.7 14.8 %collective-permute-done.6.refs_4_ = bf16[64,5,8,128]{3,2,1,0:T(8,128)(2,1)S(1)} collective-permute-done((bf16[64,5,8,128]{3,2,1,0:T(8,128)(2,1)S(1)}, bf16[64,5,8,128]{3,2,1,0:T(8,128)(2,1)S(1)}, u32[]{:S(2)}, u32[]{:S(2)}) %collective-permute-start.6) | collective-permute-done | bytes 655392 | tf_op jit(solution)/shard_map/ppermute | solution.py:406
  98.5 4.4 %correlate.2.refs_6_ = f32[2,8,256,512]{3,2,1,0:T(8,128)} custom-call(s32[2]{0:T(128)S(1)} %pad_add_fusion.place.refs_0_, bf16[64,2,5,8,128]{4,3,2,1,0:T(8,128)(2,1)S(1)} %all-to-all-done.1.refs_1_, bf16[64,5,8,128]{3,2,1,0:T(8,128)(2,1)S(1)} %collective-permute-done.4.refs_2_, bf16[64,5,8,128]{3,2,1,0:T(8,128)(2,1)S(1)} %collective-permute-done.5.refs_3_, ...), custom_call_target="tpu_custom_call" | custom-call | flops 2000000000 | bytes 7864320 | tf_op jit(solution)/shard_map/correlate/pallas_call | solution.py:384
  102.9 3.0 %all-to-all-done.refs_1_.refs_2_.refs_3_.refs_4_ = bf16[64,4,3,8,128]{4,3,2,1,0:T(8,128)(2,1)S(1)} async-done(((bf16[64,4,3,8,128]{4,3,2,1,0:T(8,128)(2,1)}), bf16[64,4,3,8,128]{4,3,2,1,0:T(8,128)(2,1)S(1)}, u32[]{:S(2)}, u32[]{:S(2)}) %all-to-all-start) | async-done | bytes 1572896 | tf_op jit(solution)/shard_map/all_to_all | solution.py:426
  105.9 3.3 %correlate.3 = f32[2,8,256,512]{3,2,1,0:T(8,128)} custom-call(s32[2]{0:T(128)S(1)} %pad_add_fusion.place.refs_0_, bf16[64,4,3,8,128]{4,3,2,1,0:T(8,128)(2,1)S(1)} %all-to-all-done.refs_1_.refs_2_.refs_3_.refs_4_, bf16[64,4,3,8,128]{4,3,2,1,0:T(8,128)(2,1)S(1)} %all-to-all-done.refs_1_.refs_2_.refs_3_.refs_4_, ...), custom_call_target="tpu_custom_call", output_to_operand_aliasing={{}: (6, {})} | custom-call | flops 1200000000 | bytes 4718592 | tf_op jit(solution)/shard_map/correlate/pallas_call | solution.py:384
  (9 shorter events, 0.0 us)
Async XLA Ops:
  0.9 7.7 %collective-permute-start = (bf16[2,96,128]{2,1,0:T(8,128)(2,1)S(1)}, bf16[2,96,128]{2,1,0:T(8,128)(2,1)S(1)}, u32[]{:S(2)}, u32[]{:S(2)}) collective-permute-start(bf16[2,96,128]{2,1,0:T(8,128)(2,1)S(1)} %slice_convert_fusion), channel_id=1, source_target_pairs={{0,1},{1,0},{2,3},{3,2},{4,5},{5,4},{6,7},{7,6},{8,9},{9,8},{10,11... | collective-permute-start | bytes 147464 | tf_op jit(solution)/shard_map/ppermute | solution.py:415
  13.3 46.6 %all-to-all-start.1 = ((bf16[64,2,5,8,128]{4,3,2,1,0:T(8,128)(2,1)}), bf16[64,2,5,8,128]{4,3,2,1,0:T(8,128)(2,1)S(1)}, u32[]{:S(2)}, u32[]{:S(2)}) async-start(bf16[64,2,5,8,128]{4,3,2,1,0:T(8,128)(2,1)} %get-tuple-element.22), calls=%async_computation.1 | async-start | bytes 2621440 | tf_op jit(solution)/shard_map/all_to_all | solution.py:423
  25.7 2.2 %copy-start = (bf16[8,4,256,256]{3,2,1,0:T(8,128)(2,1)S(1)}, bf16[8,4,256,256]{3,2,1,0:T(8,128)(2,1)}, u32[]{:S(2)}) copy-start(bf16[8,4,256,256]{3,2,1,0:T(8,128)(2,1)} %constant.82.clone.turn) | copy-start | bytes 12582916
  29.6 11.9 %collective-permute-start.1 = (bf16[64,3,8,128]{3,2,1,0:T(8,128)(2,1)S(1)}, bf16[64,3,8,128]{3,2,1,0:T(8,128)(2,1)S(1)}, u32[]{:S(2)}, u32[]{:S(2)}) collective-permute-start(bf16[64,3,8,128]{3,2,1,0:T(8,128)(2,1)S(1)} %get-tuple-element.20), channel_id=1, source_target_pairs={{0,1},{1,0},{2,3},{3,2},{4,5},{5,4},{6,7},{7,6},{8,9},{9,8},{10,11... | collective-permute-start | bytes 1179656 | tf_op jit(solution)/shard_map/ppermute | solution.py:407
  31.1 19.6 %collective-permute-start.3 = (bf16[64,3,8,128]{3,2,1,0:T(8,128)(2,1)S(1)}, bf16[64,3,8,128]{3,2,1,0:T(8,128)(2,1)S(1)}, u32[]{:S(2)}, u32[]{:S(2)}) collective-permute-start(bf16[64,3,8,128]{3,2,1,0:T(8,128)(2,1)S(1)} %get-tuple-element.21), channel_id=1, source_target_pairs={{0,129},{129,0},{1,128},{128,1},{2,131},{131,2},{3,130},{130,3},{4... | collective-permute-start | bytes 1179656 | tf_op jit(solution)/shard_map/ppermute | solution.py:406
  32.5 18.2 %collective-permute-start.2 = (bf16[64,3,8,128]{3,2,1,0:T(8,128)(2,1)S(1)}, bf16[64,3,8,128]{3,2,1,0:T(8,128)(2,1)S(1)}, u32[]{:S(2)}, u32[]{:S(2)}) collective-permute-start(bf16[64,3,8,128]{3,2,1,0:T(8,128)(2,1)S(1)} %get-tuple-element.21), channel_id=1, source_target_pairs={{0,128},{128,0},{1,129},{129,1},{2,130},{130,2},{3,131},{131,3},{4... | collective-permute-start | bytes 1179656 | tf_op jit(solution)/shard_map/ppermute | solution.py:405
  59.9 46.0 %all-to-all-start = ((bf16[64,4,3,8,128]{4,3,2,1,0:T(8,128)(2,1)}), bf16[64,4,3,8,128]{4,3,2,1,0:T(8,128)(2,1)S(1)}, u32[]{:S(2)}, u32[]{:S(2)}) async-start(bf16[64,4,3,8,128]{4,3,2,1,0:T(8,128)(2,1)} %pad_maximum_fusion), calls=%async_computation | async-start | bytes 3145728 | tf_op jit(solution)/shard_map/all_to_all | solution.py:426
  66.1 32.4 %copy-start.1 = (bf16[256,256]{1,0:T(8,128)(2,1)S(1)}, bf16[256,256]{1,0:T(8,128)(2,1)}, u32[]{:S(2)}) copy-start(bf16[256,256]{1,0:T(8,128)(2,1)} %constant.83.clone.refs_5_) | copy-start | bytes 393220
  66.2 17.5 %collective-permute-start.4 = (bf16[64,5,8,128]{3,2,1,0:T(8,128)(2,1)S(1)}, bf16[64,5,8,128]{3,2,1,0:T(8,128)(2,1)S(1)}, u32[]{:S(2)}, u32[]{:S(2)}) collective-permute-start(bf16[64,5,8,128]{3,2,1,0:T(8,128)(2,1)S(1)} %get-tuple-element.24), channel_id=1, source_target_pairs={{0,1},{1,0},{2,3},{3,2},{4,5},{5,4},{6,7},{7,6},{8,9},{9,8},{10,11... | collective-permute-start | bytes 1966088 | tf_op jit(solution)/shard_map/ppermute | solution.py:407
  67.7 30.8 %collective-permute-start.6 = (bf16[64,5,8,128]{3,2,1,0:T(8,128)(2,1)S(1)}, bf16[64,5,8,128]{3,2,1,0:T(8,128)(2,1)S(1)}, u32[]{:S(2)}, u32[]{:S(2)}) collective-permute-start(bf16[64,5,8,128]{3,2,1,0:T(8,128)(2,1)S(1)} %get-tuple-element.23), channel_id=1, source_target_pairs={{0,129},{129,0},{1,128},{128,1},{2,131},{131,2},{3,130},{130,3},{4... | collective-permute-start | bytes 1966088 | tf_op jit(solution)/shard_map/ppermute | solution.py:406
  69.1 29.4 %collective-permute-start.5 = (bf16[64,5,8,128]{3,2,1,0:T(8,128)(2,1)S(1)}, bf16[64,5,8,128]{3,2,1,0:T(8,128)(2,1)S(1)}, u32[]{:S(2)}, u32[]{:S(2)}) collective-permute-start(bf16[64,5,8,128]{3,2,1,0:T(8,128)(2,1)S(1)} %get-tuple-element.23), channel_id=1, source_target_pairs={{0,128},{128,0},{1,129},{129,1},{2,130},{130,2},{3,131},{131,3},{4... | collective-permute-start | bytes 1966088 | tf_op jit(solution)/shard_map/ppermute | solution.py:405

commit v6 on v5

--- a/solution.py
+++ b/solution.py
@@ -16,7 +16,7 @@
 SPEC = 128
 STEP = 16
 BODY = SPEC - STEP
-BATCH = 8
+BATCH = 16
 SLOTS = 5
 VMEM_KIB = 50 * 1024
 MORE_KIB = 50 * 1024

time: 110 us -> 110 us (level)
  no operation moved by 1% of the time
where the time goes in v6:
time: 110 us; the launch traced here: 109 us
  waiting for transfers between devices  58.5 us (53%)
  starting transfers between devices  28.2 us (26%)
  Pallas kernels  17.4 us (16%)
  other arithmetic  2.45 us (2%)
  local copies, waits for them, and re-layouts  2.32 us (2%)
    ppermute x2, waiting for transfers between devices, exchange(): cross = lax.ppermute(near_part, ('y_lo', 'tm'), both)  24 us
    ppermute x2, waiting for transfers between devices, exchange(): far = lax.ppermute(far_part, 'tm', flip)  23.6 us
    all_to_all x1, starting transfers between devices, local(): over = lax.all_to_all(rest, PLANE, split_axis=0, concat_axis=0, tiled=True)  12.4 us
    all_to_all x1, waiting for transfers between devices, local(): over = lax.all_to_all(rest, PLANE, split_axis=0, concat_axis=0, tiled=True)  7.88 us
    pallas_call x2, Pallas kernels, correlate(): pl.pallas_call(kernel, in_specs=in_specs, out_specs=hbm, scratch_shapes=[...  7.61 us
    all_to_all x1, starting transfers between devices, local(): lax.all_to_all(early, PLANE, split_axis=0, concat_axis=0, tiled=True)  6.16 us
    pallas_call x1, Pallas kernels, channelize(): pl.pallas_call(channel_kernel, in_specs=[pl.BlockSpec(memory_space=pltpu....  4.63 us
    ppermute x1, starting transfers between devices, local(): tail = lax.ppermute(tail, 'tm', [(0, 1), (1, 0)])  3.83 us
  transfers between devices with their start and end apart: 9, of which 6 were waited for; matrix products, arithmetic and copies ran while one was open for 2% of the time, Pallas kernels for 9%

profile of v6, /device:TPU:1, one launch (start us, length us, event | category | flops | bytes accessed | tf_op | source)
XLA Modules:
  0.0 109.1 jit_solution(5095487891475241484)
XLA Ops:
  0.0 0.9 slice_convert_fusion
  0.9 3.8 %collective-permute-start = (bf16[2,96,128]{2,1,0:T(8,128)(2,1)S(1)}, bf16[2,96,128]{2,1,0:T(8,128)(2,1)S(1)}, u32[]{:S(2)}, u32[]{:S(2)}) collective-permute-start(bf16[2,96,128]{2,1,0:T(8,128)(2,1)S(1)} %slice_convert_fusion), channel_id=1, source_target_pairs={{0,1},{1,0},{2,3},{3,2},{4,5},{5,4},{6,7},{7,6},{8,9},{9,8},{10,11... | collective-permute-start | bytes 147464 | tf_op jit(solution)/shard_map/ppermute | solution.py:415
  4.7 0.1 fusion.13
  4.8 0.1 pad_add_fusion.place.refs_0_
  4.9 3.5 %channelize_body.1 = (bf16[5,448,256]{2,1,0:T(8,128)(2,1)S(1)}, bf16[5,448,256]{2,1,0:T(8,128)(2,1)S(1)}, bf16[3,448,256]{2,1,0:T(8,128)(2,1)S(1)}, bf16[3,448,256]{2,1,0:T(8,128)(2,1)S(1)}) custom-call(s32[2,4096,128]{2,1,0:T(8,128)} %bitcast.24, f32[4,32,128]{2,1,0:T(8,128)S(1)} %bitcast.20), custom_call_target="tpu_custom_call" | custom-call | flops 1000000000 | bytes 8388608 | tf_op jit(solution)/shard_map/channelize_body/pallas_call | solution.py:251
  8.5 4.6 %channelize.1 = (bf16[64,2,5,8,128]{4,3,2,1,0:T(8,128)(2,1)}, bf16[3,64,256]{2,1,0:T(8,128)(2,1)S(1)}, bf16[3,64,256]{2,1,0:T(8,128)(2,1)S(1)}) custom-call(s32[2]{0:T(128)S(1)} %pad_add_fusion.place.refs_0_, s32[2,4096,128]{2,1,0:T(8,128)} %bitcast.25, bf16[2,96,128]{2,1,0:T(8,128)(2,1)S(1)} %collective-permute-done.tail, f32[4,32,128]{2,1,0:T(8,128)S(1)} %bitcast.21, ...), custom_call_target="tpu_custom_call" | custom-call | flops 1000000000 | bytes 6291456 | tf_op jit(solution)/shard_map/channelize/pallas_call | solution.py:274
  13.1 12.4 %all-to-all-start.1 = ((bf16[64,2,5,8,128]{4,3,2,1,0:T(8,128)(2,1)}), bf16[64,2,5,8,128]{4,3,2,1,0:T(8,128)(2,1)S(1)}, u32[]{:S(2)}, u32[]{:S(2)}) async-start(bf16[64,2,5,8,128]{4,3,2,1,0:T(8,128)(2,1)} %get-tuple-element.22), calls=%async_computation.1 | async-start | bytes 2621440 | tf_op jit(solution)/shard_map/all_to_all | solution.py:423
  25.6 2.2 %copy-done = bf16[8,4,256,256]{3,2,1,0:T(8,128)(2,1)S(1)} copy-done((bf16[8,4,256,256]{3,2,1,0:T(8,128)(2,1)S(1)}, bf16[8,4,256,256]{3,2,1,0:T(8,128)(2,1)}, u32[]{:S(2)}) %copy-start) | copy-done | bytes 4194328
  27.8 1.7 %channelize_late.1 = (bf16[64,3,8,128]{3,2,1,0:T(8,128)(2,1)S(1)}, bf16[64,3,8,128]{3,2,1,0:T(8,128)(2,1)S(1)}) custom-call(s32[2]{0:T(128)S(1)} %pad_add_fusion.place.refs_0_, bf16[8,4,256,256]{3,2,1,0:T(8,128)(2,1)S(1)} %copy-done, bf16[3,448,256]{2,1,0:T(8,128)(2,1)S(1)} %get-tuple-element.14.body_high, ...), custom_call_target="tpu_custom_call" | custom-call | flops 600000000 | bytes 3145728 | tf_op jit(solution)/shard_map/channelize_late/pallas_call | solution.py:301
  29.4 1.6 %collective-permute-start.1 = (bf16[64,3,8,128]{3,2,1,0:T(8,128)(2,1)S(1)}, bf16[64,3,8,128]{3,2,1,0:T(8,128)(2,1)S(1)}, u32[]{:S(2)}, u32[]{:S(2)}) collective-permute-start(bf16[64,3,8,128]{3,2,1,0:T(8,128)(2,1)S(1)} %get-tuple-element.20), channel_id=1, source_target_pairs={{0,1},{1,0},{2,3},{3,2},{4,5},{5,4},{6,7},{7,6},{8,9},{9,8},{10,11... | collective-permute-start | bytes 1179656 | tf_op jit(solution)/shard_map/ppermute | solution.py:407
  31.1 1.2 %collective-permute-start.3 = (bf16[64,3,8,128]{3,2,1,0:T(8,128)(2,1)S(1)}, bf16[64,3,8,128]{3,2,1,0:T(8,128)(2,1)S(1)}, u32[]{:S(2)}, u32[]{:S(2)}) collective-permute-start(bf16[64,3,8,128]{3,2,1,0:T(8,128)(2,1)S(1)} %get-tuple-element.21), channel_id=1, source_target_pairs={{0,129},{129,0},{1,128},{128,1},{2,131},{131,2},{3,130},{130,3},{4... | collective-permute-start | bytes 1179656 | tf_op jit(solution)/shard_map/ppermute | solution.py:406
  32.3 9.0 %collective-permute-done.1 = bf16[64,3,8,128]{3,2,1,0:T(8,128)(2,1)S(1)} collective-permute-done((bf16[64,3,8,128]{3,2,1,0:T(8,128)(2,1)S(1)}, bf16[64,3,8,128]{3,2,1,0:T(8,128)(2,1)S(1)}, u32[]{:S(2)}, u32[]{:S(2)}) %collective-permute-start.1) | collective-permute-done | bytes 393248 | tf_op jit(solution)/shard_map/ppermute | solution.py:407
  41.3 9.2 %collective-permute-done.3 = bf16[64,3,8,128]{3,2,1,0:T(8,128)(2,1)S(1)} collective-permute-done((bf16[64,3,8,128]{3,2,1,0:T(8,128)(2,1)S(1)}, bf16[64,3,8,128]{3,2,1,0:T(8,128)(2,1)S(1)}, u32[]{:S(2)}, u32[]{:S(2)}) %collective-permute-start.3) | collective-permute-done | bytes 393248 | tf_op jit(solution)/shard_map/ppermute | solution.py:406
  50.5 1.4 %pad_maximum_fusion = bf16[64,4,3,8,128]{4,3,2,1,0:T(8,128)(2,1)} fusion(bf16[64,1,3,8,128]{4,3,2,1,0:T(8,128)(2,1)S(1)} %bitcast.27, bf16[64,1,3,8,128]{4,3,2,1,0:T(8,128)(2,1)S(1)} %bitcast.28, bf16[64,1,3,8,128]{4,3,2,1,0:T(8,128)(2,1)S(1)} %bitcast.26, bf16[64,1,3,8,128]{4,3,2,1,0:T(8,128)(2,1)S(1)} %bitcast.22), kind=kLoop, calls=%fused_computation | loop fusion | flops 2359296 | bytes 3145728 | tf_op jit(solution)/shard_map/stack | solution.py:424
  51.9 7.9 %all-to-all-done.1.refs_1_ = bf16[64,2,5,8,128]{4,3,2,1,0:T(8,128)(2,1)S(1)} async-done(((bf16[64,2,5,8,128]{4,3,2,1,0:T(8,128)(2,1)}), bf16[64,2,5,8,128]{4,3,2,1,0:T(8,128)(2,1)S(1)}, u32[]{:S(2)}, u32[]{:S(2)}) %all-to-all-start.1) | async-done | bytes 1310752 | tf_op jit(solution)/shard_map/all_to_all | solution.py:423
  59.8 6.2 %all-to-all-start = ((bf16[64,4,3,8,128]{4,3,2,1,0:T(8,128)(2,1)}), bf16[64,4,3,8,128]{4,3,2,1,0:T(8,128)(2,1)S(1)}, u32[]{:S(2)}, u32[]{:S(2)}) async-start(bf16[64,4,3,8,128]{4,3,2,1,0:T(8,128)(2,1)} %pad_maximum_fusion), calls=%async_computation | async-start | bytes 3145728 | tf_op jit(solution)/shard_map/all_to_all | solution.py:426
  65.9 0.1 slice_bitcast_fusion
  66.1 1.6 %collective-permute-start.4 = (bf16[64,5,8,128]{3,2,1,0:T(8,128)(2,1)S(1)}, bf16[64,5,8,128]{3,2,1,0:T(8,128)(2,1)S(1)}, u32[]{:S(2)}, u32[]{:S(2)}) collective-permute-start(bf16[64,5,8,128]{3,2,1,0:T(8,128)(2,1)S(1)} %get-tuple-element.24), channel_id=1, source_target_pairs={{0,1},{1,0},{2,3},{3,2},{4,5},{5,4},{6,7},{7,6},{8,9},{9,8},{10,11... | collective-permute-start | bytes 1966088 | tf_op jit(solution)/shard_map/ppermute | solution.py:407
  67.7 1.2 %collective-permute-start.6 = (bf16[64,5,8,128]{3,2,1,0:T(8,128)(2,1)S(1)}, bf16[64,5,8,128]{3,2,1,0:T(8,128)(2,1)S(1)}, u32[]{:S(2)}, u32[]{:S(2)}) collective-permute-start(bf16[64,5,8,128]{3,2,1,0:T(8,128)(2,1)S(1)} %get-tuple-element.23), channel_id=1, source_target_pairs={{0,129},{129,0},{1,128},{128,1},{2,131},{131,2},{3,130},{130,3},{4... | collective-permute-start | bytes 1966088 | tf_op jit(solution)/shard_map/ppermute | solution.py:406
  69.0 14.6 %collective-permute-done.4.refs_2_ = bf16[64,5,8,128]{3,2,1,0:T(8,128)(2,1)S(1)} collective-permute-done((bf16[64,5,8,128]{3,2,1,0:T(8,128)(2,1)S(1)}, bf16[64,5,8,128]{3,2,1,0:T(8,128)(2,1)S(1)}, u32[]{:S(2)}, u32[]{:S(2)}) %collective-permute-start.4) | collective-permute-done | bytes 655392 | tf_op jit(solution)/shard_map/ppermute | solution.py:407
  83.6 14.8 %collective-permute-done.6.refs_4_ = bf16[64,5,8,128]{3,2,1,0:T(8,128)(2,1)S(1)} collective-permute-done((bf16[64,5,8,128]{3,2,1,0:T(8,128)(2,1)S(1)}, bf16[64,5,8,128]{3,2,1,0:T(8,128)(2,1)S(1)}, u32[]{:S(2)}, u32[]{:S(2)}) %collective-permute-start.6) | collective-permute-done | bytes 655392 | tf_op jit(solution)/shard_map/ppermute | solution.py:406
  98.4 4.3 %correlate.2.refs_6_ = f32[2,8,256,512]{3,2,1,0:T(8,128)} custom-call(s32[2]{0:T(128)S(1)} %pad_add_fusion.place.refs_0_, bf16[64,2,5,8,128]{4,3,2,1,0:T(8,128)(2,1)S(1)} %all-to-all-done.1.refs_1_, bf16[64,5,8,128]{3,2,1,0:T(8,128)(2,1)S(1)} %collective-permute-done.4.refs_2_, bf16[64,5,8,128]{3,2,1,0:T(8,128)(2,1)S(1)} %collective-permute-done.5.refs_3_, ...), custom_call_target="tpu_custom_call" | custom-call | flops 2000000000 | bytes 7864320 | tf_op jit(solution)/shard_map/correlate/pallas_call | solution.py:384
  102.7 3.0 %all-to-all-done.refs_1_.refs_2_.refs_3_.refs_4_ = bf16[64,4,3,8,128]{4,3,2,1,0:T(8,128)(2,1)S(1)} async-done(((bf16[64,4,3,8,128]{4,3,2,1,0:T(8,128)(2,1)}), bf16[64,4,3,8,128]{4,3,2,1,0:T(8,128)(2,1)S(1)}, u32[]{:S(2)}, u32[]{:S(2)}) %all-to-all-start) | async-done | bytes 1572896 | tf_op jit(solution)/shard_map/all_to_all | solution.py:426
  105.7 3.3 %correlate.3 = f32[2,8,256,512]{3,2,1,0:T(8,128)} custom-call(s32[2]{0:T(128)S(1)} %pad_add_fusion.place.refs_0_, bf16[64,4,3,8,128]{4,3,2,1,0:T(8,128)(2,1)S(1)} %all-to-all-done.refs_1_.refs_2_.refs_3_.refs_4_, bf16[64,4,3,8,128]{4,3,2,1,0:T(8,128)(2,1)S(1)} %all-to-all-done.refs_1_.refs_2_.refs_3_.refs_4_, ...), custom_call_target="tpu_custom_call", output_to_operand_aliasing={{}: (6, {})} | custom-call | flops 1200000000 | bytes 4718592 | tf_op jit(solution)/shard_map/correlate/pallas_call | solution.py:384
  (9 shorter events, 0.0 us)
Async XLA Ops:
  0.9 7.6 %collective-permute-start = (bf16[2,96,128]{2,1,0:T(8,128)(2,1)S(1)}, bf16[2,96,128]{2,1,0:T(8,128)(2,1)S(1)}, u32[]{:S(2)}, u32[]{:S(2)}) collective-permute-start(bf16[2,96,128]{2,1,0:T(8,128)(2,1)S(1)} %slice_convert_fusion), channel_id=1, source_target_pairs={{0,1},{1,0},{2,3},{3,2},{4,5},{5,4},{6,7},{7,6},{8,9},{9,8},{10,11... | collective-permute-start | bytes 147464 | tf_op jit(solution)/shard_map/ppermute | solution.py:415
  13.1 46.6 %all-to-all-start.1 = ((bf16[64,2,5,8,128]{4,3,2,1,0:T(8,128)(2,1)}), bf16[64,2,5,8,128]{4,3,2,1,0:T(8,128)(2,1)S(1)}, u32[]{:S(2)}, u32[]{:S(2)}) async-start(bf16[64,2,5,8,128]{4,3,2,1,0:T(8,128)(2,1)} %get-tuple-element.22), calls=%async_computation.1 | async-start | bytes 2621440 | tf_op jit(solution)/shard_map/all_to_all | solution.py:423
  25.6 2.2 %copy-start = (bf16[8,4,256,256]{3,2,1,0:T(8,128)(2,1)S(1)}, bf16[8,4,256,256]{3,2,1,0:T(8,128)(2,1)}, u32[]{:S(2)}) copy-start(bf16[8,4,256,256]{3,2,1,0:T(8,128)(2,1)} %constant.82.clone.turn) | copy-start | bytes 12582916
  29.4 11.9 %collective-permute-start.1 = (bf16[64,3,8,128]{3,2,1,0:T(8,128)(2,1)S(1)}, bf16[64,3,8,128]{3,2,1,0:T(8,128)(2,1)S(1)}, u32[]{:S(2)}, u32[]{:S(2)}) collective-permute-start(bf16[64,3,8,128]{3,2,1,0:T(8,128)(2,1)S(1)} %get-tuple-element.20), channel_id=1, source_target_pairs={{0,1},{1,0},{2,3},{3,2},{4,5},{5,4},{6,7},{7,6},{8,9},{9,8},{10,11... | collective-permute-start | bytes 1179656 | tf_op jit(solution)/shard_map/ppermute | solution.py:407
  31.1 19.4 %collective-permute-start.3 = (bf16[64,3,8,128]{3,2,1,0:T(8,128)(2,1)S(1)}, bf16[64,3,8,128]{3,2,1,0:T(8,128)(2,1)S(1)}, u32[]{:S(2)}, u32[]{:S(2)}) collective-permute-start(bf16[64,3,8,128]{3,2,1,0:T(8,128)(2,1)S(1)} %get-tuple-element.21), channel_id=1, source_target_pairs={{0,129},{129,0},{1,128},{128,1},{2,131},{131,2},{3,130},{130,3},{4... | collective-permute-start | bytes 1179656 | tf_op jit(solution)/shard_map/ppermute | solution.py:406
  32.3 18.2 %collective-permute-start.2 = (bf16[64,3,8,128]{3,2,1,0:T(8,128)(2,1)S(1)}, bf16[64,3,8,128]{3,2,1,0:T(8,128)(2,1)S(1)}, u32[]{:S(2)}, u32[]{:S(2)}) collective-permute-start(bf16[64,3,8,128]{3,2,1,0:T(8,128)(2,1)S(1)} %get-tuple-element.21), channel_id=1, source_target_pairs={{0,128},{128,0},{1,129},{129,1},{2,130},{130,2},{3,131},{131,3},{4... | collective-permute-start | bytes 1179656 | tf_op jit(solution)/shard_map/ppermute | solution.py:405
  59.8 46.0 %all-to-all-start = ((bf16[64,4,3,8,128]{4,3,2,1,0:T(8,128)(2,1)}), bf16[64,4,3,8,128]{4,3,2,1,0:T(8,128)(2,1)S(1)}, u32[]{:S(2)}, u32[]{:S(2)}) async-start(bf16[64,4,3,8,128]{4,3,2,1,0:T(8,128)(2,1)} %pad_maximum_fusion), calls=%async_computation | async-start | bytes 3145728 | tf_op jit(solution)/shard_map/all_to_all | solution.py:426
  65.9 32.4 %copy-start.1 = (bf16[256,256]{1,0:T(8,128)(2,1)S(1)}, bf16[256,256]{1,0:T(8,128)(2,1)}, u32[]{:S(2)}) copy-start(bf16[256,256]{1,0:T(8,128)(2,1)} %constant.83.clone.refs_5_) | copy-start | bytes 393220
  66.1 17.5 %collective-permute-start.4 = (bf16[64,5,8,128]{3,2,1,0:T(8,128)(2,1)S(1)}, bf16[64,5,8,128]{3,2,1,0:T(8,128)(2,1)S(1)}, u32[]{:S(2)}, u32[]{:S(2)}) collective-permute-start(bf16[64,5,8,128]{3,2,1,0:T(8,128)(2,1)S(1)} %get-tuple-element.24), channel_id=1, source_target_pairs={{0,1},{1,0},{2,3},{3,2},{4,5},{5,4},{6,7},{7,6},{8,9},{9,8},{10,11... | collective-permute-start | bytes 1966088 | tf_op jit(solution)/shard_map/ppermute | solution.py:407
  67.7 30.6 %collective-permute-start.6 = (bf16[64,5,8,128]{3,2,1,0:T(8,128)(2,1)S(1)}, bf16[64,5,8,128]{3,2,1,0:T(8,128)(2,1)S(1)}, u32[]{:S(2)}, u32[]{:S(2)}) collective-permute-start(bf16[64,5,8,128]{3,2,1,0:T(8,128)(2,1)S(1)} %get-tuple-element.23), channel_id=1, source_target_pairs={{0,129},{129,0},{1,128},{128,1},{2,131},{131,2},{3,130},{130,3},{4... | collective-permute-start | bytes 1966088 | tf_op jit(solution)/shard_map/ppermute | solution.py:406
  68.9 29.4 %collective-permute-start.5 = (bf16[64,5,8,128]{3,2,1,0:T(8,128)(2,1)S(1)}, bf16[64,5,8,128]{3,2,1,0:T(8,128)(2,1)S(1)}, u32[]{:S(2)}, u32[]{:S(2)}) collective-permute-start(bf16[64,5,8,128]{3,2,1,0:T(8,128)(2,1)S(1)} %get-tuple-element.23), channel_id=1, source_target_pairs={{0,128},{128,0},{1,129},{129,1},{2,130},{130,2},{3,131},{131,3},{4... | collective-permute-start | bytes 1966088 | tf_op jit(solution)/shard_map/ppermute | solution.py:405
